TPU v7x, 32 devices: a whole 2x2x4 slice. The times are simulated.
32 devices in a mesh: seq: 16 (over z, y, x), ch: 2 (over core).
Axes of the slice: x: 2, y: 2, z: 4, core: 2. Of those that a mesh axis runs over, the one named last changes fastest.
Arguments:
- inputs: bfloat16 [8192, 1024], P('seq', 'ch'), may hold values from -6 to 6
- conv_weight: bfloat16 [3, 1024], P(None, 'ch'), may hold values from -3 to 3
- mixing: bfloat16 [6, 128, 64, 128], P(None, 'seq'), may hold values from -0.5 to 0.5
- pattern: int32 [2, 128], P(None, 'seq'), may hold values from 0 to 7, as said below
- w_in: bfloat16 [1024, 4096], P(None, 'ch'), may hold values from -0.1875 to 0.1875
- w_out: bfloat16 [4096, 1024], P('ch'), may hold values from -0.09375 to 0.09375
- cotangent: bfloat16 [8192, 1024], P('seq', 'ch'), may hold values from -6 to 6
Outputs:
- layer_out: bfloat16 [8192, 1024], P('seq', 'ch')
- convolved: bfloat16 [8192, 1024], P('seq', 'ch')
- grad_input: bfloat16 [8192, 1024], P('seq', 'ch')
Inputs may be any that keep to these rules, and one draw needn't show every extreme that they name: `pattern`: for each of the 2 factors and each aligned run of 8 blocks (the blocks of one device), entry j of the run is a number k != j with entry k equal to j.
All inputs are finite; a program needn't handle non-finite values.
Results may differ from a plain program's by a relative error of at most 0.025.
Values may be sent and summed in bfloat16 or wider, within the bound.
No kernel may reach another device: no remote copies, remote signals or barrier semaphores. Data moves between devices by JAX's collectives and lax.ppermute only.
A program may use at most 64 MiB of HBM per device.

v0:
```python
import functools

import jax
import jax.numpy as jnp
from jax import lax
from jax.experimental import pallas as pl
from jax.experimental.pallas import tpu as pltpu
from jax.sharding import PartitionSpec as P

BLOCK = 64
LOCAL = 2
QUARTERS = 4
TILE = 512
SMALL = 8 * 1024 * 1024
LARGE = 20 * 1024 * 1024
ALL = 44 * 1024 * 1024

root_two_pi = 0.7978845608028654

IN_HBM = pl.BlockSpec(memory_space=pltpu.HBM)
IN_VMEM = pl.BlockSpec(memory_space=pltpu.VMEM)
ANYWHERE = pl.BlockSpec(memory_space=pl.ANY)
ACROSS = (((1,), (1,)), ((), ()))
OVER_ROWS = (((0,), (0,)), ((), ()))


def times(weights, value):
    return jnp.dot(weights, value, preferred_element_type=jnp.float32)


def times_transposed(weights, value):
    return lax.dot_general(weights, value, OVER_ROWS, preferred_element_type=jnp.float32)


def neighbours(edges, axis):
    count = lax.axis_size(axis)
    near = lax.ppermute(edges, axis, [(i, i ^ 1) for i in range(count)])
    route = []
    for low in range(1, count - 1, 2):
        route += [(low, low + 1), (low + 1, low)]
    return near, lax.ppermute(edges, axis, route)


def from_flipped(block, axis, mask):
    count = lax.axis_size(axis)
    return lax.ppermute(block, axis, [(i, i ^ mask) for i in range(count)])


def from_offset(block, axis, offset):
    count = lax.axis_size(axis)
    return lax.ppermute(block, axis, [((i + offset) % count, i) for i in range(count)])


def call(kernel, name, outs, arrays, distant=(), scratch=(), order=(), limit=SMALL):
    count = len(distant) + len(arrays)

    def body(*refs):
        kernel(*refs[:count], *refs[count + len(order) :])

    return pl.pallas_call(
        body,
        out_shape=[jax.ShapeDtypeStruct(shape, kind) for shape, kind in outs],
        in_specs=[ANYWHERE] * len(distant) + [IN_VMEM] * len(arrays) + [ANYWHERE] * len(order),
        out_specs=[IN_VMEM] * len(outs),
        scratch_shapes=list(scratch),
        compiler_params=pltpu.CompilerParams(vmem_limit_bytes=limit),
        cost_estimate=pl.CostEstimate(flops=0, bytes_accessed=0, transcendentals=0),
        name=name,
    )(*distant, *arrays, *order)


def own_bits():
    seat = lax.axis_index("seq")
    levels = lax.axis_size("seq").bit_length() - 1
    return (seat >> (levels - 2)) & 1, (seat >> (levels - 1)) & 1


def shifted(cells, near, far):
    rows = cells.shape[0]
    even = lax.axis_index("seq") % 2 == 0
    near, far = near.astype(jnp.float32), far.astype(jnp.float32)
    before = jnp.where(even, far[1:2], near[1:2])
    after = jnp.where(even, near[0:1], far[0:1])
    spot = lax.broadcasted_iota(jnp.int32, cells.shape, 0)
    up = jnp.where(spot == 0, before, pltpu.roll(cells, 1, 0))
    down = jnp.where(spot == rows - 1, after, pltpu.roll(cells, rows - 1, 0))
    return up, down


def chosen_blocks(subs):
    early, late = own_bits()
    return [
        sub // 2 * QUARTERS + (early ^ (1 - sub % 2)) * 2 + (late ^ other)
        for sub in subs
        for other in range(2)
    ]


def local_factor(factor, pattern, source, mixing, target, chosen):
    for spot, block in enumerate(chosen):
        pair = mixing[factor, block]
        target[spot] = (
            times(pair[:, :BLOCK], source[block])
            + times(pair[:, BLOCK:], source[pattern[factor, block]])
        ).astype(jnp.bfloat16)


def entry_kernel(units, pattern_far, cells, far, near, mixing, conv_ref, *rest):
    outs, (first, between, pattern, arrival) = rest[:-4], rest[-4:]
    fetch = pltpu.make_async_copy(pattern_far, pattern, arrival)
    fetch.start()
    values = cells[...].astype(jnp.float32)
    scale = near[2:5].astype(jnp.float32)
    up, down = shifted(values, near[...], far[...])
    convolved = (scale[0:1] * up + scale[1:2] * values + scale[2:3] * down).astype(jnp.bfloat16)
    conv_ref[...] = convolved
    first[...] = convolved.reshape(first.shape)
    fetch.wait()
    every = range(first.shape[0])
    refs = (first, between)
    for factor in range(LOCAL - 1):
        local_factor(factor, pattern, refs[factor % 2], mixing, refs[1 - factor % 2], every)
    source = refs[(LOCAL - 1) % 2]
    for unit, out in zip(units, outs):
        local_factor(LOCAL - 1, pattern, source, mixing, out, chosen_blocks(unit))


def plain_kernel(factor, unit, state, mates, mixing, *outs):
    for spot, block in enumerate(chosen_blocks(unit)):
        pair = mixing[factor, block]
        per_out = state.shape[0] // len(outs)
        outs[spot // per_out][spot % per_out] = (
            times(pair[:, :BLOCK], state[spot]) + times(pair[:, BLOCK:], mates[spot])
        ).astype(jnp.bfloat16)


def packed(message, pieces, number):
    across = message.shape[-1] // (2 * BLOCK)
    lanes = pl.ds(number % across * 2 * BLOCK, 2 * BLOCK)
    return message.at[pieces + number // across, :, lanes]


def load_kernel(mixing_far, cells_far, pattern_far, mixing, cells, pattern, arrivals):
    pairs = ((mixing_far, mixing), (cells_far, cells), (pattern_far, pattern))
    fetches = [
        pltpu.make_async_copy(far, near, arrivals.at[i]) for i, (far, near) in enumerate(pairs)
    ]
    for fetch in fetches:
        fetch.start()
    for fetch in fetches:
        fetch.wait()


def pack_kernel(factor, pieces, length, cots, mixing, own, near, across):
    messages = (near, across.at[pl.ds(0, length)], across.at[pl.ds(length, length)])
    my_early, my_late = own_bits()
    for piece in range(pieces):
        base = piece * QUARTERS
        own[piece] = cots[base + my_early * 2 + my_late]
        for flip, message in enumerate(messages, 1):
            early, late = my_early ^ (flip & 1), my_late ^ (flip >> 1)
            message[piece] = cots[base + early * 2 + late]
            for which in range(2):
                number = which * pieces + piece
                if flip == 1:
                    for other in range(2):
                        packed(message, pieces, number * 2 + other)[...] = mixing[
                            factor + which, base + early * 2 + (late ^ other)
                        ]
                else:
                    packed(message, pieces, number)[...] = mixing[
                        factor + which, base + early * 2 + late
                    ]


def forward_kernel(message, out):
    out[...] = message[out.shape[0] :]


def stack_kernel(pieces, *rest):
    quarters, outs = rest[:QUARTERS], rest[QUARTERS:]
    for piece, out in enumerate(outs):
        for quarter, values in enumerate(quarters):
            out[quarter * BLOCK : (quarter + 1) * BLOCK] = values[piece]


def mixing_of(factor, which, pieces, piece, mixing, messages, quarter, other=0):
    if quarter == 0:
        early, late = own_bits()
        return mixing[factor + which, piece * QUARTERS + early * 2 + (late ^ other)]
    number = which * pieces + piece
    if quarter == 1:
        number = number * 2 + other
    return packed(messages[quarter - 1], pieces, number)[...]


def early_kernel(factor, pieces, piece, keep, recv, mixing, message, keep_out, send_out):
    weights = functools.partial(mixing_of, factor, 0, pieces, piece, mixing, [message])
    for other, out in enumerate((keep_out, send_out)):
        mine, theirs = keep[other], recv[other]
        pair = weights(0, other)
        out[0] = (times(pair[:, :BLOCK], mine) + times(pair[:, BLOCK:], theirs)).astype(
            jnp.bfloat16
        )
        pair = weights(1, other)
        out[1] = (times(pair[:, :BLOCK], theirs) + times(pair[:, BLOCK:], mine)).astype(
            jnp.bfloat16
        )


def hold_kernel(received, out):
    out[...] = received[...]


def late_kernel(factor, pieces, piece, keep, recv, mixing, *rest):
    messages, outs = rest[:-2], rest[-2:]
    values = [keep[0], keep[1], recv[0], recv[1]]
    for quarter in range(QUARTERS):
        pair = mixing_of(factor, 1, pieces, piece, mixing, messages, quarter)
        rows = slice(quarter % 2 * BLOCK, (quarter % 2 + 1) * BLOCK)
        outs[quarter // 2][rows] = (
            times(pair[:, :BLOCK], values[quarter]) + times(pair[:, BLOCK:], values[quarter ^ 2])
        ).astype(jnp.bfloat16)


def back_kernel(factor, pieces, piece, cores, cots, total, *rest):
    count = (cores - 1) * 2
    parts, (mixing, message1, message2, message3, *outs) = rest[:count], rest[count:]
    messages = (message1, message2, message3)
    grads = []
    for quarter in range(QUARTERS):
        rows = slice(quarter * BLOCK, (quarter + 1) * BLOCK)
        grad = cots[rows].astype(jnp.float32) + total[rows]
        inner = slice(quarter % 2 * BLOCK, (quarter % 2 + 1) * BLOCK)
        for part in parts[quarter // 2 :: 2]:
            grad = grad + part[inner].astype(jnp.float32)
        grads.append(grad.astype(jnp.bfloat16))
    for which, flip in ((1, 2), (0, 1)):
        both = [
            times_transposed(
                mixing_of(factor, which, pieces, piece, mixing, messages, quarter),
                grads[quarter],
            )
            for quarter in range(QUARTERS)
        ]
        grads = [
            (both[quarter][:BLOCK] + both[quarter ^ flip][BLOCK:]).astype(jnp.bfloat16)
            for quarter in range(QUARTERS)
        ]
    for grad, out in zip(grads, outs):
        out[...] = grad


def regroup_kernel(factor, units, *rest):
    quarters, mixing, outs = rest[:QUARTERS], rest[QUARTERS], rest[QUARTERS + 1 :]
    for number, unit in enumerate(units):
        own, cross = outs[2 * number : 2 * number + 2]
        for spot, block in enumerate(chosen_blocks(unit)):
            grad = quarters[1 - unit[spot // 2] % 2 + spot % 2 * 2][...]
            both = times_transposed(mixing[factor, block], grad)
            own[spot] = both[:BLOCK]
            cross[spot] = both[BLOCK:].astype(jnp.bfloat16)


def plain_back_kernel(factor, unit, mine, theirs, mixing, own, cross):
    for spot, block in enumerate(chosen_blocks(unit)):
        grad = (mine[spot] + theirs[spot].astype(jnp.float32)).astype(jnp.bfloat16)
        both = times_transposed(mixing[factor, block], grad)
        own[spot] = both[:BLOCK]
        cross[spot] = both[BLOCK:].astype(cross.dtype)


def exit_kernel(units, pattern_far, *rest):
    count = len(units)
    mine, theirs = rest[:count], rest[count : 2 * count]
    mixing, out, edges, own, cross, pattern, arrival = rest[2 * count :]
    fetch = pltpu.make_async_copy(pattern_far, pattern, arrival)
    fetch.start()
    blocks = own.shape[0]
    for number, unit in enumerate(units):
        for spot, block in enumerate(chosen_blocks(unit)):
            own[block] = mine[number][spot]
            cross[block] = theirs[number][spot]
    fetch.wait()
    for factor in reversed(range(LOCAL)):
        for block in range(blocks):
            own[block] += cross[pattern[factor, block]]
        for block in range(blocks):
            grad = own[block].astype(jnp.bfloat16)
            if factor == 0:
                out[block * BLOCK : (block + 1) * BLOCK] = grad
                if block == 0:
                    edges[0:1] = grad[:1]
                if block == blocks - 1:
                    edges[1:2] = grad[-1:]
            else:
                both = times_transposed(mixing[factor - 1, block], grad)
                own[block] = both[:BLOCK]
                cross[block] = both[BLOCK:]


def conv_back_kernel(cells, far, near, taps, out, ready):
    ready[...] = jnp.zeros_like(ready)
    values = cells[...].astype(jnp.float32)
    scale = taps[2:5].astype(jnp.float32)
    up, down = shifted(values, near[...], far[...])
    out[...] = (scale[0:1] * down + scale[1:2] * values + scale[2:3] * up).astype(jnp.bfloat16)


def channel_spots(count, chans):
    core = lax.axis_index("ch")
    return [
        pl.ds(pl.multiple_of(lax.rem(core + i, count) * chans, chans), chans)
        for i in range(count)
    ]


def grad_act_kernel(count, *rest):
    cots, (w_out, grad_act, c_all) = rest[:count], rest[count:]
    for spot, cot in zip(channel_spots(count, cots[0].shape[1]), cots):
        c_all[:, spot] = cot[...]
    hidden = w_out.shape[0]
    tile = min(TILE, hidden)
    for start in range(0, hidden, tile):
        grad_act[:, start : start + tile] = lax.dot_general(
            c_all[...], w_out[start : start + tile], ACROSS, preferred_element_type=jnp.float32
        ).astype(grad_act.dtype)


def hidden_kernel(count, *rest):
    mixed, (grad_act, w_in, activation, own) = rest[: 2 * count], rest[2 * count : 2 * count + 4]
    backs, (x_all, back_sum) = rest[2 * count + 4 : -2], rest[-2:]
    rows, chans = mixed[0].shape
    spots = channel_spots(count, chans)
    for i, spot in enumerate(spots):
        x_all[:rows, spot] = mixed[2 * i][...]
        x_all[rows:, spot] = mixed[2 * i + 1][...]
    size = w_in.shape[1]
    tile = min(TILE, size)
    for start in range(0, size, tile):
        tiles = slice(start, start + tile)
        hidden = times(x_all[...], w_in[:, tiles])
        square = hidden * hidden
        tanh_val = jnp.tanh(hidden * (root_two_pi + root_two_pi * 0.044715 * square))
        half = 0.5 + 0.5 * tanh_val
        gelu = hidden * half
        activation[:, tiles] = gelu.astype(jnp.bfloat16)
        slope = 2.0 * root_two_pi + 6.0 * root_two_pi * 0.044715 * square
        derivative = half + gelu * (1.0 - half) * slope
        grad_hidden = (grad_act[:, tiles].astype(jnp.float32) * derivative).astype(jnp.bfloat16)
        back = lax.dot_general(
            grad_hidden, w_in[:, tiles], ACROSS, preferred_element_type=jnp.float32
        )
        if start == 0:
            back_sum[...] = back
        else:
            back_sum[...] += back
    own[...] = back_sum[:, spots[0]]
    for i, spot in enumerate(spots[1:]):
        backs[2 * i][...] = back_sum[:rows, spot].astype(jnp.bfloat16)
        backs[2 * i + 1][...] = back_sum[rows:, spot].astype(jnp.bfloat16)


def out_kernel(count, activation, top, bottom, w_out, own, *others):
    rows, chans = top.shape
    for i, spot in enumerate(channel_spots(count, chans)):
        product = times(activation[...], w_out[:, spot])
        if i == 0:
            own[:rows] = top[...].astype(jnp.float32) + product[:rows]
            own[rows:] = bottom[...].astype(jnp.float32) + product[rows:]
        else:
            cuts = len(others) // (count - 1)
            for cut in range(cuts):
                size = 2 * rows // cuts
                part = product[cut * size : (cut + 1) * size]
                others[(i - 1) * cuts + cut][...] = part.astype(jnp.bfloat16)


def combine_kernel(pieces, counts, *rest):
    owns, parts, outs = rest[:pieces], rest[pieces:-QUARTERS], rest[-QUARTERS:]
    for piece in range(pieces):
        per_piece = counts[piece]
        mine, parts = parts[:per_piece], parts[per_piece:]
        for quarter, out in enumerate(outs):
            total = owns[piece][quarter * BLOCK : (quarter + 1) * BLOCK]
            cuts = total.shape[0] * QUARTERS // mine[0].shape[0]
            start = quarter * BLOCK % mine[0].shape[0]
            for part in mine[quarter * cuts // QUARTERS :: cuts]:
                total = total + part[start : start + BLOCK].astype(jnp.float32)
            out[piece] = total.astype(jnp.bfloat16)


def assemble_kernel(*rest):
    quarters, out = rest[:-1], rest[-1]
    my_early, my_late = own_bits()
    for quarter, values in enumerate(quarters):
        spot = (my_early ^ (quarter & 1)) * 2 + (my_late ^ (quarter >> 1))
        for piece in range(values.shape[0]):
            start = pl.multiple_of((piece * QUARTERS + spot) * BLOCK, BLOCK)
            out[pl.ds(start, BLOCK)] = values[piece]


def on_device(inputs, conv_weight, mixing, pattern, w_in, w_out, cotangent):
    row_count, chan_count = inputs.shape
    blocks = row_count // BLOCK
    pieces = blocks // QUARTERS
    width, hidden = w_in.shape
    cores = lax.axis_size("ch")
    levels = lax.axis_size("seq").bit_length() - 1
    plain = list(range(LOCAL, LOCAL + levels - 2))
    last = LOCAL + levels - 2
    early_bit, late_bit = 1 << (levels - 2), 1 << (levels - 1)
    masks = [0, early_bit, late_bit, early_bit | late_bit]

    def blocks_of(size, kind=jnp.bfloat16):
        return ((size, BLOCK, chan_count), kind)

    half = blocks_of(2)
    whole = ((row_count, chan_count), jnp.bfloat16)
    piece_rows = QUARTERS * BLOCK
    flat = (piece_rows, chan_count)
    block = ((BLOCK, chan_count), jnp.bfloat16)
    half_flat = ((2 * BLOCK, chan_count), jnp.bfloat16)
    flat_piece = (flat, jnp.bfloat16)
    flops = 2 * piece_rows * width * hidden

    latest = []

    def run(kernel, name, outs, arrays, *args, **kwargs):
        results = call(kernel, name, outs, arrays, *args, order=tuple(latest), **kwargs)
        latest[:] = results[-1:]
        return results

    near, far = neighbours(jnp.concatenate([inputs[:1], inputs[-1:], conv_weight]), "seq")
    per_block = chan_count // (2 * BLOCK)
    lengths = [pieces + -(-pieces * 2 * (1 + (flip == 1)) // per_block) for flip in (1, 2, 3)]
    length = lengths[1]
    mixing, cells, pattern = run(
        load_kernel,
        "load",
        [(array.shape, array.dtype) for array in (mixing, inputs, pattern)],
        [],
        [mixing, inputs, pattern],
        [pltpu.SemaphoreType.DMA((3,))],
        limit=ALL,
    )
    units = [(s,) for s in range(2 * pieces)]
    convolved, *states = run(
        functools.partial(entry_kernel, units),
        "conv_and_local_factors",
        [whole] + [blocks_of(2 * len(unit)) for unit in units],
        [cells, far, near, mixing],
        [pattern],
        [pltpu.VMEM((blocks, BLOCK, chan_count), jnp.bfloat16)] * 2
        + [pltpu.SMEM(pattern.shape, jnp.int32), pltpu.SemaphoreType.DMA],
    )
    own_cots, *messages = run(
        functools.partial(pack_kernel, last, pieces, length),
        "pack",
        [((pieces, BLOCK, chan_count), jnp.bfloat16)]
        + [blocks_of(lengths[0]), blocks_of(2 * length)],
        [cotangent.reshape(blocks, BLOCK, chan_count), mixing],
    )
    messages = [from_flipped(m, "seq", mask) for m, mask in zip(messages, masks[1:])]

    def forward():
        (message,) = run(forward_kernel, "forward", [blocks_of(length)], [messages[1]])
        messages.append(from_flipped(message, "seq", early_bit))

    all_cots = []
    halves = {}
    transposed = [None] * pieces
    grad_acts = [None] * pieces
    parts = [None] * pieces
    mixeds = [None] * pieces
    activations = [None] * pieces
    owns = [None] * pieces
    out_owns = [None] * pieces
    out_parts = [None] * pieces

    def stack():
        stacked = run(
            functools.partial(stack_kernel, pieces),
            "stack",
            [flat_piece] * pieces,
            [own_cots, *messages],
        )
        for piece in stacked:
            all_cots.append([piece] + [from_offset(piece, "ch", i) for i in range(1, cores)])

    def grad_act(p):
        (grad_acts[p],) = run(
            functools.partial(grad_act_kernel, cores),
            "grad_act",
            [((piece_rows, hidden), jnp.bfloat16)],
            [*all_cots[p], w_out],
            scratch=[pltpu.VMEM((piece_rows, width), jnp.bfloat16)],
            limit=LARGE,
        )

    def plain_factor(factor, u):
        unit = units[u]
        mates = from_flipped(states[u], "seq", 1 << (factor - LOCAL))
        split = factor == plain[-1] and len(unit) == 2
        results = run(
            functools.partial(plain_kernel, factor, unit),
            "factor",
            [half, half] if split else [blocks_of(2 * len(unit))],
            [states[u], mates, mixing],
        )
        if factor == plain[-1]:
            halves.update(zip(unit, results))
        else:
            states[u] = results[0]

    def early_factor(p):
        send, keep = halves[2 * p], halves[2 * p + 1]
        transposed[p] = run(
            functools.partial(early_kernel, last, pieces, p),
            "early_factor",
            [half, half],
            [keep, from_flipped(send, "seq", early_bit), mixing, messages[0]],
        )

    def arrive(p):
        keep, send = transposed[p]
        (received,) = run(hold_kernel, "hold", [half], [from_flipped(send, "seq", late_bit)])
        transposed[p] = keep, received

    def late_factor(p):
        keep, received = transposed[p]
        if p > 0:
            received = from_flipped(received, "seq", late_bit)
        mixeds[p] = run(
            functools.partial(late_kernel, last, pieces, p),
            "late_factor",
            [half_flat] * 2,
            [keep, received, mixing, *messages],
        )

    def hidden_and_grad(p):
        gathered = [
            from_offset(mixed, "ch", i) if i else mixed for i in range(cores) for mixed in mixeds[p]
        ]
        activations[p], owns[p], *backs = run(
            functools.partial(hidden_kernel, cores),
            "mlp_hidden_and_grad",
            [((piece_rows, hidden), jnp.bfloat16), (flat, jnp.float32)]
            + [half_flat] * ((cores - 1) * 2),
            [*gathered, grad_acts[p], w_in],
            scratch=[
                pltpu.VMEM((piece_rows, width), jnp.bfloat16),
                pltpu.VMEM((piece_rows, width), jnp.float32),
            ],
            limit=LARGE,
        )
        parts[p] = [
            from_offset(back, "ch", cores - 1 - i // 2) for i, back in enumerate(backs)
        ]

    def transposed_back(p):
        quarters = run(
            functools.partial(back_kernel, last, pieces, p, cores),
            "late_and_early_back",
            [block] * QUARTERS,
            [all_cots[p][0], owns[p], *parts[p], mixing, *messages],
        )
        transposed[p] = [
            from_flipped(grad, "seq", mask) if mask else grad
            for grad, mask in zip(quarters, masks)
        ]

    def regroup(p):
        chosen = [u for u, unit in enumerate(back_units) if unit[0] // 2 == p]
        sizes = [2 * len(back_units[u]) for u in chosen]
        results = run(
            functools.partial(regroup_kernel, plain[-1], [back_units[u] for u in chosen]),
            "regroup_and_factor_back",
            [blocks_of(size, kind) for size in sizes for kind in (jnp.float32, jnp.bfloat16)],
            [*transposed[p], mixing],
        )
        for number, u in enumerate(chosen):
            states[u] = results[2 * number : 2 * number + 2]

    def out_product(p):
        cuts = 1 if p + 1 < pieces else 2
        out_owns[p], *others = run(
            functools.partial(out_kernel, cores),
            "mlp_out",
            [(flat, jnp.float32)] + [flat_piece if cuts == 1 else half_flat] * (cuts * (cores - 1)),
            [activations[p], *mixeds[p], w_out],
            limit=LARGE,
        )
        out_parts[p] = [
            from_offset(other, "ch", cores - 1 - i // cuts) for i, other in enumerate(others)
        ]

    def plain_back(factor, u):
        mine, cross = states[u]
        theirs = from_flipped(cross, "seq", 1 << (factor - LOCAL))
        kind = jnp.bfloat16 if factor != plain[0] else jnp.float32
        size = 2 * len(back_units[u])
        states[u] = run(
            functools.partial(plain_back_kernel, factor - 1, back_units[u]),
            "factor_back",
            [blocks_of(size, jnp.float32), blocks_of(size, kind)],
            [mine, theirs, mixing],
        )

    waves = sorted((u + 2 * i, -i, u) for i in range(len(plain)) for u in range(len(units)))
    for _, i, u in waves:
        plain_factor(plain[-i], u)
        if plain[-i] == plain[-1] and u == len(units) - 2:
            arrive(0)
        if plain[-i] == plain[-1] and u == 1:
            early_factor(0)
            forward()
    late_factor(0)
    for p in range(1, pieces):
        early_factor(p)
    stack()
    grad_act(0)
    back_units = [(2 * p, 2 * p + 1) for p in range(pieces - 1)]
    back_units.append((2 * pieces - 1, 2 * pieces - 2))
    states = [None] * len(back_units)
    for p in range(pieces):
        hidden_and_grad(p)
        if p + 1 < pieces:
            grad_act(p + 1)
            out_product(p)
            late_factor(p + 1)
        if p > 0:
            regroup(p - 1)
        if p == pieces - 1:
            out_product(p)
        transposed_back(p)
    early_units = range(pieces - 1)
    late_units = range(pieces - 1, pieces)
    def combine():
        return run(
            functools.partial(combine_kernel, pieces, [len(piece) for piece in out_parts]),
            "combine",
            [((pieces, BLOCK, chan_count), jnp.bfloat16)] * QUARTERS,
            [*out_owns, *[part for piece in out_parts for part in piece]],
        )

    outs = combine()
    regroup(pieces - 1)
    for factor in reversed(plain):
        for u in (*early_units, *late_units):
            plain_back(factor, u)
    arrived = [from_flipped(out, "seq", mask) if mask else out for out, mask in zip(outs, masks)]
    grad_conv, edges = run(
        functools.partial(exit_kernel, back_units),
        "local_factors_back",
        [whole, ((2, chan_count), jnp.bfloat16)],
        [g[0] for g in states] + [g[1] for g in states] + [mixing],
        [pattern],
        [pltpu.VMEM((blocks, BLOCK, chan_count), jnp.float32)] * 2
        + [pltpu.SMEM(pattern.shape, jnp.int32), pltpu.SemaphoreType.DMA],
        limit=LARGE,
    )
    near_grad, far_grad = neighbours(edges, "seq")
    grad_input, _ = run(
        conv_back_kernel,
        "conv_back",
        [whole, ((8, 128), jnp.float32)],
        [grad_conv, far_grad, near_grad, near],
    )
    (layer_out,) = run(assemble_kernel, "assemble", [whole], arrived)
    return (layer_out, convolved, grad_input)


def solution(mesh):
    return jax.shard_map(
        on_device,
        mesh=mesh,
        in_specs=(
            P("seq", "ch"),
            P(None, "ch"),
            P(None, "seq", None, None),
            P(None, "seq"),
            P(None, "ch"),
            P("ch", None),
            P("seq", "ch"),
        ),
        out_specs=(P("seq", "ch"), P("seq", "ch"), P("seq", "ch")),
        check_vma=False,
    )
```

profile of v0, /device:TPU:8, one launch (start us, length us, event | category | flops | bytes accessed | tf_op | source)
XLA Modules:
  0.0 109.4 jit_solution(9727166809863158077)
XLA Ops:
  0.6 0.7 fusion
  1.4 0.7 pad_maximum_fusion
  2.1 4.2 %collective-permute-start = (bf16[5,512]{1,0:T(8,128)(2,1)S(1)}, bf16[5,512]{1,0:T(8,128)(2,1)S(1)}, u32[]{:S(2)}, u32[]{:S(2)}) collective-permute-start(bf16[5,512]{1,0:T(8,128)(2,1)S(1)} %pad_maximum_fusion), channel_id=1, source_target_pairs={{2,4},{4,2},{6,8},{8,6},{10,12},{12,10},{14,16},{16,14},{18,20},{2... | collective-permute-start | bytes 15368 | tf_op jit(solution)/shard_map/ppermute | solution.py:41
  6.3 0.7 collective-permute-start.1
  7.0 1.1 %copy-done.2 = bf16[6,8,64,128]{3,2,1,0:T(8,128)(2,1)S(1)} copy-done((bf16[6,8,64,128]{3,2,1,0:T(8,128)(2,1)S(1)}, bf16[6,8,64,128]{3,2,1,0:T(8,128)(2,1)}, u32[]{:S(2)}) %copy-start.2) | copy-done | bytes 786456
  8.2 1.0 copy-done.3
  9.2 0.7 copy-done.5
  10.0 2.1 %conv_and_local_factors.1 = (bf16[512,512]{1,0:T(8,128)(2,1)}, bf16[2,64,512]{2,1,0:T(8,128)(2,1)S(1)}, bf16[2,64,512]{2,1,0:T(8,128)(2,1)S(1)}, bf16[2,64,512]{2,1,0:T(8,128)(2,1)S(1)}, bf16[2,64,512]{2,1,0:T(8,128)(2,1)S(1)}) custom-call(s32[2,8]{1,0:T(2,128)S(1)} %get-tuple-element.65.refs_0_.refs_5_, bf16[512,512]{1,0:T(8,128)(2,1)S(1)} %get-tuple-element.66.refs_1_, ...), custom_call_target="tpu_custom_call" | custom-call | tf_op jit(solution)/shard_map/conv_and_local_factors/pallas_call | solution.py:60
  12.1 1.5 %collective-permute-start.3 = (bf16[2,64,512]{2,1,0:T(8,128)(2,1)S(1)}, bf16[2,64,512]{2,1,0:T(8,128)(2,1)S(1)}, u32[]{:S(2)}, u32[]{:S(2)}) collective-permute-start(bf16[2,64,512]{2,1,0:T(8,128)(2,1)S(1)} %get-tuple-element.69.refs_0_), channel_id=1, source_target_pairs={{0,2},{2,0},{4,6},{6,4},{8,10},{10,8},{12,14},{14,12},{16,18},{18,... | collective-permute-start | bytes 393224 | tf_op jit(solution)/shard_map/ppermute | solution.py:46
  13.6 1.0 copy-done.4
  14.7 2.7 %collective-permute-start.12 = (bf16[6,64,512]{2,1,0:T(8,128)(2,1)S(1)}, bf16[6,64,512]{2,1,0:T(8,128)(2,1)S(1)}, u32[]{:S(2)}, u32[]{:S(2)}) collective-permute-start(bf16[6,64,512]{2,1,0:T(8,128)(2,1)S(1)} %get-tuple-element.71.refs_3_), channel_id=1, source_target_pairs={{0,16},{2,18},{4,20},{6,22},{8,24},{10,26},{12,28},{14,30},{16,0},... | collective-permute-start | bytes 1179656 | tf_op jit(solution)/shard_map/ppermute | solution.py:46
  17.4 0.7 collective-permute-start.2
  18.3 0.7 collective-permute-start.6
  19.0 1.3 %collective-permute-start.8 = (bf16[4,64,512]{2,1,0:T(8,128)(2,1)S(1)}, bf16[4,64,512]{2,1,0:T(8,128)(2,1)S(1)}, u32[]{:S(2)}, u32[]{:S(2)}) collective-permute-start(bf16[4,64,512]{2,1,0:T(8,128)(2,1)S(1)} %get-tuple-element.73), channel_id=1, source_target_pairs={{0,8},{2,10},{4,12},{6,14},{8,0},{10,2},{12,4},{14,6},{16,24},{18,... | collective-permute-start | bytes 786440 | tf_op jit(solution)/shard_map/ppermute | solution.py:46
  20.3 0.9 collective-permute-start.5
  21.2 2.4 %collective-permute-done.2.refs_1_ = bf16[2,64,512]{2,1,0:T(8,128)(2,1)S(1)} collective-permute-done((bf16[2,64,512]{2,1,0:T(8,128)(2,1)S(1)}, bf16[2,64,512]{2,1,0:T(8,128)(2,1)S(1)}, u32[]{:S(2)}, u32[]{:S(2)}) %collective-permute-start.2) | collective-permute-done | bytes 131104 | tf_op jit(solution)/shard_map/ppermute | solution.py:46
  23.9 0.6 collective-permute-start.4
  24.7 0.7 collective-permute-start.7
  25.4 1.3 %collective-permute-start.11 = (bf16[2,64,512]{2,1,0:T(8,128)(2,1)S(1)}, bf16[2,64,512]{2,1,0:T(8,128)(2,1)S(1)}, u32[]{:S(2)}, u32[]{:S(2)}) collective-permute-start(bf16[2,64,512]{2,1,0:T(8,128)(2,1)S(1)} %get-tuple-element.70.refs_2_.refs_0_), channel_id=1, source_target_pairs={{0,2},{2,0},{4,6},{6,4},{8,10},{10,8},{12,14},{14,12},{16,18},{18,... | collective-permute-start | bytes 393224 | tf_op jit(solution)/shard_map/ppermute | solution.py:46
  27.0 3.2 %collective-permute-done.4.refs_1_ = bf16[2,64,512]{2,1,0:T(8,128)(2,1)S(1)} collective-permute-done((bf16[2,64,512]{2,1,0:T(8,128)(2,1)S(1)}, bf16[2,64,512]{2,1,0:T(8,128)(2,1)S(1)}, u32[]{:S(2)}, u32[]{:S(2)}) %collective-permute-start.4) | collective-permute-done | bytes 131104 | tf_op jit(solution)/shard_map/ppermute | solution.py:46
  30.2 0.5 collective-permute-start.10
  31.0 1.9 %collective-permute-done.8.refs_3_.refs_1_.refs_5_ = bf16[4,64,512]{2,1,0:T(8,128)(2,1)S(1)} collective-permute-done((bf16[4,64,512]{2,1,0:T(8,128)(2,1)S(1)}, bf16[4,64,512]{2,1,0:T(8,128)(2,1)S(1)}, u32[]{:S(2)}, u32[]{:S(2)}) %collective-permute-start.8) | collective-permute-done | bytes 262176 | tf_op jit(solution)/shard_map/ppermute | solution.py:46
  32.9 1.9 %collective-permute-done.7.refs_1_ = bf16[2,64,512]{2,1,0:T(8,128)(2,1)S(1)} collective-permute-done((bf16[2,64,512]{2,1,0:T(8,128)(2,1)S(1)}, bf16[2,64,512]{2,1,0:T(8,128)(2,1)S(1)}, u32[]{:S(2)}, u32[]{:S(2)}) %collective-permute-start.7) | collective-permute-done | bytes 131104 | tf_op jit(solution)/shard_map/ppermute | solution.py:46
  35.1 2.6 %collective-permute-start.13 = (bf16[3,64,512]{2,1,0:T(8,128)(2,1)S(1)}, bf16[3,64,512]{2,1,0:T(8,128)(2,1)S(1)}, u32[]{:S(2)}, u32[]{:S(2)}) collective-permute-start(bf16[3,64,512]{2,1,0:T(8,128)(2,1)S(1)} %forward.1.refs_3_), channel_id=1, source_target_pairs={{0,8},{2,10},{4,12},{6,14},{8,0},{10,2},{12,4},{14,6},{16,24},{18,... | collective-permute-start | bytes 589832 | tf_op jit(solution)/shard_map/ppermute | solution.py:46
  37.7 1.9 %collective-permute-start.9 = (bf16[2,64,512]{2,1,0:T(8,128)(2,1)S(1)}, bf16[2,64,512]{2,1,0:T(8,128)(2,1)S(1)}, u32[]{:S(2)}, u32[]{:S(2)}) collective-permute-start(bf16[2,64,512]{2,1,0:T(8,128)(2,1)S(1)} %get-tuple-element.75.refs_1_), channel_id=1, source_target_pairs={{0,16},{2,18},{4,20},{6,22},{8,24},{10,26},{12,28},{14,30},{16,0},... | collective-permute-start | bytes 393224 | tf_op jit(solution)/shard_map/ppermute | solution.py:46
  39.8 1.0 collective-permute-start.14
  41.1 2.0 %collective-permute-start.17 = (bf16[2,64,512]{2,1,0:T(8,128)(2,1)S(1)}, bf16[2,64,512]{2,1,0:T(8,128)(2,1)S(1)}, u32[]{:S(2)}, u32[]{:S(2)}) collective-permute-start(bf16[2,64,512]{2,1,0:T(8,128)(2,1)S(1)} %factor.14.refs_1_), channel_id=1, source_target_pairs={{0,8},{2,10},{4,12},{6,14},{8,0},{10,2},{12,4},{14,6},{16,24},{18,... | collective-permute-start | bytes 393224 | tf_op jit(solution)/shard_map/ppermute | solution.py:46
  43.2 2.9 %collective-permute-done.9.refs_0_ = bf16[2,64,512]{2,1,0:T(8,128)(2,1)S(1)} collective-permute-done((bf16[2,64,512]{2,1,0:T(8,128)(2,1)S(1)}, bf16[2,64,512]{2,1,0:T(8,128)(2,1)S(1)}, u32[]{:S(2)}, u32[]{:S(2)}) %collective-permute-start.9) | collective-permute-done | bytes 131104 | tf_op jit(solution)/shard_map/ppermute | solution.py:46
  47.3 0.5 collective-permute-start.19
  48.3 2.4 %collective-permute-start.20 = (bf16[2,64,512]{2,1,0:T(8,128)(2,1)S(1)}, bf16[2,64,512]{2,1,0:T(8,128)(2,1)S(1)}, u32[]{:S(2)}, u32[]{:S(2)}) collective-permute-start(bf16[2,64,512]{2,1,0:T(8,128)(2,1)S(1)} %get-tuple-element.79.refs_4_), channel_id=1, source_target_pairs={{0,16},{2,18},{4,20},{6,22},{8,24},{10,26},{12,28},{14,30},{16,0},... | collective-permute-start | bytes 393224 | tf_op jit(solution)/shard_map/ppermute | solution.py:46
  50.6 1.3 %grad_act.2.refs_4_.refs_6_ = bf16[256,2048]{1,0:T(8,128)(2,1)S(1)} custom-call(bf16[256,512]{1,0:T(8,128)(2,1)S(1)} %get-tuple-element.80.refs_0_, bf16[256,512]{1,0:T(8,128)(2,1)S(1)} %collective-permute-done.18.refs_1_, bf16[2048,1024]{1,0:T(8,128)(2,1)S(1)} %copy-done, bf16[256,512]{1,0:T(8,128)(2,1)S(1)} %get-tuple-element.81.refs_3_.refs_0_), custom_call_target="tpu_custom_call" | custom-call | tf_op jit(solution)/shard_map/grad_act/pallas_call | solution.py:60
  52.0 3.6 %mlp_hidden_and_grad.2 = (bf16[256,2048]{1,0:T(8,128)(2,1)S(1)}, f32[256,512]{1,0:T(8,128)S(1)}, bf16[128,512]{1,0:T(8,128)(2,1)S(1)}, bf16[128,512]{1,0:T(8,128)(2,1)S(1)}) custom-call(bf16[128,512]{1,0:T(8,128)(2,1)S(1)} %get-tuple-element.76.refs_0_.refs_1_, bf16[128,512]{1,0:T(8,128)(2,1)S(1)} %get-tuple-element.77.refs_4_.refs_1_.refs_2_, ...), custom_call_target="tpu_custom_call" | custom-call | tf_op jit(solution)/shard_map/mlp_hidden_and_grad/pallas_call | solution.py:60
  55.6 0.5 collective-permute-start.24
  56.1 1.3 %grad_act.3.refs_4_ = bf16[256,2048]{1,0:T(8,128)(2,1)S(1)} custom-call(bf16[256,512]{1,0:T(8,128)(2,1)S(1)} %get-tuple-element.81.refs_3_.refs_0_, bf16[256,512]{1,0:T(8,128)(2,1)S(1)} %collective-permute-done.19.refs_1_, bf16[2048,1024]{1,0:T(8,128)(2,1)S(1)} %copy-done, bf16[128,512]{1,0:T(8,128)(2,1)S(1)} %get-tuple-element.83.refs_3_), custom_call_target="tpu_custom_call" | custom-call | tf_op jit(solution)/shard_map/grad_act/pallas_call | solution.py:60
  57.4 1.3 %mlp_out.2 = (f32[256,512]{1,0:T(8,128)S(1)}, bf16[256,512]{1,0:T(8,128)(2,1)S(1)}) custom-call(bf16[256,2048]{1,0:T(8,128)(2,1)S(1)} %get-tuple-element.82.refs_0_, bf16[128,512]{1,0:T(8,128)(2,1)S(1)} %get-tuple-element.76.refs_0_.refs_1_, bf16[128,512]{1,0:T(8,128)(2,1)S(1)} %get-tuple-element.77.refs_4_.refs_1_.refs_2_, bf16[2048,1024]{1,0:T(8,128)(2,1)S(1)} %copy-done, ...), custom_call_target="tpu_custom_call" | custom-call | tf_op jit(solution)/shard_map/mlp_out/pallas_call | solution.py:60
  59.2 0.4 collective-permute-start.22
  59.7 0.6 late_and_early_back.2
  60.6 1.6 %collective-permute-start.26 = (bf16[64,512]{1,0:T(8,128)(2,1)S(1)}, bf16[64,512]{1,0:T(8,128)(2,1)S(1)}, u32[]{:S(2)}, u32[]{:S(2)}) collective-permute-start(bf16[64,512]{1,0:T(8,128)(2,1)S(1)} %get-tuple-element.95), channel_id=1, source_target_pairs={{0,16},{2,18},{4,20},{6,22},{8,24},{10,26},{12,28},{14,30},{16,0},... | collective-permute-start | bytes 196616 | tf_op jit(solution)/shard_map/ppermute | solution.py:46
  62.2 1.6 %collective-permute-start.27 = (bf16[64,512]{1,0:T(8,128)(2,1)S(1)}, bf16[64,512]{1,0:T(8,128)(2,1)S(1)}, u32[]{:S(2)}, u32[]{:S(2)}) collective-permute-start(bf16[64,512]{1,0:T(8,128)(2,1)S(1)} %get-tuple-element.91.refs_6_), channel_id=1, source_target_pairs={{0,24},{2,26},{4,28},{6,30},{8,16},{10,18},{12,20},{14,22},{16,8},... | collective-permute-start | bytes 196616 | tf_op jit(solution)/shard_map/ppermute | solution.py:46
  63.8 3.7 %mlp_hidden_and_grad.3 = (bf16[256,2048]{1,0:T(8,128)(2,1)S(1)}, f32[256,512]{1,0:T(8,128)S(1)}, bf16[128,512]{1,0:T(8,128)(2,1)S(1)}, bf16[128,512]{1,0:T(8,128)(2,1)S(1)}) custom-call(bf16[128,512]{1,0:T(8,128)(2,1)S(1)} %get-tuple-element.87.refs_0_.refs_1_, bf16[128,512]{1,0:T(8,128)(2,1)S(1)} %get-tuple-element.88.refs_8_.refs_1_.refs_2_, ...), custom_call_target="tpu_custom_call" | custom-call | tf_op jit(solution)/shard_map/mlp_hidden_and_grad/pallas_call | solution.py:60
  67.7 0.5 collective-permute-start.32
  68.2 1.9 %collective-permute-done.27.refs_3_ = bf16[64,512]{1,0:T(8,128)(2,1)S(1)} collective-permute-done((bf16[64,512]{1,0:T(8,128)(2,1)S(1)}, bf16[64,512]{1,0:T(8,128)(2,1)S(1)}, u32[]{:S(2)}, u32[]{:S(2)}) %collective-permute-start.27) | collective-permute-done | bytes 65568 | tf_op jit(solution)/shard_map/ppermute | solution.py:46
  70.4 1.3 %mlp_out.3 = (f32[256,512]{1,0:T(8,128)S(1)}, bf16[128,512]{1,0:T(8,128)(2,1)S(1)}, bf16[128,512]{1,0:T(8,128)(2,1)S(1)}) custom-call(bf16[256,2048]{1,0:T(8,128)(2,1)S(1)} %get-tuple-element.92.refs_0_, bf16[128,512]{1,0:T(8,128)(2,1)S(1)} %get-tuple-element.87.refs_0_.refs_1_, bf16[128,512]{1,0:T(8,128)(2,1)S(1)} %get-tuple-element.88.refs_8_.refs_1_.refs_2_, ...), custom_call_target="tpu_custom_call" | custom-call | tf_op jit(solution)/shard_map/mlp_out/pallas_call | solution.py:60
  71.7 0.5 collective-permute-start.30
  72.2 0.6 late_and_early_back.3
  72.8 0.4 collective-permute-start.37
  73.3 1.7 %collective-permute-start.38 = (bf16[64,512]{1,0:T(8,128)(2,1)S(1)}, bf16[64,512]{1,0:T(8,128)(2,1)S(1)}, u32[]{:S(2)}, u32[]{:S(2)}) collective-permute-start(bf16[64,512]{1,0:T(8,128)(2,1)S(1)} %get-tuple-element.111), channel_id=1, source_target_pairs={{0,16},{2,18},{4,20},{6,22},{8,24},{10,26},{12,28},{14,30},{16,0},... | collective-permute-start | bytes 196616 | tf_op jit(solution)/shard_map/ppermute | solution.py:46
  75.0 1.4 %collective-permute-start.39 = (bf16[64,512]{1,0:T(8,128)(2,1)S(1)}, bf16[64,512]{1,0:T(8,128)(2,1)S(1)}, u32[]{:S(2)}, u32[]{:S(2)}) collective-permute-start(bf16[64,512]{1,0:T(8,128)(2,1)S(1)} %get-tuple-element.103.refs_5_), channel_id=1, source_target_pairs={{0,24},{2,26},{4,28},{6,30},{8,16},{10,18},{12,20},{14,22},{16,8},... | collective-permute-start | bytes 196616 | tf_op jit(solution)/shard_map/ppermute | solution.py:46
  76.4 0.8 collective-permute-start.36
  77.7 2.1 %collective-permute-done.38.refs_2_ = bf16[64,512]{1,0:T(8,128)(2,1)S(1)} collective-permute-done((bf16[64,512]{1,0:T(8,128)(2,1)S(1)}, bf16[64,512]{1,0:T(8,128)(2,1)S(1)}, u32[]{:S(2)}, u32[]{:S(2)}) %collective-permute-start.38) | collective-permute-done | bytes 65568 | tf_op jit(solution)/shard_map/ppermute | solution.py:46
  79.8 2.5 %collective-permute-done.39.refs_3_ = bf16[64,512]{1,0:T(8,128)(2,1)S(1)} collective-permute-done((bf16[64,512]{1,0:T(8,128)(2,1)S(1)}, bf16[64,512]{1,0:T(8,128)(2,1)S(1)}, u32[]{:S(2)}, u32[]{:S(2)}) %collective-permute-start.39) | collective-permute-done | bytes 65568 | tf_op jit(solution)/shard_map/ppermute | solution.py:46
  82.6 0.9 collective-permute-start.41
  84.2 1.9 %collective-permute-start.40 = (bf16[4,64,512]{2,1,0:T(8,128)(2,1)S(1)}, bf16[4,64,512]{2,1,0:T(8,128)(2,1)S(1)}, u32[]{:S(2)}, u32[]{:S(2)}) collective-permute-start(bf16[4,64,512]{2,1,0:T(8,128)(2,1)S(1)} %get-tuple-element.114.refs_3_), channel_id=1, source_target_pairs={{0,2},{2,0},{4,6},{6,4},{8,10},{10,8},{12,14},{14,12},{16,18},{18,... | collective-permute-start | bytes 786440 | tf_op jit(solution)/shard_map/ppermute | solution.py:46
  86.1 4.3 %collective-permute-done.41.refs_1_ = bf16[4,64,512]{2,1,0:T(8,128)(2,1)S(1)} collective-permute-done((bf16[4,64,512]{2,1,0:T(8,128)(2,1)S(1)}, bf16[4,64,512]{2,1,0:T(8,128)(2,1)S(1)}, u32[]{:S(2)}, u32[]{:S(2)}) %collective-permute-start.41) | collective-permute-done | bytes 262176 | tf_op jit(solution)/shard_map/ppermute | solution.py:46
  90.7 1.9 %collective-permute-start.42 = (bf16[4,64,512]{2,1,0:T(8,128)(2,1)S(1)}, bf16[4,64,512]{2,1,0:T(8,128)(2,1)S(1)}, u32[]{:S(2)}, u32[]{:S(2)}) collective-permute-start(bf16[4,64,512]{2,1,0:T(8,128)(2,1)S(1)} %get-tuple-element.116.refs_3_), channel_id=1, source_target_pairs={{0,2},{2,0},{4,6},{6,4},{8,10},{10,8},{12,14},{14,12},{16,18},{18,... | collective-permute-start | bytes 786440 | tf_op jit(solution)/shard_map/ppermute | solution.py:46
  93.1 2.5 %collective-permute-start.34 = (bf16[2,64,512]{2,1,0:T(8,128)(2,1)S(1)}, bf16[2,64,512]{2,1,0:T(8,128)(2,1)S(1)}, u32[]{:S(2)}, u32[]{:S(2)}) collective-permute-start(bf16[2,64,512]{2,1,0:T(8,128)(2,1)S(1)} %get-tuple-element.106), channel_id=1, source_target_pairs={{0,16},{2,18},{4,20},{6,22},{8,24},{10,26},{12,28},{14,30},{16,0},... | collective-permute-start | bytes 393224 | tf_op jit(solution)/shard_map/ppermute | solution.py:46
  95.5 0.6 collective-permute-start.35
  96.5 1.1 %collective-permute-done.42.refs_1_ = bf16[4,64,512]{2,1,0:T(8,128)(2,1)S(1)} collective-permute-done((bf16[4,64,512]{2,1,0:T(8,128)(2,1)S(1)}, bf16[4,64,512]{2,1,0:T(8,128)(2,1)S(1)}, u32[]{:S(2)}, u32[]{:S(2)}) %collective-permute-start.42) | collective-permute-done | bytes 262176 | tf_op jit(solution)/shard_map/ppermute | solution.py:46
  98.0 1.2 %local_factors_back.1 = (bf16[512,512]{1,0:T(8,128)(2,1)S(1)}, bf16[2,512]{1,0:T(2,128)(2,1)S(1)}) custom-call(s32[2,8]{1,0:T(2,128)S(1)} %get-tuple-element.65.refs_0_.refs_5_, f32[4,64,512]{2,1,0:T(8,128)S(1)} %get-tuple-element.117.refs_1_, f32[4,64,512]{2,1,0:T(8,128)S(1)} %get-tuple-element.120.refs_2_, f32[4,64,512]{2,1,0:T(8,128)S(1)} %get-tuple-element.119.refs_3_, ...), custom_call_target="tpu_custom_call" | custom-call | tf_op jit(solution)/shard_map/local_factors_back/pallas_call | solution.py:60
  99.2 4.5 %collective-permute-start.43 = (bf16[2,512]{1,0:T(2,128)(2,1)S(1)}, bf16[2,512]{1,0:T(2,128)(2,1)S(1)}, u32[]{:S(2)}, u32[]{:S(2)}) collective-permute-start(bf16[2,512]{1,0:T(2,128)(2,1)S(1)} %get-tuple-element.123.refs_4_), channel_id=1, source_target_pairs={{2,4},{4,2},{6,8},{8,6},{10,12},{12,10},{14,16},{16,14},{18,20},{2... | collective-permute-start | bytes 6152 | tf_op jit(solution)/shard_map/ppermute | solution.py:41
  103.8 2.6 %collective-permute-done.43.refs_1_ = bf16[2,512]{1,0:T(2,128)(2,1)S(1)} collective-permute-done((bf16[2,512]{1,0:T(2,128)(2,1)S(1)}, bf16[2,512]{1,0:T(2,128)(2,1)S(1)}, u32[]{:S(2)}, u32[]{:S(2)}) %collective-permute-start.43) | collective-permute-done | bytes 2080 | tf_op jit(solution)/shard_map/ppermute | solution.py:41
  106.4 0.9 collective-permute-done.44.refs_2_
  107.4 1.2 %conv_back.1 = (bf16[512,512]{1,0:T(8,128)(2,1)}, f32[8,128]{1,0:T(8,128)S(1)}) custom-call(bf16[512,512]{1,0:T(8,128)(2,1)S(1)} %get-tuple-element.122.refs_0_, bf16[2,512]{1,0:T(2,128)(2,1)S(1)} %collective-permute-done.43.refs_1_, bf16[2,512]{1,0:T(2,128)(2,1)S(1)} %collective-permute-done.44.refs_2_, bf16[5,512]{1,0:T(8,128)(2,1)S(1)} %collective-permute-done.1.refs_3_, ...), custom_call_target="tpu_custom_call" | custom-call | tf_op jit(solution)/shard_map/conv_back/pallas_call | solution.py:60
  108.5 0.8 assemble.1
  (76 shorter events, 8.7 us)
Async XLA Ops:
  2.1 8.0 %collective-permute-start = (bf16[5,512]{1,0:T(8,128)(2,1)S(1)}, bf16[5,512]{1,0:T(8,128)(2,1)S(1)}, u32[]{:S(2)}, u32[]{:S(2)}) collective-permute-start(bf16[5,512]{1,0:T(8,128)(2,1)S(1)} %pad_maximum_fusion), channel_id=1, source_target_pairs={{2,4},{4,2},{6,8},{8,6},{10,12},{12,10},{14,16},{16,14},{18,20},{2... | collective-permute-start | bytes 15368 | tf_op jit(solution)/shard_map/ppermute | solution.py:41
  6.3 3.7 %collective-permute-start.1 = (bf16[5,512]{1,0:T(8,128)(2,1)S(1)}, bf16[5,512]{1,0:T(8,128)(2,1)S(1)}, u32[]{:S(2)}, u32[]{:S(2)}) collective-permute-start(bf16[5,512]{1,0:T(8,128)(2,1)S(1)} %pad_maximum_fusion), channel_id=1, source_target_pairs={{0,2},{2,0},{4,6},{6,4},{8,10},{10,8},{12,14},{14,12},{16,18},{18,... | collective-permute-start | bytes 15368 | tf_op jit(solution)/shard_map/ppermute | solution.py:37
  7.0 1.1 %copy-start.2 = (bf16[6,8,64,128]{3,2,1,0:T(8,128)(2,1)S(1)}, bf16[6,8,64,128]{3,2,1,0:T(8,128)(2,1)}, u32[]{:S(2)}) copy-start(bf16[6,8,64,128]{3,2,1,0:T(8,128)(2,1)} %refs_0_.1) | copy-start | bytes 2359300
  8.2 1.0 copy-start.3
  9.2 0.7 copy-start.5
  12.1 5.9 %collective-permute-start.3 = (bf16[2,64,512]{2,1,0:T(8,128)(2,1)S(1)}, bf16[2,64,512]{2,1,0:T(8,128)(2,1)S(1)}, u32[]{:S(2)}, u32[]{:S(2)}) collective-permute-start(bf16[2,64,512]{2,1,0:T(8,128)(2,1)S(1)} %get-tuple-element.69.refs_0_), channel_id=1, source_target_pairs={{0,2},{2,0},{4,6},{6,4},{8,10},{10,8},{12,14},{14,12},{16,18},{18,... | collective-permute-start | bytes 393224 | tf_op jit(solution)/shard_map/ppermute | solution.py:46
  13.6 1.0 copy-start.4
  14.7 20.4 %collective-permute-start.12 = (bf16[6,64,512]{2,1,0:T(8,128)(2,1)S(1)}, bf16[6,64,512]{2,1,0:T(8,128)(2,1)S(1)}, u32[]{:S(2)}, u32[]{:S(2)}) collective-permute-start(bf16[6,64,512]{2,1,0:T(8,128)(2,1)S(1)} %get-tuple-element.71.refs_3_), channel_id=1, source_target_pairs={{0,16},{2,18},{4,20},{6,22},{8,24},{10,26},{12,28},{14,30},{16,0},... | collective-permute-start | bytes 1179656 | tf_op jit(solution)/shard_map/ppermute | solution.py:46
  17.4 6.2 %collective-permute-start.2 = (bf16[2,64,512]{2,1,0:T(8,128)(2,1)S(1)}, bf16[2,64,512]{2,1,0:T(8,128)(2,1)S(1)}, u32[]{:S(2)}, u32[]{:S(2)}) collective-permute-start(bf16[2,64,512]{2,1,0:T(8,128)(2,1)S(1)} %get-tuple-element.68.refs_0_), channel_id=1, source_target_pairs={{0,2},{2,0},{4,6},{6,4},{8,10},{10,8},{12,14},{14,12},{16,18},{18,... | collective-permute-start | bytes 393224 | tf_op jit(solution)/shard_map/ppermute | solution.py:46
  18.3 6.2 %collective-permute-start.6 = (bf16[2,64,512]{2,1,0:T(8,128)(2,1)S(1)}, bf16[2,64,512]{2,1,0:T(8,128)(2,1)S(1)}, u32[]{:S(2)}, u32[]{:S(2)}) collective-permute-start(bf16[2,64,512]{2,1,0:T(8,128)(2,1)S(1)} %factor.8.refs_3_.refs_0_), channel_id=1, source_target_pairs={{0,4},{2,6},{4,0},{6,2},{8,12},{10,14},{12,8},{14,10},{16,20},{18,... | collective-permute-start | bytes 393224 | tf_op jit(solution)/shard_map/ppermute | solution.py:46
  19.0 13.9 %collective-permute-start.8 = (bf16[4,64,512]{2,1,0:T(8,128)(2,1)S(1)}, bf16[4,64,512]{2,1,0:T(8,128)(2,1)S(1)}, u32[]{:S(2)}, u32[]{:S(2)}) collective-permute-start(bf16[4,64,512]{2,1,0:T(8,128)(2,1)S(1)} %get-tuple-element.73), channel_id=1, source_target_pairs={{0,8},{2,10},{4,12},{6,14},{8,0},{10,2},{12,4},{14,6},{16,24},{18,... | collective-permute-start | bytes 786440 | tf_op jit(solution)/shard_map/ppermute | solution.py:46
  20.3 5.1 %collective-permute-start.5 = (bf16[2,64,512]{2,1,0:T(8,128)(2,1)S(1)}, bf16[2,64,512]{2,1,0:T(8,128)(2,1)S(1)}, u32[]{:S(2)}, u32[]{:S(2)}) collective-permute-start(bf16[2,64,512]{2,1,0:T(8,128)(2,1)S(1)} %get-tuple-element.72.refs_0_), channel_id=1, source_target_pairs={{0,2},{2,0},{4,6},{6,4},{8,10},{10,8},{12,14},{14,12},{16,18},{18,... | collective-permute-start | bytes 393224 | tf_op jit(solution)/shard_map/ppermute | solution.py:46
  23.9 6.4 %collective-permute-start.4 = (bf16[2,64,512]{2,1,0:T(8,128)(2,1)S(1)}, bf16[2,64,512]{2,1,0:T(8,128)(2,1)S(1)}, u32[]{:S(2)}, u32[]{:S(2)}) collective-permute-start(bf16[2,64,512]{2,1,0:T(8,128)(2,1)S(1)} %factor.9.refs_3_.refs_0_), channel_id=1, source_target_pairs={{0,4},{2,6},{4,0},{6,2},{8,12},{10,14},{12,8},{14,10},{16,20},{18,... | collective-permute-start | bytes 393224 | tf_op jit(solution)/shard_map/ppermute | solution.py:46
  24.7 10.0 %collective-permute-start.7 = (bf16[2,64,512]{2,1,0:T(8,128)(2,1)S(1)}, bf16[2,64,512]{2,1,0:T(8,128)(2,1)S(1)}, u32[]{:S(2)}, u32[]{:S(2)}) collective-permute-start(bf16[2,64,512]{2,1,0:T(8,128)(2,1)S(1)} %factor.10.refs_3_), channel_id=1, source_target_pairs={{0,8},{2,10},{4,12},{6,14},{8,0},{10,2},{12,4},{14,6},{16,24},{18,... | collective-permute-start | bytes 393224 | tf_op jit(solution)/shard_map/ppermute | solution.py:46
  25.4 14.1 %collective-permute-start.11 = (bf16[2,64,512]{2,1,0:T(8,128)(2,1)S(1)}, bf16[2,64,512]{2,1,0:T(8,128)(2,1)S(1)}, u32[]{:S(2)}, u32[]{:S(2)}) collective-permute-start(bf16[2,64,512]{2,1,0:T(8,128)(2,1)S(1)} %get-tuple-element.70.refs_2_.refs_0_), channel_id=1, source_target_pairs={{0,2},{2,0},{4,6},{6,4},{8,10},{10,8},{12,14},{14,12},{16,18},{18,... | collective-permute-start | bytes 393224 | tf_op jit(solution)/shard_map/ppermute | solution.py:46
  30.2 10.6 %collective-permute-start.10 = (bf16[2,64,512]{2,1,0:T(8,128)(2,1)S(1)}, bf16[2,64,512]{2,1,0:T(8,128)(2,1)S(1)}, u32[]{:S(2)}, u32[]{:S(2)}) collective-permute-start(bf16[2,64,512]{2,1,0:T(8,128)(2,1)S(1)} %factor.11.refs_3_.refs_0_), channel_id=1, source_target_pairs={{0,4},{2,6},{4,0},{6,2},{8,12},{10,14},{12,8},{14,10},{16,20},{18,... | collective-permute-start | bytes 393224 | tf_op jit(solution)/shard_map/ppermute | solution.py:46
  35.1 15.5 %copy-start = (bf16[2048,1024]{1,0:T(8,128)(2,1)S(1)}, bf16[2048,1024]{1,0:T(8,128)(2,1)}, u32[]{:S(2)}) copy-start(bf16[2048,1024]{1,0:T(8,128)(2,1)} %refs_3_.3) | copy-start | bytes 12582916
  35.1 11.2 %collective-permute-start.13 = (bf16[3,64,512]{2,1,0:T(8,128)(2,1)S(1)}, bf16[3,64,512]{2,1,0:T(8,128)(2,1)S(1)}, u32[]{:S(2)}, u32[]{:S(2)}) collective-permute-start(bf16[3,64,512]{2,1,0:T(8,128)(2,1)S(1)} %forward.1.refs_3_), channel_id=1, source_target_pairs={{0,8},{2,10},{4,12},{6,14},{8,0},{10,2},{12,4},{14,6},{16,24},{18,... | collective-permute-start | bytes 589832 | tf_op jit(solution)/shard_map/ppermute | solution.py:46
  37.7 8.3 %collective-permute-start.9 = (bf16[2,64,512]{2,1,0:T(8,128)(2,1)S(1)}, bf16[2,64,512]{2,1,0:T(8,128)(2,1)S(1)}, u32[]{:S(2)}, u32[]{:S(2)}) collective-permute-start(bf16[2,64,512]{2,1,0:T(8,128)(2,1)S(1)} %get-tuple-element.75.refs_1_), channel_id=1, source_target_pairs={{0,16},{2,18},{4,20},{6,22},{8,24},{10,26},{12,28},{14,30},{16,0},... | collective-permute-start | bytes 393224 | tf_op jit(solution)/shard_map/ppermute | solution.py:46
  39.8 6.2 %collective-permute-start.14 = (bf16[2,64,512]{2,1,0:T(8,128)(2,1)S(1)}, bf16[2,64,512]{2,1,0:T(8,128)(2,1)S(1)}, u32[]{:S(2)}, u32[]{:S(2)}) collective-permute-start(bf16[2,64,512]{2,1,0:T(8,128)(2,1)S(1)} %factor.13.refs_3_.refs_0_), channel_id=1, source_target_pairs={{0,4},{2,6},{4,0},{6,2},{8,12},{10,14},{12,8},{14,10},{16,20},{18,... | collective-permute-start | bytes 393224 | tf_op jit(solution)/shard_map/ppermute | solution.py:46
  41.1 5.6 %collective-permute-start.17 = (bf16[2,64,512]{2,1,0:T(8,128)(2,1)S(1)}, bf16[2,64,512]{2,1,0:T(8,128)(2,1)S(1)}, u32[]{:S(2)}, u32[]{:S(2)}) collective-permute-start(bf16[2,64,512]{2,1,0:T(8,128)(2,1)S(1)} %factor.14.refs_1_), channel_id=1, source_target_pairs={{0,8},{2,10},{4,12},{6,14},{8,0},{10,2},{12,4},{14,6},{16,24},{18,... | collective-permute-start | bytes 393224 | tf_op jit(solution)/shard_map/ppermute | solution.py:46
  46.8 5.2 %copy-start.1 = (bf16[1024,2048]{1,0:T(8,128)(2,1)S(1)}, bf16[1024,2048]{1,0:T(8,128)(2,1)}, u32[]{:S(2)}) copy-start(bf16[1024,2048]{1,0:T(8,128)(2,1)} %refs_5_.3) | copy-start | bytes 12582916
  47.2 3.5 %collective-permute-start.18 = (bf16[256,512]{1,0:T(8,128)(2,1)S(1)}, bf16[256,512]{1,0:T(8,128)(2,1)S(1)}, u32[]{:S(2)}, u32[]{:S(2)}) collective-permute-start(bf16[256,512]{1,0:T(8,128)(2,1)S(1)} %get-tuple-element.80.refs_0_), channel_id=1, source_target_pairs={{1,0},{0,1},{3,2},{2,3},{5,4},{4,5},{7,6},{6,7},{9,8},{8,9},{11,10... | collective-permute-start | bytes 786440 | tf_op jit(solution)/shard_map/ppermute | solution.py:51
  47.3 8.9 %collective-permute-start.19 = (bf16[256,512]{1,0:T(8,128)(2,1)S(1)}, bf16[256,512]{1,0:T(8,128)(2,1)S(1)}, u32[]{:S(2)}, u32[]{:S(2)}) collective-permute-start(bf16[256,512]{1,0:T(8,128)(2,1)S(1)} %get-tuple-element.81.refs_3_.refs_0_), channel_id=1, source_target_pairs={{1,0},{0,1},{3,2},{2,3},{5,4},{4,5},{7,6},{6,7},{9,8},{8,9},{11,10... | collective-permute-start | bytes 786440 | tf_op jit(solution)/shard_map/ppermute | solution.py:51
  47.7 4.2 %collective-permute-start.15 = (bf16[128,512]{1,0:T(8,128)(2,1)S(1)}, bf16[128,512]{1,0:T(8,128)(2,1)S(1)}, u32[]{:S(2)}, u32[]{:S(2)}) collective-permute-start(bf16[128,512]{1,0:T(8,128)(2,1)S(1)} %get-tuple-element.76.refs_0_.refs_1_), channel_id=1, source_target_pairs={{1,0},{0,1},{3,2},{2,3},{5,4},{4,5},{7,6},{6,7},{9,8},{8,9},{11,10... | collective-permute-start | bytes 393224 | tf_op jit(solution)/shard_map/ppermute | solution.py:51
  47.8 4.1 %collective-permute-start.16 = (bf16[128,512]{1,0:T(8,128)(2,1)S(1)}, bf16[128,512]{1,0:T(8,128)(2,1)S(1)}, u32[]{:S(2)}, u32[]{:S(2)}) collective-permute-start(bf16[128,512]{1,0:T(8,128)(2,1)S(1)} %get-tuple-element.77.refs_4_.refs_1_.refs_2_), channel_id=1, source_target_pairs={{1,0},{0,1},{3,2},{2,3},{5,4},{4,5},{7,6},{6,7},{9,8},{8,9},{11,10... | collective-permute-start | bytes 393224 | tf_op jit(solution)/shard_map/ppermute | solution.py:51
  48.3 10.4 %collective-permute-start.20 = (bf16[2,64,512]{2,1,0:T(8,128)(2,1)S(1)}, bf16[2,64,512]{2,1,0:T(8,128)(2,1)S(1)}, u32[]{:S(2)}, u32[]{:S(2)}) collective-permute-start(bf16[2,64,512]{2,1,0:T(8,128)(2,1)S(1)} %get-tuple-element.79.refs_4_), channel_id=1, source_target_pairs={{0,16},{2,18},{4,20},{6,22},{8,24},{10,26},{12,28},{14,30},{16,0},... | collective-permute-start | bytes 393224 | tf_op jit(solution)/shard_map/ppermute | solution.py:46
  55.5 4.2 %collective-permute-start.23 = (bf16[128,512]{1,0:T(8,128)(2,1)S(1)}, bf16[128,512]{1,0:T(8,128)(2,1)S(1)}, u32[]{:S(2)}, u32[]{:S(2)}) collective-permute-start(bf16[128,512]{1,0:T(8,128)(2,1)S(1)} %get-tuple-element.90), channel_id=1, source_target_pairs={{1,0},{0,1},{3,2},{2,3},{5,4},{4,5},{7,6},{6,7},{9,8},{8,9},{11,10... | collective-permute-start | bytes 393224 | tf_op jit(solution)/shard_map/ppermute | solution.py:51
  55.6 4.1 %collective-permute-start.24 = (bf16[128,512]{1,0:T(8,128)(2,1)S(1)}, bf16[128,512]{1,0:T(8,128)(2,1)S(1)}, u32[]{:S(2)}, u32[]{:S(2)}) collective-permute-start(bf16[128,512]{1,0:T(8,128)(2,1)S(1)} %get-tuple-element.83.refs_3_), channel_id=1, source_target_pairs={{1,0},{0,1},{3,2},{2,3},{5,4},{4,5},{7,6},{6,7},{9,8},{8,9},{11,10... | collective-permute-start | bytes 393224 | tf_op jit(solution)/shard_map/ppermute | solution.py:51
  59.0 3.2 %collective-permute-start.21 = (bf16[128,512]{1,0:T(8,128)(2,1)S(1)}, bf16[128,512]{1,0:T(8,128)(2,1)S(1)}, u32[]{:S(2)}, u32[]{:S(2)}) collective-permute-start(bf16[128,512]{1,0:T(8,128)(2,1)S(1)} %get-tuple-element.87.refs_0_.refs_1_), channel_id=1, source_target_pairs={{1,0},{0,1},{3,2},{2,3},{5,4},{4,5},{7,6},{6,7},{9,8},{8,9},{11,10... | collective-permute-start | bytes 393224 | tf_op jit(solution)/shard_map/ppermute | solution.py:51
  59.2 4.7 %collective-permute-start.22 = (bf16[128,512]{1,0:T(8,128)(2,1)S(1)}, bf16[128,512]{1,0:T(8,128)(2,1)S(1)}, u32[]{:S(2)}, u32[]{:S(2)}) collective-permute-start(bf16[128,512]{1,0:T(8,128)(2,1)S(1)} %get-tuple-element.88.refs_8_.refs_1_.refs_2_), channel_id=1, source_target_pairs={{1,0},{0,1},{3,2},{2,3},{5,4},{4,5},{7,6},{6,7},{9,8},{8,9},{11,10... | collective-permute-start | bytes 393224 | tf_op jit(solution)/shard_map/ppermute | solution.py:51
  59.6 15.4 %collective-permute-start.28 = (bf16[256,512]{1,0:T(8,128)(2,1)S(1)}, bf16[256,512]{1,0:T(8,128)(2,1)S(1)}, u32[]{:S(2)}, u32[]{:S(2)}) collective-permute-start(bf16[256,512]{1,0:T(8,128)(2,1)S(1)} %get-tuple-element.86.refs_6_), channel_id=1, source_target_pairs={{1,0},{0,1},{3,2},{2,3},{5,4},{4,5},{7,6},{6,7},{9,8},{8,9},{11,10... | collective-permute-start | bytes 786440 | tf_op jit(solution)/shard_map/ppermute | solution.py:51
  60.3 7.4 %collective-permute-start.25 = (bf16[64,512]{1,0:T(8,128)(2,1)S(1)}, bf16[64,512]{1,0:T(8,128)(2,1)S(1)}, u32[]{:S(2)}, u32[]{:S(2)}) collective-permute-start(bf16[64,512]{1,0:T(8,128)(2,1)S(1)} %get-tuple-element.94), channel_id=1, source_target_pairs={{0,8},{2,10},{4,12},{6,14},{8,0},{10,2},{12,4},{14,6},{16,24},{18,... | collective-permute-start | bytes 196616 | tf_op jit(solution)/shard_map/ppermute | solution.py:46
  60.6 7.5 %collective-permute-start.26 = (bf16[64,512]{1,0:T(8,128)(2,1)S(1)}, bf16[64,512]{1,0:T(8,128)(2,1)S(1)}, u32[]{:S(2)}, u32[]{:S(2)}) collective-permute-start(bf16[64,512]{1,0:T(8,128)(2,1)S(1)} %get-tuple-element.95), channel_id=1, source_target_pairs={{0,16},{2,18},{4,20},{6,22},{8,24},{10,26},{12,28},{14,30},{16,0},... | collective-permute-start | bytes 196616 | tf_op jit(solution)/shard_map/ppermute | solution.py:46
  62.2 7.8 %collective-permute-start.27 = (bf16[64,512]{1,0:T(8,128)(2,1)S(1)}, bf16[64,512]{1,0:T(8,128)(2,1)S(1)}, u32[]{:S(2)}, u32[]{:S(2)}) collective-permute-start(bf16[64,512]{1,0:T(8,128)(2,1)S(1)} %get-tuple-element.91.refs_6_), channel_id=1, source_target_pairs={{0,24},{2,26},{4,28},{6,30},{8,16},{10,18},{12,20},{14,22},{16,8},... | collective-permute-start | bytes 196616 | tf_op jit(solution)/shard_map/ppermute | solution.py:46
  67.6 4.7 %collective-permute-start.31 = (bf16[128,512]{1,0:T(8,128)(2,1)S(1)}, bf16[128,512]{1,0:T(8,128)(2,1)S(1)}, u32[]{:S(2)}, u32[]{:S(2)}) collective-permute-start(bf16[128,512]{1,0:T(8,128)(2,1)S(1)} %get-tuple-element.102), channel_id=1, source_target_pairs={{1,0},{0,1},{3,2},{2,3},{5,4},{4,5},{7,6},{6,7},{9,8},{8,9},{11,10... | collective-permute-start | bytes 393224 | tf_op jit(solution)/shard_map/ppermute | solution.py:51
  67.7 4.6 %collective-permute-start.32 = (bf16[128,512]{1,0:T(8,128)(2,1)S(1)}, bf16[128,512]{1,0:T(8,128)(2,1)S(1)}, u32[]{:S(2)}, u32[]{:S(2)}) collective-permute-start(bf16[128,512]{1,0:T(8,128)(2,1)S(1)} %get-tuple-element.96.refs_5_), channel_id=1, source_target_pairs={{1,0},{0,1},{3,2},{2,3},{5,4},{4,5},{7,6},{6,7},{9,8},{8,9},{11,10... | collective-permute-start | bytes 393224 | tf_op jit(solution)/shard_map/ppermute | solution.py:51
  71.7 4.7 %collective-permute-start.29 = (bf16[128,512]{1,0:T(8,128)(2,1)S(1)}, bf16[128,512]{1,0:T(8,128)(2,1)S(1)}, u32[]{:S(2)}, u32[]{:S(2)}) collective-permute-start(bf16[128,512]{1,0:T(8,128)(2,1)S(1)} %get-tuple-element.99), channel_id=1, source_target_pairs={{1,0},{0,1},{3,2},{2,3},{5,4},{4,5},{7,6},{6,7},{9,8},{8,9},{11,10... | collective-permute-start | bytes 393224 | tf_op jit(solution)/shard_map/ppermute | solution.py:51
  71.7 5.4 %collective-permute-start.30 = (bf16[128,512]{1,0:T(8,128)(2,1)S(1)}, bf16[128,512]{1,0:T(8,128)(2,1)S(1)}, u32[]{:S(2)}, u32[]{:S(2)}) collective-permute-start(bf16[128,512]{1,0:T(8,128)(2,1)S(1)} %get-tuple-element.100.refs_8_), channel_id=1, source_target_pairs={{1,0},{0,1},{3,2},{2,3},{5,4},{4,5},{7,6},{6,7},{9,8},{8,9},{11,10... | collective-permute-start | bytes 393224 | tf_op jit(solution)/shard_map/ppermute | solution.py:51
  72.8 4.8 %collective-permute-start.37 = (bf16[64,512]{1,0:T(8,128)(2,1)S(1)}, bf16[64,512]{1,0:T(8,128)(2,1)S(1)}, u32[]{:S(2)}, u32[]{:S(2)}) collective-permute-start(bf16[64,512]{1,0:T(8,128)(2,1)S(1)} %get-tuple-element.110), channel_id=1, source_target_pairs={{0,8},{2,10},{4,12},{6,14},{8,0},{10,2},{12,4},{14,6},{16,24},{18,... | collective-permute-start | bytes 196616 | tf_op jit(solution)/shard_map/ppermute | solution.py:46
  73.3 6.5 %collective-permute-start.38 = (bf16[64,512]{1,0:T(8,128)(2,1)S(1)}, bf16[64,512]{1,0:T(8,128)(2,1)S(1)}, u32[]{:S(2)}, u32[]{:S(2)}) collective-permute-start(bf16[64,512]{1,0:T(8,128)(2,1)S(1)} %get-tuple-element.111), channel_id=1, source_target_pairs={{0,16},{2,18},{4,20},{6,22},{8,24},{10,26},{12,28},{14,30},{16,0},... | collective-permute-start | bytes 196616 | tf_op jit(solution)/shard_map/ppermute | solution.py:46
  75.0 7.3 %collective-permute-start.39 = (bf16[64,512]{1,0:T(8,128)(2,1)S(1)}, bf16[64,512]{1,0:T(8,128)(2,1)S(1)}, u32[]{:S(2)}, u32[]{:S(2)}) collective-permute-start(bf16[64,512]{1,0:T(8,128)(2,1)S(1)} %get-tuple-element.103.refs_5_), channel_id=1, source_target_pairs={{0,24},{2,26},{4,28},{6,30},{8,16},{10,18},{12,20},{14,22},{16,8},... | collective-permute-start | bytes 196616 | tf_op jit(solution)/shard_map/ppermute | solution.py:46
  76.4 7.5 %collective-permute-start.36 = (bf16[4,64,512]{2,1,0:T(8,128)(2,1)S(1)}, bf16[4,64,512]{2,1,0:T(8,128)(2,1)S(1)}, u32[]{:S(2)}, u32[]{:S(2)}) collective-permute-start(bf16[4,64,512]{2,1,0:T(8,128)(2,1)S(1)} %get-tuple-element.97.refs_4_), channel_id=1, source_target_pairs={{0,4},{2,6},{4,0},{6,2},{8,12},{10,14},{12,8},{14,10},{16,20},{18,... | collective-permute-start | bytes 786440 | tf_op jit(solution)/shard_map/ppermute | solution.py:46
  82.6 7.8 %collective-permute-start.41 = (bf16[4,64,512]{2,1,0:T(8,128)(2,1)S(1)}, bf16[4,64,512]{2,1,0:T(8,128)(2,1)S(1)}, u32[]{:S(2)}, u32[]{:S(2)}) collective-permute-start(bf16[4,64,512]{2,1,0:T(8,128)(2,1)S(1)} %get-tuple-element.112.refs_3_), channel_id=1, source_target_pairs={{0,4},{2,6},{4,0},{6,2},{8,12},{10,14},{12,8},{14,10},{16,20},{18,... | collective-permute-start | bytes 786440 | tf_op jit(solution)/shard_map/ppermute | solution.py:46
  84.2 12.0 %collective-permute-start.40 = (bf16[4,64,512]{2,1,0:T(8,128)(2,1)S(1)}, bf16[4,64,512]{2,1,0:T(8,128)(2,1)S(1)}, u32[]{:S(2)}, u32[]{:S(2)}) collective-permute-start(bf16[4,64,512]{2,1,0:T(8,128)(2,1)S(1)} %get-tuple-element.114.refs_3_), channel_id=1, source_target_pairs={{0,2},{2,0},{4,6},{6,4},{8,10},{10,8},{12,14},{14,12},{16,18},{18,... | collective-permute-start | bytes 786440 | tf_op jit(solution)/shard_map/ppermute | solution.py:46
  90.7 6.9 %collective-permute-start.42 = (bf16[4,64,512]{2,1,0:T(8,128)(2,1)S(1)}, bf16[4,64,512]{2,1,0:T(8,128)(2,1)S(1)}, u32[]{:S(2)}, u32[]{:S(2)}) collective-permute-start(bf16[4,64,512]{2,1,0:T(8,128)(2,1)S(1)} %get-tuple-element.116.refs_3_), channel_id=1, source_target_pairs={{0,2},{2,0},{4,6},{6,4},{8,10},{10,8},{12,14},{14,12},{16,18},{18,... | collective-permute-start | bytes 786440 | tf_op jit(solution)/shard_map/ppermute | solution.py:46
  92.7 15.9 %collective-permute-start.33 = (bf16[2,64,512]{2,1,0:T(8,128)(2,1)S(1)}, bf16[2,64,512]{2,1,0:T(8,128)(2,1)S(1)}, u32[]{:S(2)}, u32[]{:S(2)}) collective-permute-start(bf16[2,64,512]{2,1,0:T(8,128)(2,1)S(1)} %get-tuple-element.105), channel_id=1, source_target_pairs={{0,8},{2,10},{4,12},{6,14},{8,0},{10,2},{12,4},{14,6},{16,24},{18,... | collective-permute-start | bytes 393224 | tf_op jit(solution)/shard_map/ppermute | solution.py:46
  93.1 15.5 %collective-permute-start.34 = (bf16[2,64,512]{2,1,0:T(8,128)(2,1)S(1)}, bf16[2,64,512]{2,1,0:T(8,128)(2,1)S(1)}, u32[]{:S(2)}, u32[]{:S(2)}) collective-permute-start(bf16[2,64,512]{2,1,0:T(8,128)(2,1)S(1)} %get-tuple-element.106), channel_id=1, source_target_pairs={{0,16},{2,18},{4,20},{6,22},{8,24},{10,26},{12,28},{14,30},{16,0},... | collective-permute-start | bytes 393224 | tf_op jit(solution)/shard_map/ppermute | solution.py:46
  95.5 13.0 %collective-permute-start.35 = (bf16[2,64,512]{2,1,0:T(8,128)(2,1)S(1)}, bf16[2,64,512]{2,1,0:T(8,128)(2,1)S(1)}, u32[]{:S(2)}, u32[]{:S(2)}) collective-permute-start(bf16[2,64,512]{2,1,0:T(8,128)(2,1)S(1)} %get-tuple-element.107.refs_5_), channel_id=1, source_target_pairs={{0,24},{2,26},{4,28},{6,30},{8,16},{10,18},{12,20},{14,22},{16,8},... | collective-permute-start | bytes 393224 | tf_op jit(solution)/shard_map/ppermute | solution.py:46
  99.2 7.3 %collective-permute-start.43 = (bf16[2,512]{1,0:T(2,128)(2,1)S(1)}, bf16[2,512]{1,0:T(2,128)(2,1)S(1)}, u32[]{:S(2)}, u32[]{:S(2)}) collective-permute-start(bf16[2,512]{1,0:T(2,128)(2,1)S(1)} %get-tuple-element.123.refs_4_), channel_id=1, source_target_pairs={{2,4},{4,2},{6,8},{8,6},{10,12},{12,10},{14,16},{16,14},{18,20},{2... | collective-permute-start | bytes 6152 | tf_op jit(solution)/shard_map/ppermute | solution.py:41
  103.7 3.7 %collective-permute-start.44 = (bf16[2,512]{1,0:T(2,128)(2,1)S(1)}, bf16[2,512]{1,0:T(2,128)(2,1)S(1)}, u32[]{:S(2)}, u32[]{:S(2)}) collective-permute-start(bf16[2,512]{1,0:T(2,128)(2,1)S(1)} %get-tuple-element.123.refs_4_), channel_id=1, source_target_pairs={{0,2},{2,0},{4,6},{6,4},{8,10},{10,8},{12,14},{14,12},{16,18},{18,... | collective-permute-start | bytes 6152 | tf_op jit(solution)/shard_map/ppermute | solution.py:37
where the time goes:
time: 110 us; the launch traced here: 109 us
  starting transfers between devices  49.6 us (45%)
  waiting for transfers between devices  28.7 us (26%)
  Pallas kernels  24.7 us (22%)
  local copies, waits for them, and re-layouts  4.63 us (4%)
    ppermute x28, starting transfers between devices, from_flipped(): return lax.ppermute(block, axis, [(i, i ^ mask) for i in range(count)])  36.6 us
    ppermute x28, waiting for transfers between devices, from_flipped(): return lax.ppermute(block, axis, [(i, i ^ mask) for i in range(count)])  25.1 us
    pallas_call x36, Pallas kernels, call(): pl.pallas_call(body, out_shape=[jax.ShapeDtypeStruct(shape, kind) for sha...  24.7 us
    ppermute x2, starting transfers between devices, neighbours(): return (near, lax.ppermute(edges, axis, route))  8.79 us
    unnamed x12, local copies, waits for them, and re-layouts  3.9 us
    ppermute x13, starting transfers between devices, from_offset(): lax.ppermute(block, axis, [((i + offset) % count, i) for i in range(count)])  3.43 us
    ppermute x2, waiting for transfers between devices, neighbours(): return (near, lax.ppermute(edges, axis, route))  2.64 us
  transfers between devices with their start and end apart: 45, of which 15 were waited for; matrix products, arithmetic and copies ran while one was open for 0% of the time, Pallas kernels for 20%

commit v1 on v0

--- a/solution.py
+++ b/solution.py
@@ -337,9 +337,12 @@
         x_all[rows:, spot] = mixed[2 * i + 1][...]
     size = w_in.shape[1]
     tile = min(TILE, size)
-    for start in range(0, size, tile):
-        tiles = slice(start, start + tile)
-        hidden = times(x_all[...], w_in[:, tiles])
+    every = [slice(start, start + tile) for start in range(0, size, tile)]
+    hidden = times(x_all[...], w_in[:, every[0]])
+    for number, tiles in enumerate(every):
+        following = None
+        if number + 1 < len(every):
+            following = times(x_all[...], w_in[:, every[number + 1]])
         square = hidden * hidden
         tanh_val = jnp.tanh(hidden * (root_two_pi + root_two_pi * 0.044715 * square))
         half = 0.5 + 0.5 * tanh_val
@@ -351,10 +354,11 @@
         back = lax.dot_general(
             grad_hidden, w_in[:, tiles], ACROSS, preferred_element_type=jnp.float32
         )
-        if start == 0:
+        if number == 0:
             back_sum[...] = back
         else:
             back_sum[...] += back
+        hidden = following
     own[...] = back_sum[:, spots[0]]
     for i, spot in enumerate(spots[1:]):
         backs[2 * i][...] = back_sum[:rows, spot].astype(jnp.bfloat16)

time: 110 us -> 110 us (level)
  Pallas kernels: 24.7 us -> 23.5 us
  waiting for transfers between devices: 28.7 us -> 29.8 us
    pallas_call x36, Pallas kernels: 24.7 us -> 23.5 us  [call(): pl.pallas_call(body, out_shape=[jax.ShapeDtypeStruct(shape, kind) for sha...]
    ppermute x28, waiting for transfers between devices: 25.1 us -> 26.2 us  [from_flipped(): return lax.ppermute(block, axis, [(i, i ^ mask) for i in range(count)])]
  transfers between devices with their start and end apart: 45 -> 45, of which waited for: 15 -> 15; matrix products, arithmetic and copies ran while one was open for 0% -> 0% of each run, Pallas kernels for 20% -> 18%
where the time goes in v1:
time: 110 us; the launch traced here: 109 us
  starting transfers between devices  49.6 us (45%)
  waiting for transfers between devices  29.8 us (27%)
  Pallas kernels  23.5 us (21%)
  local copies, waits for them, and re-layouts  4.63 us (4%)
    ppermute x28, starting transfers between devices, from_flipped(): return lax.ppermute(block, axis, [(i, i ^ mask) for i in range(count)])  36.2 us
    ppermute x28, waiting for transfers between devices, from_flipped(): return lax.ppermute(block, axis, [(i, i ^ mask) for i in range(count)])  26.2 us
    pallas_call x36, Pallas kernels, call(): pl.pallas_call(body, out_shape=[jax.ShapeDtypeStruct(shape, kind) for sha...  23.5 us
    ppermute x2, starting transfers between devices, neighbours(): return (near, lax.ppermute(edges, axis, route))  9.16 us
    unnamed x12, local copies, waits for them, and re-layouts  3.9 us
    ppermute x13, starting transfers between devices, from_offset(): lax.ppermute(block, axis, [((i + offset) % count, i) for i in range(count)])  3.43 us
    ppermute x2, waiting for transfers between devices, neighbours(): return (near, lax.ppermute(edges, axis, route))  2.27 us
  transfers between devices with their start and end apart: 45, of which 15 were waited for; matrix products, arithmetic and copies ran while one was open for 0% of the time, Pallas kernels for 18%

profile of v1, /device:TPU:8, one launch (start us, length us, event | category | flops | bytes accessed | tf_op | source)
XLA Modules:
  0.0 109.3 jit_solution(5514597421845321430)
XLA Ops:
  0.6 0.7 fusion
  1.4 0.7 pad_maximum_fusion
  2.1 4.2 %collective-permute-start = (bf16[5,512]{1,0:T(8,128)(2,1)S(1)}, bf16[5,512]{1,0:T(8,128)(2,1)S(1)}, u32[]{:S(2)}, u32[]{:S(2)}) collective-permute-start(bf16[5,512]{1,0:T(8,128)(2,1)S(1)} %pad_maximum_fusion), channel_id=1, source_target_pairs={{2,4},{4,2},{6,8},{8,6},{10,12},{12,10},{14,16},{16,14},{18,20},{2... | collective-permute-start | bytes 15368 | tf_op jit(solution)/shard_map/ppermute | solution.py:41
  6.3 0.7 collective-permute-start.1
  7.0 1.1 %copy-done.2 = bf16[6,8,64,128]{3,2,1,0:T(8,128)(2,1)S(1)} copy-done((bf16[6,8,64,128]{3,2,1,0:T(8,128)(2,1)S(1)}, bf16[6,8,64,128]{3,2,1,0:T(8,128)(2,1)}, u32[]{:S(2)}) %copy-start.2) | copy-done | bytes 786456
  8.2 1.0 copy-done.3
  9.2 0.7 copy-done.5
  10.0 2.1 %conv_and_local_factors.1 = (bf16[512,512]{1,0:T(8,128)(2,1)}, bf16[2,64,512]{2,1,0:T(8,128)(2,1)S(1)}, bf16[2,64,512]{2,1,0:T(8,128)(2,1)S(1)}, bf16[2,64,512]{2,1,0:T(8,128)(2,1)S(1)}, bf16[2,64,512]{2,1,0:T(8,128)(2,1)S(1)}) custom-call(s32[2,8]{1,0:T(2,128)S(1)} %get-tuple-element.65.refs_0_.refs_5_, bf16[512,512]{1,0:T(8,128)(2,1)S(1)} %get-tuple-element.66.refs_1_, ...), custom_call_target="tpu_custom_call" | custom-call | tf_op jit(solution)/shard_map/conv_and_local_factors/pallas_call | solution.py:60
  12.1 1.5 %collective-permute-start.3 = (bf16[2,64,512]{2,1,0:T(8,128)(2,1)S(1)}, bf16[2,64,512]{2,1,0:T(8,128)(2,1)S(1)}, u32[]{:S(2)}, u32[]{:S(2)}) collective-permute-start(bf16[2,64,512]{2,1,0:T(8,128)(2,1)S(1)} %get-tuple-element.69.refs_0_), channel_id=1, source_target_pairs={{0,2},{2,0},{4,6},{6,4},{8,10},{10,8},{12,14},{14,12},{16,18},{18,... | collective-permute-start | bytes 393224 | tf_op jit(solution)/shard_map/ppermute | solution.py:46
  13.6 1.0 copy-done.4
  14.7 2.7 %collective-permute-start.12 = (bf16[6,64,512]{2,1,0:T(8,128)(2,1)S(1)}, bf16[6,64,512]{2,1,0:T(8,128)(2,1)S(1)}, u32[]{:S(2)}, u32[]{:S(2)}) collective-permute-start(bf16[6,64,512]{2,1,0:T(8,128)(2,1)S(1)} %get-tuple-element.71.refs_3_), channel_id=1, source_target_pairs={{0,16},{2,18},{4,20},{6,22},{8,24},{10,26},{12,28},{14,30},{16,0},... | collective-permute-start | bytes 1179656 | tf_op jit(solution)/shard_map/ppermute | solution.py:46
  17.4 0.6 collective-permute-start.2
  18.3 0.7 collective-permute-start.6
  19.0 1.3 %collective-permute-start.8 = (bf16[4,64,512]{2,1,0:T(8,128)(2,1)S(1)}, bf16[4,64,512]{2,1,0:T(8,128)(2,1)S(1)}, u32[]{:S(2)}, u32[]{:S(2)}) collective-permute-start(bf16[4,64,512]{2,1,0:T(8,128)(2,1)S(1)} %get-tuple-element.73), channel_id=1, source_target_pairs={{0,8},{2,10},{4,12},{6,14},{8,0},{10,2},{12,4},{14,6},{16,24},{18,... | collective-permute-start | bytes 786440 | tf_op jit(solution)/shard_map/ppermute | solution.py:46
  20.3 0.9 collective-permute-start.5
  21.2 2.4 %collective-permute-done.2.refs_1_ = bf16[2,64,512]{2,1,0:T(8,128)(2,1)S(1)} collective-permute-done((bf16[2,64,512]{2,1,0:T(8,128)(2,1)S(1)}, bf16[2,64,512]{2,1,0:T(8,128)(2,1)S(1)}, u32[]{:S(2)}, u32[]{:S(2)}) %collective-permute-start.2) | collective-permute-done | bytes 131104 | tf_op jit(solution)/shard_map/ppermute | solution.py:46
  23.9 0.6 collective-permute-start.4
  24.7 0.7 collective-permute-start.7
  25.4 1.3 %collective-permute-start.11 = (bf16[2,64,512]{2,1,0:T(8,128)(2,1)S(1)}, bf16[2,64,512]{2,1,0:T(8,128)(2,1)S(1)}, u32[]{:S(2)}, u32[]{:S(2)}) collective-permute-start(bf16[2,64,512]{2,1,0:T(8,128)(2,1)S(1)} %get-tuple-element.70.refs_2_.refs_0_), channel_id=1, source_target_pairs={{0,2},{2,0},{4,6},{6,4},{8,10},{10,8},{12,14},{14,12},{16,18},{18,... | collective-permute-start | bytes 393224 | tf_op jit(solution)/shard_map/ppermute | solution.py:46
  27.0 3.2 %collective-permute-done.4.refs_1_ = bf16[2,64,512]{2,1,0:T(8,128)(2,1)S(1)} collective-permute-done((bf16[2,64,512]{2,1,0:T(8,128)(2,1)S(1)}, bf16[2,64,512]{2,1,0:T(8,128)(2,1)S(1)}, u32[]{:S(2)}, u32[]{:S(2)}) %collective-permute-start.4) | collective-permute-done | bytes 131104 | tf_op jit(solution)/shard_map/ppermute | solution.py:46
  31.0 1.9 %collective-permute-done.8.refs_3_.refs_1_.refs_5_ = bf16[4,64,512]{2,1,0:T(8,128)(2,1)S(1)} collective-permute-done((bf16[4,64,512]{2,1,0:T(8,128)(2,1)S(1)}, bf16[4,64,512]{2,1,0:T(8,128)(2,1)S(1)}, u32[]{:S(2)}, u32[]{:S(2)}) %collective-permute-start.8) | collective-permute-done | bytes 262176 | tf_op jit(solution)/shard_map/ppermute | solution.py:46
  32.9 1.9 %collective-permute-done.7.refs_1_ = bf16[2,64,512]{2,1,0:T(8,128)(2,1)S(1)} collective-permute-done((bf16[2,64,512]{2,1,0:T(8,128)(2,1)S(1)}, bf16[2,64,512]{2,1,0:T(8,128)(2,1)S(1)}, u32[]{:S(2)}, u32[]{:S(2)}) %collective-permute-start.7) | collective-permute-done | bytes 131104 | tf_op jit(solution)/shard_map/ppermute | solution.py:46
  35.1 2.6 %collective-permute-start.13 = (bf16[3,64,512]{2,1,0:T(8,128)(2,1)S(1)}, bf16[3,64,512]{2,1,0:T(8,128)(2,1)S(1)}, u32[]{:S(2)}, u32[]{:S(2)}) collective-permute-start(bf16[3,64,512]{2,1,0:T(8,128)(2,1)S(1)} %forward.1.refs_3_), channel_id=1, source_target_pairs={{0,8},{2,10},{4,12},{6,14},{8,0},{10,2},{12,4},{14,6},{16,24},{18,... | collective-permute-start | bytes 589832 | tf_op jit(solution)/shard_map/ppermute | solution.py:46
  37.7 1.9 %collective-permute-start.9 = (bf16[2,64,512]{2,1,0:T(8,128)(2,1)S(1)}, bf16[2,64,512]{2,1,0:T(8,128)(2,1)S(1)}, u32[]{:S(2)}, u32[]{:S(2)}) collective-permute-start(bf16[2,64,512]{2,1,0:T(8,128)(2,1)S(1)} %get-tuple-element.75.refs_1_), channel_id=1, source_target_pairs={{0,16},{2,18},{4,20},{6,22},{8,24},{10,26},{12,28},{14,30},{16,0},... | collective-permute-start | bytes 393224 | tf_op jit(solution)/shard_map/ppermute | solution.py:46
  39.8 1.0 collective-permute-start.14
  41.1 2.0 %collective-permute-start.17 = (bf16[2,64,512]{2,1,0:T(8,128)(2,1)S(1)}, bf16[2,64,512]{2,1,0:T(8,128)(2,1)S(1)}, u32[]{:S(2)}, u32[]{:S(2)}) collective-permute-start(bf16[2,64,512]{2,1,0:T(8,128)(2,1)S(1)} %factor.14.refs_1_), channel_id=1, source_target_pairs={{0,8},{2,10},{4,12},{6,14},{8,0},{10,2},{12,4},{14,6},{16,24},{18,... | collective-permute-start | bytes 393224 | tf_op jit(solution)/shard_map/ppermute | solution.py:46
  43.2 2.9 %collective-permute-done.9.refs_0_ = bf16[2,64,512]{2,1,0:T(8,128)(2,1)S(1)} collective-permute-done((bf16[2,64,512]{2,1,0:T(8,128)(2,1)S(1)}, bf16[2,64,512]{2,1,0:T(8,128)(2,1)S(1)}, u32[]{:S(2)}, u32[]{:S(2)}) %collective-permute-start.9) | collective-permute-done | bytes 131104 | tf_op jit(solution)/shard_map/ppermute | solution.py:46
  47.3 0.5 collective-permute-start.19
  48.3 2.4 %collective-permute-start.20 = (bf16[2,64,512]{2,1,0:T(8,128)(2,1)S(1)}, bf16[2,64,512]{2,1,0:T(8,128)(2,1)S(1)}, u32[]{:S(2)}, u32[]{:S(2)}) collective-permute-start(bf16[2,64,512]{2,1,0:T(8,128)(2,1)S(1)} %get-tuple-element.79.refs_4_), channel_id=1, source_target_pairs={{0,16},{2,18},{4,20},{6,22},{8,24},{10,26},{12,28},{14,30},{16,0},... | collective-permute-start | bytes 393224 | tf_op jit(solution)/shard_map/ppermute | solution.py:46
  50.6 1.3 %grad_act.2.refs_4_.refs_6_ = bf16[256,2048]{1,0:T(8,128)(2,1)S(1)} custom-call(bf16[256,512]{1,0:T(8,128)(2,1)S(1)} %get-tuple-element.80.refs_0_, bf16[256,512]{1,0:T(8,128)(2,1)S(1)} %collective-permute-done.18.refs_1_, bf16[2048,1024]{1,0:T(8,128)(2,1)S(1)} %copy-done, bf16[256,512]{1,0:T(8,128)(2,1)S(1)} %get-tuple-element.81.refs_3_.refs_0_), custom_call_target="tpu_custom_call" | custom-call | tf_op jit(solution)/shard_map/grad_act/pallas_call | solution.py:60
  52.0 3.0 %mlp_hidden_and_grad.2 = (bf16[256,2048]{1,0:T(8,128)(2,1)S(1)}, f32[256,512]{1,0:T(8,128)S(1)}, bf16[128,512]{1,0:T(8,128)(2,1)S(1)}, bf16[128,512]{1,0:T(8,128)(2,1)S(1)}) custom-call(bf16[128,512]{1,0:T(8,128)(2,1)S(1)} %get-tuple-element.76.refs_0_.refs_1_, bf16[128,512]{1,0:T(8,128)(2,1)S(1)} %get-tuple-element.77.refs_4_.refs_1_.refs_2_, ...), custom_call_target="tpu_custom_call" | custom-call | tf_op jit(solution)/shard_map/mlp_hidden_and_grad/pallas_call | solution.py:60
  55.0 0.5 collective-permute-start.24
  55.5 1.3 %grad_act.3.refs_4_ = bf16[256,2048]{1,0:T(8,128)(2,1)S(1)} custom-call(bf16[256,512]{1,0:T(8,128)(2,1)S(1)} %get-tuple-element.81.refs_3_.refs_0_, bf16[256,512]{1,0:T(8,128)(2,1)S(1)} %collective-permute-done.19.refs_1_, bf16[2048,1024]{1,0:T(8,128)(2,1)S(1)} %copy-done, bf16[128,512]{1,0:T(8,128)(2,1)S(1)} %get-tuple-element.83.refs_3_), custom_call_target="tpu_custom_call" | custom-call | tf_op jit(solution)/shard_map/grad_act/pallas_call | solution.py:60
  56.8 1.3 %mlp_out.2 = (f32[256,512]{1,0:T(8,128)S(1)}, bf16[256,512]{1,0:T(8,128)(2,1)S(1)}) custom-call(bf16[256,2048]{1,0:T(8,128)(2,1)S(1)} %get-tuple-element.82.refs_0_, bf16[128,512]{1,0:T(8,128)(2,1)S(1)} %get-tuple-element.76.refs_0_.refs_1_, bf16[128,512]{1,0:T(8,128)(2,1)S(1)} %get-tuple-element.77.refs_4_.refs_1_.refs_2_, bf16[2048,1024]{1,0:T(8,128)(2,1)S(1)} %copy-done, ...), custom_call_target="tpu_custom_call" | custom-call | tf_op jit(solution)/shard_map/mlp_out/pallas_call | solution.py:60
  59.1 0.6 late_and_early_back.2
  59.7 0.7 collective-permute-start.25
  60.4 1.2 %collective-permute-start.26 = (bf16[64,512]{1,0:T(8,128)(2,1)S(1)}, bf16[64,512]{1,0:T(8,128)(2,1)S(1)}, u32[]{:S(2)}, u32[]{:S(2)}) collective-permute-start(bf16[64,512]{1,0:T(8,128)(2,1)S(1)} %get-tuple-element.95), channel_id=1, source_target_pairs={{0,16},{2,18},{4,20},{6,22},{8,24},{10,26},{12,28},{14,30},{16,0},... | collective-permute-start | bytes 196616 | tf_op jit(solution)/shard_map/ppermute | solution.py:46
  61.7 1.6 %collective-permute-start.27 = (bf16[64,512]{1,0:T(8,128)(2,1)S(1)}, bf16[64,512]{1,0:T(8,128)(2,1)S(1)}, u32[]{:S(2)}, u32[]{:S(2)}) collective-permute-start(bf16[64,512]{1,0:T(8,128)(2,1)S(1)} %get-tuple-element.91.refs_6_), channel_id=1, source_target_pairs={{0,24},{2,26},{4,28},{6,30},{8,16},{10,18},{12,20},{14,22},{16,8},... | collective-permute-start | bytes 196616 | tf_op jit(solution)/shard_map/ppermute | solution.py:46
  63.3 3.2 %mlp_hidden_and_grad.3 = (bf16[256,2048]{1,0:T(8,128)(2,1)S(1)}, f32[256,512]{1,0:T(8,128)S(1)}, bf16[128,512]{1,0:T(8,128)(2,1)S(1)}, bf16[128,512]{1,0:T(8,128)(2,1)S(1)}) custom-call(bf16[128,512]{1,0:T(8,128)(2,1)S(1)} %get-tuple-element.87.refs_0_.refs_1_, bf16[128,512]{1,0:T(8,128)(2,1)S(1)} %get-tuple-element.88.refs_8_.refs_1_.refs_2_, ...), custom_call_target="tpu_custom_call" | custom-call | tf_op jit(solution)/shard_map/mlp_hidden_and_grad/pallas_call | solution.py:60
  66.5 0.5 collective-permute-start.32
  67.0 2.6 %collective-permute-done.27.refs_3_ = bf16[64,512]{1,0:T(8,128)(2,1)S(1)} collective-permute-done((bf16[64,512]{1,0:T(8,128)(2,1)S(1)}, bf16[64,512]{1,0:T(8,128)(2,1)S(1)}, u32[]{:S(2)}, u32[]{:S(2)}) %collective-permute-start.27) | collective-permute-done | bytes 65568 | tf_op jit(solution)/shard_map/ppermute | solution.py:46
  70.0 1.3 %mlp_out.3 = (f32[256,512]{1,0:T(8,128)S(1)}, bf16[128,512]{1,0:T(8,128)(2,1)S(1)}, bf16[128,512]{1,0:T(8,128)(2,1)S(1)}) custom-call(bf16[256,2048]{1,0:T(8,128)(2,1)S(1)} %get-tuple-element.92.refs_0_, bf16[128,512]{1,0:T(8,128)(2,1)S(1)} %get-tuple-element.87.refs_0_.refs_1_, bf16[128,512]{1,0:T(8,128)(2,1)S(1)} %get-tuple-element.88.refs_8_.refs_1_.refs_2_, ...), custom_call_target="tpu_custom_call" | custom-call | tf_op jit(solution)/shard_map/mlp_out/pallas_call | solution.py:60
  71.3 0.5 collective-permute-start.30
  71.8 0.6 late_and_early_back.3
  72.7 1.7 %collective-permute-start.38 = (bf16[64,512]{1,0:T(8,128)(2,1)S(1)}, bf16[64,512]{1,0:T(8,128)(2,1)S(1)}, u32[]{:S(2)}, u32[]{:S(2)}) collective-permute-start(bf16[64,512]{1,0:T(8,128)(2,1)S(1)} %get-tuple-element.111), channel_id=1, source_target_pairs={{0,16},{2,18},{4,20},{6,22},{8,24},{10,26},{12,28},{14,30},{16,0},... | collective-permute-start | bytes 196616 | tf_op jit(solution)/shard_map/ppermute | solution.py:46
  74.4 1.5 %collective-permute-start.39 = (bf16[64,512]{1,0:T(8,128)(2,1)S(1)}, bf16[64,512]{1,0:T(8,128)(2,1)S(1)}, u32[]{:S(2)}, u32[]{:S(2)}) collective-permute-start(bf16[64,512]{1,0:T(8,128)(2,1)S(1)} %get-tuple-element.103.refs_5_), channel_id=1, source_target_pairs={{0,24},{2,26},{4,28},{6,30},{8,16},{10,18},{12,20},{14,22},{16,8},... | collective-permute-start | bytes 196616 | tf_op jit(solution)/shard_map/ppermute | solution.py:46
  76.0 0.7 collective-permute-start.36
  76.7 0.5 collective-permute-done.37.refs_1_
  77.2 2.0 %collective-permute-done.38.refs_2_ = bf16[64,512]{1,0:T(8,128)(2,1)S(1)} collective-permute-done((bf16[64,512]{1,0:T(8,128)(2,1)S(1)}, bf16[64,512]{1,0:T(8,128)(2,1)S(1)}, u32[]{:S(2)}, u32[]{:S(2)}) %collective-permute-start.38) | collective-permute-done | bytes 65568 | tf_op jit(solution)/shard_map/ppermute | solution.py:46
  79.3 2.6 %collective-permute-done.39.refs_3_ = bf16[64,512]{1,0:T(8,128)(2,1)S(1)} collective-permute-done((bf16[64,512]{1,0:T(8,128)(2,1)S(1)}, bf16[64,512]{1,0:T(8,128)(2,1)S(1)}, u32[]{:S(2)}, u32[]{:S(2)}) %collective-permute-start.39) | collective-permute-done | bytes 65568 | tf_op jit(solution)/shard_map/ppermute | solution.py:46
  82.2 0.8 collective-permute-start.41
  82.9 0.5 collective-permute-done.36.refs_1_
  83.7 1.8 %collective-permute-start.40 = (bf16[4,64,512]{2,1,0:T(8,128)(2,1)S(1)}, bf16[4,64,512]{2,1,0:T(8,128)(2,1)S(1)}, u32[]{:S(2)}, u32[]{:S(2)}) collective-permute-start(bf16[4,64,512]{2,1,0:T(8,128)(2,1)S(1)} %get-tuple-element.114.refs_3_), channel_id=1, source_target_pairs={{0,2},{2,0},{4,6},{6,4},{8,10},{10,8},{12,14},{14,12},{16,18},{18,... | collective-permute-start | bytes 786440 | tf_op jit(solution)/shard_map/ppermute | solution.py:46
  85.5 4.4 %collective-permute-done.41.refs_1_ = bf16[4,64,512]{2,1,0:T(8,128)(2,1)S(1)} collective-permute-done((bf16[4,64,512]{2,1,0:T(8,128)(2,1)S(1)}, bf16[4,64,512]{2,1,0:T(8,128)(2,1)S(1)}, u32[]{:S(2)}, u32[]{:S(2)}) %collective-permute-start.41) | collective-permute-done | bytes 262176 | tf_op jit(solution)/shard_map/ppermute | solution.py:46
  90.3 1.9 %collective-permute-start.42 = (bf16[4,64,512]{2,1,0:T(8,128)(2,1)S(1)}, bf16[4,64,512]{2,1,0:T(8,128)(2,1)S(1)}, u32[]{:S(2)}, u32[]{:S(2)}) collective-permute-start(bf16[4,64,512]{2,1,0:T(8,128)(2,1)S(1)} %get-tuple-element.116.refs_3_), channel_id=1, source_target_pairs={{0,2},{2,0},{4,6},{6,4},{8,10},{10,8},{12,14},{14,12},{16,18},{18,... | collective-permute-start | bytes 786440 | tf_op jit(solution)/shard_map/ppermute | solution.py:46
  92.5 2.7 %collective-permute-start.34 = (bf16[2,64,512]{2,1,0:T(8,128)(2,1)S(1)}, bf16[2,64,512]{2,1,0:T(8,128)(2,1)S(1)}, u32[]{:S(2)}, u32[]{:S(2)}) collective-permute-start(bf16[2,64,512]{2,1,0:T(8,128)(2,1)S(1)} %get-tuple-element.106), channel_id=1, source_target_pairs={{0,16},{2,18},{4,20},{6,22},{8,24},{10,26},{12,28},{14,30},{16,0},... | collective-permute-start | bytes 393224 | tf_op jit(solution)/shard_map/ppermute | solution.py:46
  95.1 0.5 collective-permute-start.35
  96.0 1.2 %collective-permute-done.42.refs_1_ = bf16[4,64,512]{2,1,0:T(8,128)(2,1)S(1)} collective-permute-done((bf16[4,64,512]{2,1,0:T(8,128)(2,1)S(1)}, bf16[4,64,512]{2,1,0:T(8,128)(2,1)S(1)}, u32[]{:S(2)}, u32[]{:S(2)}) %collective-permute-start.42) | collective-permute-done | bytes 262176 | tf_op jit(solution)/shard_map/ppermute | solution.py:46
  97.5 1.2 %local_factors_back.1 = (bf16[512,512]{1,0:T(8,128)(2,1)S(1)}, bf16[2,512]{1,0:T(2,128)(2,1)S(1)}) custom-call(s32[2,8]{1,0:T(2,128)S(1)} %get-tuple-element.65.refs_0_.refs_5_, f32[4,64,512]{2,1,0:T(8,128)S(1)} %get-tuple-element.117.refs_1_, f32[4,64,512]{2,1,0:T(8,128)S(1)} %get-tuple-element.120.refs_2_, f32[4,64,512]{2,1,0:T(8,128)S(1)} %get-tuple-element.119.refs_3_, ...), custom_call_target="tpu_custom_call" | custom-call | tf_op jit(solution)/shard_map/local_factors_back/pallas_call | solution.py:60
  98.7 4.9 %collective-permute-start.43 = (bf16[2,512]{1,0:T(2,128)(2,1)S(1)}, bf16[2,512]{1,0:T(2,128)(2,1)S(1)}, u32[]{:S(2)}, u32[]{:S(2)}) collective-permute-start(bf16[2,512]{1,0:T(2,128)(2,1)S(1)} %get-tuple-element.123.refs_4_), channel_id=1, source_target_pairs={{2,4},{4,2},{6,8},{8,6},{10,12},{12,10},{14,16},{16,14},{18,20},{2... | collective-permute-start | bytes 6152 | tf_op jit(solution)/shard_map/ppermute | solution.py:41
  103.7 2.3 %collective-permute-done.43.refs_1_ = bf16[2,512]{1,0:T(2,128)(2,1)S(1)} collective-permute-done((bf16[2,512]{1,0:T(2,128)(2,1)S(1)}, bf16[2,512]{1,0:T(2,128)(2,1)S(1)}, u32[]{:S(2)}, u32[]{:S(2)}) %collective-permute-start.43) | collective-permute-done | bytes 2080 | tf_op jit(solution)/shard_map/ppermute | solution.py:41
  106.0 1.3 %collective-permute-done.44.refs_2_ = bf16[2,512]{1,0:T(2,128)(2,1)S(1)} collective-permute-done((bf16[2,512]{1,0:T(2,128)(2,1)S(1)}, bf16[2,512]{1,0:T(2,128)(2,1)S(1)}, u32[]{:S(2)}, u32[]{:S(2)}) %collective-permute-start.44) | collective-permute-done | bytes 2080 | tf_op jit(solution)/shard_map/ppermute | solution.py:37
  107.3 1.2 %conv_back.1 = (bf16[512,512]{1,0:T(8,128)(2,1)}, f32[8,128]{1,0:T(8,128)S(1)}) custom-call(bf16[512,512]{1,0:T(8,128)(2,1)S(1)} %get-tuple-element.122.refs_0_, bf16[2,512]{1,0:T(2,128)(2,1)S(1)} %collective-permute-done.43.refs_1_, bf16[2,512]{1,0:T(2,128)(2,1)S(1)} %collective-permute-done.44.refs_2_, bf16[5,512]{1,0:T(8,128)(2,1)S(1)} %collective-permute-done.1.refs_3_, ...), custom_call_target="tpu_custom_call" | custom-call | tf_op jit(solution)/shard_map/conv_back/pallas_call | solution.py:60
  108.5 0.8 assemble.1
  (76 shorter events, 8.6 us)
Async XLA Ops:
  2.1 8.0 %collective-permute-start = (bf16[5,512]{1,0:T(8,128)(2,1)S(1)}, bf16[5,512]{1,0:T(8,128)(2,1)S(1)}, u32[]{:S(2)}, u32[]{:S(2)}) collective-permute-start(bf16[5,512]{1,0:T(8,128)(2,1)S(1)} %pad_maximum_fusion), channel_id=1, source_target_pairs={{2,4},{4,2},{6,8},{8,6},{10,12},{12,10},{14,16},{16,14},{18,20},{2... | collective-permute-start | bytes 15368 | tf_op jit(solution)/shard_map/ppermute | solution.py:41
  6.3 3.7 %collective-permute-start.1 = (bf16[5,512]{1,0:T(8,128)(2,1)S(1)}, bf16[5,512]{1,0:T(8,128)(2,1)S(1)}, u32[]{:S(2)}, u32[]{:S(2)}) collective-permute-start(bf16[5,512]{1,0:T(8,128)(2,1)S(1)} %pad_maximum_fusion), channel_id=1, source_target_pairs={{0,2},{2,0},{4,6},{6,4},{8,10},{10,8},{12,14},{14,12},{16,18},{18,... | collective-permute-start | bytes 15368 | tf_op jit(solution)/shard_map/ppermute | solution.py:37
  7.0 1.1 %copy-start.2 = (bf16[6,8,64,128]{3,2,1,0:T(8,128)(2,1)S(1)}, bf16[6,8,64,128]{3,2,1,0:T(8,128)(2,1)}, u32[]{:S(2)}) copy-start(bf16[6,8,64,128]{3,2,1,0:T(8,128)(2,1)} %refs_0_.1) | copy-start | bytes 2359300
  8.2 1.0 copy-start.3
  9.2 0.7 copy-start.5
  12.1 5.9 %collective-permute-start.3 = (bf16[2,64,512]{2,1,0:T(8,128)(2,1)S(1)}, bf16[2,64,512]{2,1,0:T(8,128)(2,1)S(1)}, u32[]{:S(2)}, u32[]{:S(2)}) collective-permute-start(bf16[2,64,512]{2,1,0:T(8,128)(2,1)S(1)} %get-tuple-element.69.refs_0_), channel_id=1, source_target_pairs={{0,2},{2,0},{4,6},{6,4},{8,10},{10,8},{12,14},{14,12},{16,18},{18,... | collective-permute-start | bytes 393224 | tf_op jit(solution)/shard_map/ppermute | solution.py:46
  13.6 1.0 copy-start.4
  14.7 20.4 %collective-permute-start.12 = (bf16[6,64,512]{2,1,0:T(8,128)(2,1)S(1)}, bf16[6,64,512]{2,1,0:T(8,128)(2,1)S(1)}, u32[]{:S(2)}, u32[]{:S(2)}) collective-permute-start(bf16[6,64,512]{2,1,0:T(8,128)(2,1)S(1)} %get-tuple-element.71.refs_3_), channel_id=1, source_target_pairs={{0,16},{2,18},{4,20},{6,22},{8,24},{10,26},{12,28},{14,30},{16,0},... | collective-permute-start | bytes 1179656 | tf_op jit(solution)/shard_map/ppermute | solution.py:46
  17.4 6.2 %collective-permute-start.2 = (bf16[2,64,512]{2,1,0:T(8,128)(2,1)S(1)}, bf16[2,64,512]{2,1,0:T(8,128)(2,1)S(1)}, u32[]{:S(2)}, u32[]{:S(2)}) collective-permute-start(bf16[2,64,512]{2,1,0:T(8,128)(2,1)S(1)} %get-tuple-element.68.refs_0_), channel_id=1, source_target_pairs={{0,2},{2,0},{4,6},{6,4},{8,10},{10,8},{12,14},{14,12},{16,18},{18,... | collective-permute-start | bytes 393224 | tf_op jit(solution)/shard_map/ppermute | solution.py:46
  18.3 6.2 %collective-permute-start.6 = (bf16[2,64,512]{2,1,0:T(8,128)(2,1)S(1)}, bf16[2,64,512]{2,1,0:T(8,128)(2,1)S(1)}, u32[]{:S(2)}, u32[]{:S(2)}) collective-permute-start(bf16[2,64,512]{2,1,0:T(8,128)(2,1)S(1)} %factor.8.refs_3_.refs_0_), channel_id=1, source_target_pairs={{0,4},{2,6},{4,0},{6,2},{8,12},{10,14},{12,8},{14,10},{16,20},{18,... | collective-permute-start | bytes 393224 | tf_op jit(solution)/shard_map/ppermute | solution.py:46
  19.0 13.9 %collective-permute-start.8 = (bf16[4,64,512]{2,1,0:T(8,128)(2,1)S(1)}, bf16[4,64,512]{2,1,0:T(8,128)(2,1)S(1)}, u32[]{:S(2)}, u32[]{:S(2)}) collective-permute-start(bf16[4,64,512]{2,1,0:T(8,128)(2,1)S(1)} %get-tuple-element.73), channel_id=1, source_target_pairs={{0,8},{2,10},{4,12},{6,14},{8,0},{10,2},{12,4},{14,6},{16,24},{18,... | collective-permute-start | bytes 786440 | tf_op jit(solution)/shard_map/ppermute | solution.py:46
  20.3 5.1 %collective-permute-start.5 = (bf16[2,64,512]{2,1,0:T(8,128)(2,1)S(1)}, bf16[2,64,512]{2,1,0:T(8,128)(2,1)S(1)}, u32[]{:S(2)}, u32[]{:S(2)}) collective-permute-start(bf16[2,64,512]{2,1,0:T(8,128)(2,1)S(1)} %get-tuple-element.72.refs_0_), channel_id=1, source_target_pairs={{0,2},{2,0},{4,6},{6,4},{8,10},{10,8},{12,14},{14,12},{16,18},{18,... | collective-permute-start | bytes 393224 | tf_op jit(solution)/shard_map/ppermute | solution.py:46
  23.9 6.4 %collective-permute-start.4 = (bf16[2,64,512]{2,1,0:T(8,128)(2,1)S(1)}, bf16[2,64,512]{2,1,0:T(8,128)(2,1)S(1)}, u32[]{:S(2)}, u32[]{:S(2)}) collective-permute-start(bf16[2,64,512]{2,1,0:T(8,128)(2,1)S(1)} %factor.9.refs_3_.refs_0_), channel_id=1, source_target_pairs={{0,4},{2,6},{4,0},{6,2},{8,12},{10,14},{12,8},{14,10},{16,20},{18,... | collective-permute-start | bytes 393224 | tf_op jit(solution)/shard_map/ppermute | solution.py:46
  24.7 10.0 %collective-permute-start.7 = (bf16[2,64,512]{2,1,0:T(8,128)(2,1)S(1)}, bf16[2,64,512]{2,1,0:T(8,128)(2,1)S(1)}, u32[]{:S(2)}, u32[]{:S(2)}) collective-permute-start(bf16[2,64,512]{2,1,0:T(8,128)(2,1)S(1)} %factor.10.refs_3_), channel_id=1, source_target_pairs={{0,8},{2,10},{4,12},{6,14},{8,0},{10,2},{12,4},{14,6},{16,24},{18,... | collective-permute-start | bytes 393224 | tf_op jit(solution)/shard_map/ppermute | solution.py:46
  25.4 14.1 %collective-permute-start.11 = (bf16[2,64,512]{2,1,0:T(8,128)(2,1)S(1)}, bf16[2,64,512]{2,1,0:T(8,128)(2,1)S(1)}, u32[]{:S(2)}, u32[]{:S(2)}) collective-permute-start(bf16[2,64,512]{2,1,0:T(8,128)(2,1)S(1)} %get-tuple-element.70.refs_2_.refs_0_), channel_id=1, source_target_pairs={{0,2},{2,0},{4,6},{6,4},{8,10},{10,8},{12,14},{14,12},{16,18},{18,... | collective-permute-start | bytes 393224 | tf_op jit(solution)/shard_map/ppermute | solution.py:46
  30.2 10.6 %collective-permute-start.10 = (bf16[2,64,512]{2,1,0:T(8,128)(2,1)S(1)}, bf16[2,64,512]{2,1,0:T(8,128)(2,1)S(1)}, u32[]{:S(2)}, u32[]{:S(2)}) collective-permute-start(bf16[2,64,512]{2,1,0:T(8,128)(2,1)S(1)} %factor.11.refs_3_.refs_0_), channel_id=1, source_target_pairs={{0,4},{2,6},{4,0},{6,2},{8,12},{10,14},{12,8},{14,10},{16,20},{18,... | collective-permute-start | bytes 393224 | tf_op jit(solution)/shard_map/ppermute | solution.py:46
  35.1 15.5 %copy-start = (bf16[2048,1024]{1,0:T(8,128)(2,1)S(1)}, bf16[2048,1024]{1,0:T(8,128)(2,1)}, u32[]{:S(2)}) copy-start(bf16[2048,1024]{1,0:T(8,128)(2,1)} %refs_3_.3) | copy-start | bytes 12582916
  35.1 11.2 %collective-permute-start.13 = (bf16[3,64,512]{2,1,0:T(8,128)(2,1)S(1)}, bf16[3,64,512]{2,1,0:T(8,128)(2,1)S(1)}, u32[]{:S(2)}, u32[]{:S(2)}) collective-permute-start(bf16[3,64,512]{2,1,0:T(8,128)(2,1)S(1)} %forward.1.refs_3_), channel_id=1, source_target_pairs={{0,8},{2,10},{4,12},{6,14},{8,0},{10,2},{12,4},{14,6},{16,24},{18,... | collective-permute-start | bytes 589832 | tf_op jit(solution)/shard_map/ppermute | solution.py:46
  37.7 8.3 %collective-permute-start.9 = (bf16[2,64,512]{2,1,0:T(8,128)(2,1)S(1)}, bf16[2,64,512]{2,1,0:T(8,128)(2,1)S(1)}, u32[]{:S(2)}, u32[]{:S(2)}) collective-permute-start(bf16[2,64,512]{2,1,0:T(8,128)(2,1)S(1)} %get-tuple-element.75.refs_1_), channel_id=1, source_target_pairs={{0,16},{2,18},{4,20},{6,22},{8,24},{10,26},{12,28},{14,30},{16,0},... | collective-permute-start | bytes 393224 | tf_op jit(solution)/shard_map/ppermute | solution.py:46
  39.8 6.2 %collective-permute-start.14 = (bf16[2,64,512]{2,1,0:T(8,128)(2,1)S(1)}, bf16[2,64,512]{2,1,0:T(8,128)(2,1)S(1)}, u32[]{:S(2)}, u32[]{:S(2)}) collective-permute-start(bf16[2,64,512]{2,1,0:T(8,128)(2,1)S(1)} %factor.13.refs_3_.refs_0_), channel_id=1, source_target_pairs={{0,4},{2,6},{4,0},{6,2},{8,12},{10,14},{12,8},{14,10},{16,20},{18,... | collective-permute-start | bytes 393224 | tf_op jit(solution)/shard_map/ppermute | solution.py:46
  41.1 5.6 %collective-permute-start.17 = (bf16[2,64,512]{2,1,0:T(8,128)(2,1)S(1)}, bf16[2,64,512]{2,1,0:T(8,128)(2,1)S(1)}, u32[]{:S(2)}, u32[]{:S(2)}) collective-permute-start(bf16[2,64,512]{2,1,0:T(8,128)(2,1)S(1)} %factor.14.refs_1_), channel_id=1, source_target_pairs={{0,8},{2,10},{4,12},{6,14},{8,0},{10,2},{12,4},{14,6},{16,24},{18,... | collective-permute-start | bytes 393224 | tf_op jit(solution)/shard_map/ppermute | solution.py:46
  46.8 5.2 %copy-start.1 = (bf16[1024,2048]{1,0:T(8,128)(2,1)S(1)}, bf16[1024,2048]{1,0:T(8,128)(2,1)}, u32[]{:S(2)}) copy-start(bf16[1024,2048]{1,0:T(8,128)(2,1)} %refs_5_.3) | copy-start | bytes 12582916
  47.2 3.5 %collective-permute-start.18 = (bf16[256,512]{1,0:T(8,128)(2,1)S(1)}, bf16[256,512]{1,0:T(8,128)(2,1)S(1)}, u32[]{:S(2)}, u32[]{:S(2)}) collective-permute-start(bf16[256,512]{1,0:T(8,128)(2,1)S(1)} %get-tuple-element.80.refs_0_), channel_id=1, source_target_pairs={{1,0},{0,1},{3,2},{2,3},{5,4},{4,5},{7,6},{6,7},{9,8},{8,9},{11,10... | collective-permute-start | bytes 786440 | tf_op jit(solution)/shard_map/ppermute | solution.py:51
  47.3 8.3 %collective-permute-start.19 = (bf16[256,512]{1,0:T(8,128)(2,1)S(1)}, bf16[256,512]{1,0:T(8,128)(2,1)S(1)}, u32[]{:S(2)}, u32[]{:S(2)}) collective-permute-start(bf16[256,512]{1,0:T(8,128)(2,1)S(1)} %get-tuple-element.81.refs_3_.refs_0_), channel_id=1, source_target_pairs={{1,0},{0,1},{3,2},{2,3},{5,4},{4,5},{7,6},{6,7},{9,8},{8,9},{11,10... | collective-permute-start | bytes 786440 | tf_op jit(solution)/shard_map/ppermute | solution.py:51
  47.7 4.2 %collective-permute-start.15 = (bf16[128,512]{1,0:T(8,128)(2,1)S(1)}, bf16[128,512]{1,0:T(8,128)(2,1)S(1)}, u32[]{:S(2)}, u32[]{:S(2)}) collective-permute-start(bf16[128,512]{1,0:T(8,128)(2,1)S(1)} %get-tuple-element.76.refs_0_.refs_1_), channel_id=1, source_target_pairs={{1,0},{0,1},{3,2},{2,3},{5,4},{4,5},{7,6},{6,7},{9,8},{8,9},{11,10... | collective-permute-start | bytes 393224 | tf_op jit(solution)/shard_map/ppermute | solution.py:51
  47.8 4.1 %collective-permute-start.16 = (bf16[128,512]{1,0:T(8,128)(2,1)S(1)}, bf16[128,512]{1,0:T(8,128)(2,1)S(1)}, u32[]{:S(2)}, u32[]{:S(2)}) collective-permute-start(bf16[128,512]{1,0:T(8,128)(2,1)S(1)} %get-tuple-element.77.refs_4_.refs_1_.refs_2_), channel_id=1, source_target_pairs={{1,0},{0,1},{3,2},{2,3},{5,4},{4,5},{7,6},{6,7},{9,8},{8,9},{11,10... | collective-permute-start | bytes 393224 | tf_op jit(solution)/shard_map/ppermute | solution.py:51
  48.3 9.9 %collective-permute-start.20 = (bf16[2,64,512]{2,1,0:T(8,128)(2,1)S(1)}, bf16[2,64,512]{2,1,0:T(8,128)(2,1)S(1)}, u32[]{:S(2)}, u32[]{:S(2)}) collective-permute-start(bf16[2,64,512]{2,1,0:T(8,128)(2,1)S(1)} %get-tuple-element.79.refs_4_), channel_id=1, source_target_pairs={{0,16},{2,18},{4,20},{6,22},{8,24},{10,26},{12,28},{14,30},{16,0},... | collective-permute-start | bytes 393224 | tf_op jit(solution)/shard_map/ppermute | solution.py:46
  55.0 4.2 %collective-permute-start.23 = (bf16[128,512]{1,0:T(8,128)(2,1)S(1)}, bf16[128,512]{1,0:T(8,128)(2,1)S(1)}, u32[]{:S(2)}, u32[]{:S(2)}) collective-permute-start(bf16[128,512]{1,0:T(8,128)(2,1)S(1)} %get-tuple-element.90), channel_id=1, source_target_pairs={{1,0},{0,1},{3,2},{2,3},{5,4},{4,5},{7,6},{6,7},{9,8},{8,9},{11,10... | collective-permute-start | bytes 393224 | tf_op jit(solution)/shard_map/ppermute | solution.py:51
  55.0 4.1 %collective-permute-start.24 = (bf16[128,512]{1,0:T(8,128)(2,1)S(1)}, bf16[128,512]{1,0:T(8,128)(2,1)S(1)}, u32[]{:S(2)}, u32[]{:S(2)}) collective-permute-start(bf16[128,512]{1,0:T(8,128)(2,1)S(1)} %get-tuple-element.83.refs_3_), channel_id=1, source_target_pairs={{1,0},{0,1},{3,2},{2,3},{5,4},{4,5},{7,6},{6,7},{9,8},{8,9},{11,10... | collective-permute-start | bytes 393224 | tf_op jit(solution)/shard_map/ppermute | solution.py:51
  58.5 3.2 %collective-permute-start.21 = (bf16[128,512]{1,0:T(8,128)(2,1)S(1)}, bf16[128,512]{1,0:T(8,128)(2,1)S(1)}, u32[]{:S(2)}, u32[]{:S(2)}) collective-permute-start(bf16[128,512]{1,0:T(8,128)(2,1)S(1)} %get-tuple-element.87.refs_0_.refs_1_), channel_id=1, source_target_pairs={{1,0},{0,1},{3,2},{2,3},{5,4},{4,5},{7,6},{6,7},{9,8},{8,9},{11,10... | collective-permute-start | bytes 393224 | tf_op jit(solution)/shard_map/ppermute | solution.py:51
  58.6 4.7 %collective-permute-start.22 = (bf16[128,512]{1,0:T(8,128)(2,1)S(1)}, bf16[128,512]{1,0:T(8,128)(2,1)S(1)}, u32[]{:S(2)}, u32[]{:S(2)}) collective-permute-start(bf16[128,512]{1,0:T(8,128)(2,1)S(1)} %get-tuple-element.88.refs_8_.refs_1_.refs_2_), channel_id=1, source_target_pairs={{1,0},{0,1},{3,2},{2,3},{5,4},{4,5},{7,6},{6,7},{9,8},{8,9},{11,10... | collective-permute-start | bytes 393224 | tf_op jit(solution)/shard_map/ppermute | solution.py:51
  59.1 15.4 %collective-permute-start.28 = (bf16[256,512]{1,0:T(8,128)(2,1)S(1)}, bf16[256,512]{1,0:T(8,128)(2,1)S(1)}, u32[]{:S(2)}, u32[]{:S(2)}) collective-permute-start(bf16[256,512]{1,0:T(8,128)(2,1)S(1)} %get-tuple-element.86.refs_6_), channel_id=1, source_target_pairs={{1,0},{0,1},{3,2},{2,3},{5,4},{4,5},{7,6},{6,7},{9,8},{8,9},{11,10... | collective-permute-start | bytes 786440 | tf_op jit(solution)/shard_map/ppermute | solution.py:51
  59.7 6.8 %collective-permute-start.25 = (bf16[64,512]{1,0:T(8,128)(2,1)S(1)}, bf16[64,512]{1,0:T(8,128)(2,1)S(1)}, u32[]{:S(2)}, u32[]{:S(2)}) collective-permute-start(bf16[64,512]{1,0:T(8,128)(2,1)S(1)} %get-tuple-element.94), channel_id=1, source_target_pairs={{0,8},{2,10},{4,12},{6,14},{8,0},{10,2},{12,4},{14,6},{16,24},{18,... | collective-permute-start | bytes 196616 | tf_op jit(solution)/shard_map/ppermute | solution.py:46
  60.4 6.6 %collective-permute-start.26 = (bf16[64,512]{1,0:T(8,128)(2,1)S(1)}, bf16[64,512]{1,0:T(8,128)(2,1)S(1)}, u32[]{:S(2)}, u32[]{:S(2)}) collective-permute-start(bf16[64,512]{1,0:T(8,128)(2,1)S(1)} %get-tuple-element.95), channel_id=1, source_target_pairs={{0,16},{2,18},{4,20},{6,22},{8,24},{10,26},{12,28},{14,30},{16,0},... | collective-permute-start | bytes 196616 | tf_op jit(solution)/shard_map/ppermute | solution.py:46
  61.7 8.0 %collective-permute-start.27 = (bf16[64,512]{1,0:T(8,128)(2,1)S(1)}, bf16[64,512]{1,0:T(8,128)(2,1)S(1)}, u32[]{:S(2)}, u32[]{:S(2)}) collective-permute-start(bf16[64,512]{1,0:T(8,128)(2,1)S(1)} %get-tuple-element.91.refs_6_), channel_id=1, source_target_pairs={{0,24},{2,26},{4,28},{6,30},{8,16},{10,18},{12,20},{14,22},{16,8},... | collective-permute-start | bytes 196616 | tf_op jit(solution)/shard_map/ppermute | solution.py:46
  66.4 5.4 %collective-permute-start.31 = (bf16[128,512]{1,0:T(8,128)(2,1)S(1)}, bf16[128,512]{1,0:T(8,128)(2,1)S(1)}, u32[]{:S(2)}, u32[]{:S(2)}) collective-permute-start(bf16[128,512]{1,0:T(8,128)(2,1)S(1)} %get-tuple-element.102), channel_id=1, source_target_pairs={{1,0},{0,1},{3,2},{2,3},{5,4},{4,5},{7,6},{6,7},{9,8},{8,9},{11,10... | collective-permute-start | bytes 393224 | tf_op jit(solution)/shard_map/ppermute | solution.py:51
  66.5 5.3 %collective-permute-start.32 = (bf16[128,512]{1,0:T(8,128)(2,1)S(1)}, bf16[128,512]{1,0:T(8,128)(2,1)S(1)}, u32[]{:S(2)}, u32[]{:S(2)}) collective-permute-start(bf16[128,512]{1,0:T(8,128)(2,1)S(1)} %get-tuple-element.96.refs_5_), channel_id=1, source_target_pairs={{1,0},{0,1},{3,2},{2,3},{5,4},{4,5},{7,6},{6,7},{9,8},{8,9},{11,10... | collective-permute-start | bytes 393224 | tf_op jit(solution)/shard_map/ppermute | solution.py:51
  71.2 4.7 %collective-permute-start.29 = (bf16[128,512]{1,0:T(8,128)(2,1)S(1)}, bf16[128,512]{1,0:T(8,128)(2,1)S(1)}, u32[]{:S(2)}, u32[]{:S(2)}) collective-permute-start(bf16[128,512]{1,0:T(8,128)(2,1)S(1)} %get-tuple-element.99), channel_id=1, source_target_pairs={{1,0},{0,1},{3,2},{2,3},{5,4},{4,5},{7,6},{6,7},{9,8},{8,9},{11,10... | collective-permute-start | bytes 393224 | tf_op jit(solution)/shard_map/ppermute | solution.py:51
  71.3 5.3 %collective-permute-start.30 = (bf16[128,512]{1,0:T(8,128)(2,1)S(1)}, bf16[128,512]{1,0:T(8,128)(2,1)S(1)}, u32[]{:S(2)}, u32[]{:S(2)}) collective-permute-start(bf16[128,512]{1,0:T(8,128)(2,1)S(1)} %get-tuple-element.100.refs_8_), channel_id=1, source_target_pairs={{1,0},{0,1},{3,2},{2,3},{5,4},{4,5},{7,6},{6,7},{9,8},{8,9},{11,10... | collective-permute-start | bytes 393224 | tf_op jit(solution)/shard_map/ppermute | solution.py:51
  72.4 4.8 %collective-permute-start.37 = (bf16[64,512]{1,0:T(8,128)(2,1)S(1)}, bf16[64,512]{1,0:T(8,128)(2,1)S(1)}, u32[]{:S(2)}, u32[]{:S(2)}) collective-permute-start(bf16[64,512]{1,0:T(8,128)(2,1)S(1)} %get-tuple-element.110), channel_id=1, source_target_pairs={{0,8},{2,10},{4,12},{6,14},{8,0},{10,2},{12,4},{14,6},{16,24},{18,... | collective-permute-start | bytes 196616 | tf_op jit(solution)/shard_map/ppermute | solution.py:46
  72.7 6.5 %collective-permute-start.38 = (bf16[64,512]{1,0:T(8,128)(2,1)S(1)}, bf16[64,512]{1,0:T(8,128)(2,1)S(1)}, u32[]{:S(2)}, u32[]{:S(2)}) collective-permute-start(bf16[64,512]{1,0:T(8,128)(2,1)S(1)} %get-tuple-element.111), channel_id=1, source_target_pairs={{0,16},{2,18},{4,20},{6,22},{8,24},{10,26},{12,28},{14,30},{16,0},... | collective-permute-start | bytes 196616 | tf_op jit(solution)/shard_map/ppermute | solution.py:46
  74.4 7.4 %collective-permute-start.39 = (bf16[64,512]{1,0:T(8,128)(2,1)S(1)}, bf16[64,512]{1,0:T(8,128)(2,1)S(1)}, u32[]{:S(2)}, u32[]{:S(2)}) collective-permute-start(bf16[64,512]{1,0:T(8,128)(2,1)S(1)} %get-tuple-element.103.refs_5_), channel_id=1, source_target_pairs={{0,24},{2,26},{4,28},{6,30},{8,16},{10,18},{12,20},{14,22},{16,8},... | collective-permute-start | bytes 196616 | tf_op jit(solution)/shard_map/ppermute | solution.py:46
  76.0 7.5 %collective-permute-start.36 = (bf16[4,64,512]{2,1,0:T(8,128)(2,1)S(1)}, bf16[4,64,512]{2,1,0:T(8,128)(2,1)S(1)}, u32[]{:S(2)}, u32[]{:S(2)}) collective-permute-start(bf16[4,64,512]{2,1,0:T(8,128)(2,1)S(1)} %get-tuple-element.97.refs_4_), channel_id=1, source_target_pairs={{0,4},{2,6},{4,0},{6,2},{8,12},{10,14},{12,8},{14,10},{16,20},{18,... | collective-permute-start | bytes 786440 | tf_op jit(solution)/shard_map/ppermute | solution.py:46
  82.2 7.8 %collective-permute-start.41 = (bf16[4,64,512]{2,1,0:T(8,128)(2,1)S(1)}, bf16[4,64,512]{2,1,0:T(8,128)(2,1)S(1)}, u32[]{:S(2)}, u32[]{:S(2)}) collective-permute-start(bf16[4,64,512]{2,1,0:T(8,128)(2,1)S(1)} %get-tuple-element.112.refs_3_), channel_id=1, source_target_pairs={{0,4},{2,6},{4,0},{6,2},{8,12},{10,14},{12,8},{14,10},{16,20},{18,... | collective-permute-start | bytes 786440 | tf_op jit(solution)/shard_map/ppermute | solution.py:46
  83.7 11.9 %collective-permute-start.40 = (bf16[4,64,512]{2,1,0:T(8,128)(2,1)S(1)}, bf16[4,64,512]{2,1,0:T(8,128)(2,1)S(1)}, u32[]{:S(2)}, u32[]{:S(2)}) collective-permute-start(bf16[4,64,512]{2,1,0:T(8,128)(2,1)S(1)} %get-tuple-element.114.refs_3_), channel_id=1, source_target_pairs={{0,2},{2,0},{4,6},{6,4},{8,10},{10,8},{12,14},{14,12},{16,18},{18,... | collective-permute-start | bytes 786440 | tf_op jit(solution)/shard_map/ppermute | solution.py:46
  90.3 6.9 %collective-permute-start.42 = (bf16[4,64,512]{2,1,0:T(8,128)(2,1)S(1)}, bf16[4,64,512]{2,1,0:T(8,128)(2,1)S(1)}, u32[]{:S(2)}, u32[]{:S(2)}) collective-permute-start(bf16[4,64,512]{2,1,0:T(8,128)(2,1)S(1)} %get-tuple-element.116.refs_3_), channel_id=1, source_target_pairs={{0,2},{2,0},{4,6},{6,4},{8,10},{10,8},{12,14},{14,12},{16,18},{18,... | collective-permute-start | bytes 786440 | tf_op jit(solution)/shard_map/ppermute | solution.py:46
  92.2 16.3 %collective-permute-start.33 = (bf16[2,64,512]{2,1,0:T(8,128)(2,1)S(1)}, bf16[2,64,512]{2,1,0:T(8,128)(2,1)S(1)}, u32[]{:S(2)}, u32[]{:S(2)}) collective-permute-start(bf16[2,64,512]{2,1,0:T(8,128)(2,1)S(1)} %get-tuple-element.105), channel_id=1, source_target_pairs={{0,8},{2,10},{4,12},{6,14},{8,0},{10,2},{12,4},{14,6},{16,24},{18,... | collective-permute-start | bytes 393224 | tf_op jit(solution)/shard_map/ppermute | solution.py:46
  92.5 16.0 %collective-permute-start.34 = (bf16[2,64,512]{2,1,0:T(8,128)(2,1)S(1)}, bf16[2,64,512]{2,1,0:T(8,128)(2,1)S(1)}, u32[]{:S(2)}, u32[]{:S(2)}) collective-permute-start(bf16[2,64,512]{2,1,0:T(8,128)(2,1)S(1)} %get-tuple-element.106), channel_id=1, source_target_pairs={{0,16},{2,18},{4,20},{6,22},{8,24},{10,26},{12,28},{14,30},{16,0},... | collective-permute-start | bytes 393224 | tf_op jit(solution)/shard_map/ppermute | solution.py:46
  95.1 13.3 %collective-permute-start.35 = (bf16[2,64,512]{2,1,0:T(8,128)(2,1)S(1)}, bf16[2,64,512]{2,1,0:T(8,128)(2,1)S(1)}, u32[]{:S(2)}, u32[]{:S(2)}) collective-permute-start(bf16[2,64,512]{2,1,0:T(8,128)(2,1)S(1)} %get-tuple-element.107.refs_5_), channel_id=1, source_target_pairs={{0,24},{2,26},{4,28},{6,30},{8,16},{10,18},{12,20},{14,22},{16,8},... | collective-permute-start | bytes 393224 | tf_op jit(solution)/shard_map/ppermute | solution.py:46
  98.7 7.3 %collective-permute-start.43 = (bf16[2,512]{1,0:T(2,128)(2,1)S(1)}, bf16[2,512]{1,0:T(2,128)(2,1)S(1)}, u32[]{:S(2)}, u32[]{:S(2)}) collective-permute-start(bf16[2,512]{1,0:T(2,128)(2,1)S(1)} %get-tuple-element.123.refs_4_), channel_id=1, source_target_pairs={{2,4},{4,2},{6,8},{8,6},{10,12},{12,10},{14,16},{16,14},{18,20},{2... | collective-permute-start | bytes 6152 | tf_op jit(solution)/shard_map/ppermute | solution.py:41
  103.6 3.7 %collective-permute-start.44 = (bf16[2,512]{1,0:T(2,128)(2,1)S(1)}, bf16[2,512]{1,0:T(2,128)(2,1)S(1)}, u32[]{:S(2)}, u32[]{:S(2)}) collective-permute-start(bf16[2,512]{1,0:T(2,128)(2,1)S(1)} %get-tuple-element.123.refs_4_), channel_id=1, source_target_pairs={{0,2},{2,0},{4,6},{6,4},{8,10},{10,8},{12,14},{14,12},{16,18},{18,... | collective-permute-start | bytes 6152 | tf_op jit(solution)/shard_map/ppermute | solution.py:37

commit v2 on v1

--- a/solution.py
+++ b/solution.py
@@ -633,10 +633,10 @@
             grad_act(p + 1)
             out_product(p)
             late_factor(p + 1)
+        if p == pieces - 1:
+            out_product(p)
         if p > 0:
             regroup(p - 1)
-        if p == pieces - 1:
-            out_product(p)
         transposed_back(p)
     early_units = range(pieces - 1)
     late_units = range(pieces - 1, pieces)

time: 110 us -> 108 us (0.982)
    ppermute x2, starting transfers between devices: 9.16 us -> 6.36 us  [neighbours(): return (near, lax.ppermute(edges, axis, route))]
    ppermute x2, starting transfers between devices: 0.79 us -> 3.09 us  [neighbours(): near = lax.ppermute(edges, axis, [(i, i ^ 1) for i in range(count)])]
    ppermute x2, waiting for transfers between devices: 2.27 us -> 3.69 us  [neighbours(): return (near, lax.ppermute(edges, axis, route))]
    ppermute x2, waiting for transfers between devices: 1.31 us -> 0.01 us  [neighbours(): near = lax.ppermute(edges, axis, [(i, i ^ 1) for i in range(count)])]
  transfers between devices with their start and end apart: 45 -> 45, of which waited for: 15 -> 14; matrix products, arithmetic and copies ran while one was open for 0% -> 0% of each run, Pallas kernels for 18% -> 19%
where the time goes in v2:
time: 108 us
  starting transfers between devices  48.7 us (45%)
  waiting for transfers between devices  29.2 us (27%)
  Pallas kernels  23.5 us (22%)
  local copies, waits for them, and re-layouts  4.62 us (4%)
    ppermute x28, starting transfers between devices, from_flipped(): return lax.ppermute(block, axis, [(i, i ^ mask) for i in range(count)])  36 us
    ppermute x28, waiting for transfers between devices, from_flipped(): return lax.ppermute(block, axis, [(i, i ^ mask) for i in range(count)])  25.4 us
    pallas_call x36, Pallas kernels, call(): pl.pallas_call(body, out_shape=[jax.ShapeDtypeStruct(shape, kind) for sha...  23.5 us
    ppermute x2, starting transfers between devices, neighbours(): return (near, lax.ppermute(edges, axis, route))  6.36 us
    unnamed x12, local copies, waits for them, and re-layouts  3.9 us
    ppermute x2, waiting for transfers between devices, neighbours(): return (near, lax.ppermute(edges, axis, route))  3.69 us
    ppermute x13, starting transfers between devices, from_offset(): lax.ppermute(block, axis, [((i + offset) % count, i) for i in range(count)])  3.19 us
    ppermute x2, starting transfers between devices, neighbours(): near = lax.ppermute(edges, axis, [(i, i ^ 1) for i in range(count)])  3.09 us
  transfers between devices with their start and end apart: 45, of which 14 were waited for; matrix products, arithmetic and copies ran while one was open for 0% of the time, Pallas kernels for 19%

profile of v2, /device:TPU:8, one launch (start us, length us, event | category | flops | bytes accessed | tf_op | source)
XLA Modules:
  0.0 107.7 jit_solution(872589840333314071)
XLA Ops:
  0.6 0.7 fusion
  1.4 0.7 pad_maximum_fusion
  2.1 1.6 %collective-permute-start.1 = (bf16[5,512]{1,0:T(8,128)(2,1)S(1)}, bf16[5,512]{1,0:T(8,128)(2,1)S(1)}, u32[]{:S(2)}, u32[]{:S(2)}) collective-permute-start(bf16[5,512]{1,0:T(8,128)(2,1)S(1)} %pad_maximum_fusion), channel_id=1, source_target_pairs={{0,2},{2,0},{4,6},{6,4},{8,10},{10,8},{12,14},{14,12},{16,18},{18,... | collective-permute-start | bytes 15368 | tf_op jit(solution)/shard_map/ppermute | solution.py:37
  3.6 3.3 %collective-permute-start = (bf16[5,512]{1,0:T(8,128)(2,1)S(1)}, bf16[5,512]{1,0:T(8,128)(2,1)S(1)}, u32[]{:S(2)}, u32[]{:S(2)}) collective-permute-start(bf16[5,512]{1,0:T(8,128)(2,1)S(1)} %pad_maximum_fusion), channel_id=1, source_target_pairs={{2,4},{4,2},{6,8},{8,6},{10,12},{12,10},{14,16},{16,14},{18,20},{2... | collective-permute-start | bytes 15368 | tf_op jit(solution)/shard_map/ppermute | solution.py:41
  6.9 1.1 %copy-done.2 = bf16[6,8,64,128]{3,2,1,0:T(8,128)(2,1)S(1)} copy-done((bf16[6,8,64,128]{3,2,1,0:T(8,128)(2,1)S(1)}, bf16[6,8,64,128]{3,2,1,0:T(8,128)(2,1)}, u32[]{:S(2)}) %copy-start.2) | copy-done | bytes 786456
  8.0 1.0 copy-done.3
  9.1 0.7 copy-done.5
  9.9 1.1 collective-permute-done.refs_2_
  10.9 2.1 %conv_and_local_factors.1 = (bf16[512,512]{1,0:T(8,128)(2,1)}, bf16[2,64,512]{2,1,0:T(8,128)(2,1)S(1)}, bf16[2,64,512]{2,1,0:T(8,128)(2,1)S(1)}, bf16[2,64,512]{2,1,0:T(8,128)(2,1)S(1)}, bf16[2,64,512]{2,1,0:T(8,128)(2,1)S(1)}) custom-call(s32[2,8]{1,0:T(2,128)S(1)} %get-tuple-element.65.refs_0_.refs_5_, bf16[512,512]{1,0:T(8,128)(2,1)S(1)} %get-tuple-element.66.refs_1_, ...), custom_call_target="tpu_custom_call" | custom-call | tf_op jit(solution)/shard_map/conv_and_local_factors/pallas_call | solution.py:60
  13.1 0.6 collective-permute-start.3
  13.7 1.0 copy-done.4
  14.8 2.7 %collective-permute-start.12 = (bf16[6,64,512]{2,1,0:T(8,128)(2,1)S(1)}, bf16[6,64,512]{2,1,0:T(8,128)(2,1)S(1)}, u32[]{:S(2)}, u32[]{:S(2)}) collective-permute-start(bf16[6,64,512]{2,1,0:T(8,128)(2,1)S(1)} %get-tuple-element.71.refs_3_), channel_id=1, source_target_pairs={{0,16},{2,18},{4,20},{6,22},{8,24},{10,26},{12,28},{14,30},{16,0},... | collective-permute-start | bytes 1179656 | tf_op jit(solution)/shard_map/ppermute | solution.py:46
  17.4 1.5 %collective-permute-start.2 = (bf16[2,64,512]{2,1,0:T(8,128)(2,1)S(1)}, bf16[2,64,512]{2,1,0:T(8,128)(2,1)S(1)}, u32[]{:S(2)}, u32[]{:S(2)}) collective-permute-start(bf16[2,64,512]{2,1,0:T(8,128)(2,1)S(1)} %get-tuple-element.68.refs_0_), channel_id=1, source_target_pairs={{0,2},{2,0},{4,6},{6,4},{8,10},{10,8},{12,14},{14,12},{16,18},{18,... | collective-permute-start | bytes 393224 | tf_op jit(solution)/shard_map/ppermute | solution.py:46
  19.2 0.7 collective-permute-start.6
  19.9 0.4 collective-permute-start.8
  20.3 1.5 %collective-permute-start.5 = (bf16[2,64,512]{2,1,0:T(8,128)(2,1)S(1)}, bf16[2,64,512]{2,1,0:T(8,128)(2,1)S(1)}, u32[]{:S(2)}, u32[]{:S(2)}) collective-permute-start(bf16[2,64,512]{2,1,0:T(8,128)(2,1)S(1)} %get-tuple-element.72.refs_0_), channel_id=1, source_target_pairs={{0,2},{2,0},{4,6},{6,4},{8,10},{10,8},{12,14},{14,12},{16,18},{18,... | collective-permute-start | bytes 393224 | tf_op jit(solution)/shard_map/ppermute | solution.py:46
  21.8 1.6 %collective-permute-done.2.refs_1_ = bf16[2,64,512]{2,1,0:T(8,128)(2,1)S(1)} collective-permute-done((bf16[2,64,512]{2,1,0:T(8,128)(2,1)S(1)}, bf16[2,64,512]{2,1,0:T(8,128)(2,1)S(1)}, u32[]{:S(2)}, u32[]{:S(2)}) %collective-permute-start.2) | collective-permute-done | bytes 131104 | tf_op jit(solution)/shard_map/ppermute | solution.py:46
  24.0 1.4 %collective-permute-done.6.refs_1_ = bf16[2,64,512]{2,1,0:T(8,128)(2,1)S(1)} collective-permute-done((bf16[2,64,512]{2,1,0:T(8,128)(2,1)S(1)}, bf16[2,64,512]{2,1,0:T(8,128)(2,1)S(1)}, u32[]{:S(2)}, u32[]{:S(2)}) %collective-permute-start.6) | collective-permute-done | bytes 131104 | tf_op jit(solution)/shard_map/ppermute | solution.py:46
  25.6 0.8 collective-permute-start.7
  26.4 0.4 collective-permute-start.11
  27.1 1.8 %collective-permute-done.4.refs_1_ = bf16[2,64,512]{2,1,0:T(8,128)(2,1)S(1)} collective-permute-done((bf16[2,64,512]{2,1,0:T(8,128)(2,1)S(1)}, bf16[2,64,512]{2,1,0:T(8,128)(2,1)S(1)}, u32[]{:S(2)}, u32[]{:S(2)}) %collective-permute-start.4) | collective-permute-done | bytes 131104 | tf_op jit(solution)/shard_map/ppermute | solution.py:46
  29.2 3.7 %collective-permute-done.8.refs_3_.refs_1_.refs_5_ = bf16[4,64,512]{2,1,0:T(8,128)(2,1)S(1)} collective-permute-done((bf16[4,64,512]{2,1,0:T(8,128)(2,1)S(1)}, bf16[4,64,512]{2,1,0:T(8,128)(2,1)S(1)}, u32[]{:S(2)}, u32[]{:S(2)}) %collective-permute-start.8) | collective-permute-done | bytes 262176 | tf_op jit(solution)/shard_map/ppermute | solution.py:46
  33.0 1.4 %collective-permute-done.7.refs_1_ = bf16[2,64,512]{2,1,0:T(8,128)(2,1)S(1)} collective-permute-done((bf16[2,64,512]{2,1,0:T(8,128)(2,1)S(1)}, bf16[2,64,512]{2,1,0:T(8,128)(2,1)S(1)}, u32[]{:S(2)}, u32[]{:S(2)}) %collective-permute-start.7) | collective-permute-done | bytes 131104 | tf_op jit(solution)/shard_map/ppermute | solution.py:46
  34.8 2.5 %collective-permute-start.13 = (bf16[3,64,512]{2,1,0:T(8,128)(2,1)S(1)}, bf16[3,64,512]{2,1,0:T(8,128)(2,1)S(1)}, u32[]{:S(2)}, u32[]{:S(2)}) collective-permute-start(bf16[3,64,512]{2,1,0:T(8,128)(2,1)S(1)} %forward.1.refs_3_), channel_id=1, source_target_pairs={{0,8},{2,10},{4,12},{6,14},{8,0},{10,2},{12,4},{14,6},{16,24},{18,... | collective-permute-start | bytes 589832 | tf_op jit(solution)/shard_map/ppermute | solution.py:46
  37.3 2.7 %collective-permute-start.9 = (bf16[2,64,512]{2,1,0:T(8,128)(2,1)S(1)}, bf16[2,64,512]{2,1,0:T(8,128)(2,1)S(1)}, u32[]{:S(2)}, u32[]{:S(2)}) collective-permute-start(bf16[2,64,512]{2,1,0:T(8,128)(2,1)S(1)} %get-tuple-element.75.refs_1_), channel_id=1, source_target_pairs={{0,16},{2,18},{4,20},{6,22},{8,24},{10,26},{12,28},{14,30},{16,0},... | collective-permute-start | bytes 393224 | tf_op jit(solution)/shard_map/ppermute | solution.py:46
  40.3 2.5 %collective-permute-start.14 = (bf16[2,64,512]{2,1,0:T(8,128)(2,1)S(1)}, bf16[2,64,512]{2,1,0:T(8,128)(2,1)S(1)}, u32[]{:S(2)}, u32[]{:S(2)}) collective-permute-start(bf16[2,64,512]{2,1,0:T(8,128)(2,1)S(1)} %factor.13.refs_3_.refs_0_), channel_id=1, source_target_pairs={{0,4},{2,6},{4,0},{6,2},{8,12},{10,14},{12,8},{14,10},{16,20},{18,... | collective-permute-start | bytes 393224 | tf_op jit(solution)/shard_map/ppermute | solution.py:46
  43.1 2.0 %collective-permute-start.17 = (bf16[2,64,512]{2,1,0:T(8,128)(2,1)S(1)}, bf16[2,64,512]{2,1,0:T(8,128)(2,1)S(1)}, u32[]{:S(2)}, u32[]{:S(2)}) collective-permute-start(bf16[2,64,512]{2,1,0:T(8,128)(2,1)S(1)} %factor.14.refs_1_), channel_id=1, source_target_pairs={{0,8},{2,10},{4,12},{6,14},{8,0},{10,2},{12,4},{14,6},{16,24},{18,... | collective-permute-start | bytes 393224 | tf_op jit(solution)/shard_map/ppermute | solution.py:46
  45.1 1.0 collective-permute-done.9.refs_0_
  46.8 1.3 %collective-permute-done.17.refs_1_ = bf16[2,64,512]{2,1,0:T(8,128)(2,1)S(1)} collective-permute-done((bf16[2,64,512]{2,1,0:T(8,128)(2,1)S(1)}, bf16[2,64,512]{2,1,0:T(8,128)(2,1)S(1)}, u32[]{:S(2)}, u32[]{:S(2)}) %collective-permute-start.17) | collective-permute-done | bytes 131104 | tf_op jit(solution)/shard_map/ppermute | solution.py:46
  48.6 0.5 collective-permute-start.19
  49.2 0.4 collective-permute-start.16
  49.6 1.2 %collective-permute-start.20 = (bf16[2,64,512]{2,1,0:T(8,128)(2,1)S(1)}, bf16[2,64,512]{2,1,0:T(8,128)(2,1)S(1)}, u32[]{:S(2)}, u32[]{:S(2)}) collective-permute-start(bf16[2,64,512]{2,1,0:T(8,128)(2,1)S(1)} %get-tuple-element.79.refs_4_), channel_id=1, source_target_pairs={{0,16},{2,18},{4,20},{6,22},{8,24},{10,26},{12,28},{14,30},{16,0},... | collective-permute-start | bytes 393224 | tf_op jit(solution)/shard_map/ppermute | solution.py:46
  50.8 1.3 %grad_act.2.refs_4_.refs_6_ = bf16[256,2048]{1,0:T(8,128)(2,1)S(1)} custom-call(bf16[256,512]{1,0:T(8,128)(2,1)S(1)} %get-tuple-element.80.refs_0_, bf16[256,512]{1,0:T(8,128)(2,1)S(1)} %collective-permute-done.18.refs_1_, bf16[2048,1024]{1,0:T(8,128)(2,1)S(1)} %copy-done, bf16[256,512]{1,0:T(8,128)(2,1)S(1)} %get-tuple-element.81.refs_3_.refs_0_), custom_call_target="tpu_custom_call" | custom-call | tf_op jit(solution)/shard_map/grad_act/pallas_call | solution.py:60
  52.1 3.0 %mlp_hidden_and_grad.2 = (bf16[256,2048]{1,0:T(8,128)(2,1)S(1)}, f32[256,512]{1,0:T(8,128)S(1)}, bf16[128,512]{1,0:T(8,128)(2,1)S(1)}, bf16[128,512]{1,0:T(8,128)(2,1)S(1)}) custom-call(bf16[128,512]{1,0:T(8,128)(2,1)S(1)} %get-tuple-element.76.refs_0_.refs_1_, bf16[128,512]{1,0:T(8,128)(2,1)S(1)} %get-tuple-element.77.refs_4_.refs_1_.refs_2_, ...), custom_call_target="tpu_custom_call" | custom-call | tf_op jit(solution)/shard_map/mlp_hidden_and_grad/pallas_call | solution.py:60
  55.2 0.5 collective-permute-start.24
  55.7 1.3 %grad_act.3.refs_4_ = bf16[256,2048]{1,0:T(8,128)(2,1)S(1)} custom-call(bf16[256,512]{1,0:T(8,128)(2,1)S(1)} %get-tuple-element.81.refs_3_.refs_0_, bf16[256,512]{1,0:T(8,128)(2,1)S(1)} %collective-permute-done.19.refs_1_, bf16[2048,1024]{1,0:T(8,128)(2,1)S(1)} %copy-done, bf16[128,512]{1,0:T(8,128)(2,1)S(1)} %get-tuple-element.83.refs_3_), custom_call_target="tpu_custom_call" | custom-call | tf_op jit(solution)/shard_map/grad_act/pallas_call | solution.py:60
  57.0 1.3 %mlp_out.2 = (f32[256,512]{1,0:T(8,128)S(1)}, bf16[256,512]{1,0:T(8,128)(2,1)S(1)}) custom-call(bf16[256,2048]{1,0:T(8,128)(2,1)S(1)} %get-tuple-element.82.refs_0_, bf16[128,512]{1,0:T(8,128)(2,1)S(1)} %get-tuple-element.76.refs_0_.refs_1_, bf16[128,512]{1,0:T(8,128)(2,1)S(1)} %get-tuple-element.77.refs_4_.refs_1_.refs_2_, bf16[2048,1024]{1,0:T(8,128)(2,1)S(1)} %copy-done, ...), custom_call_target="tpu_custom_call" | custom-call | tf_op jit(solution)/shard_map/mlp_out/pallas_call | solution.py:60
  58.7 0.4 collective-permute-start.22
  59.2 0.6 late_and_early_back.2
  59.8 2.1 %collective-permute-start.30 = (bf16[64,512]{1,0:T(8,128)(2,1)S(1)}, bf16[64,512]{1,0:T(8,128)(2,1)S(1)}, u32[]{:S(2)}, u32[]{:S(2)}) collective-permute-start(bf16[64,512]{1,0:T(8,128)(2,1)S(1)} %get-tuple-element.100), channel_id=1, source_target_pairs={{0,8},{2,10},{4,12},{6,14},{8,0},{10,2},{12,4},{14,6},{16,24},{18,... | collective-permute-start | bytes 196616 | tf_op jit(solution)/shard_map/ppermute | solution.py:46
  61.8 1.7 %collective-permute-start.31 = (bf16[64,512]{1,0:T(8,128)(2,1)S(1)}, bf16[64,512]{1,0:T(8,128)(2,1)S(1)}, u32[]{:S(2)}, u32[]{:S(2)}) collective-permute-start(bf16[64,512]{1,0:T(8,128)(2,1)S(1)} %get-tuple-element.101), channel_id=1, source_target_pairs={{0,16},{2,18},{4,20},{6,22},{8,24},{10,26},{12,28},{14,30},{16,0},... | collective-permute-start | bytes 196616 | tf_op jit(solution)/shard_map/ppermute | solution.py:46
  63.5 3.2 %mlp_hidden_and_grad.3 = (bf16[256,2048]{1,0:T(8,128)(2,1)S(1)}, f32[256,512]{1,0:T(8,128)S(1)}, bf16[128,512]{1,0:T(8,128)(2,1)S(1)}, bf16[128,512]{1,0:T(8,128)(2,1)S(1)}) custom-call(bf16[128,512]{1,0:T(8,128)(2,1)S(1)} %get-tuple-element.87.refs_0_.refs_1_, bf16[128,512]{1,0:T(8,128)(2,1)S(1)} %get-tuple-element.88.refs_8_.refs_1_.refs_2_, ...), custom_call_target="tpu_custom_call" | custom-call | tf_op jit(solution)/shard_map/mlp_hidden_and_grad/pallas_call | solution.py:60
  67.3 1.3 %mlp_out.3 = (f32[256,512]{1,0:T(8,128)S(1)}, bf16[128,512]{1,0:T(8,128)(2,1)S(1)}, bf16[128,512]{1,0:T(8,128)(2,1)S(1)}) custom-call(bf16[256,2048]{1,0:T(8,128)(2,1)S(1)} %get-tuple-element.92.refs_0_, bf16[128,512]{1,0:T(8,128)(2,1)S(1)} %get-tuple-element.87.refs_0_.refs_1_, bf16[128,512]{1,0:T(8,128)(2,1)S(1)} %get-tuple-element.88.refs_8_.refs_1_.refs_2_, ...), custom_call_target="tpu_custom_call" | custom-call | tf_op jit(solution)/shard_map/mlp_out/pallas_call | solution.py:60
  68.9 1.2 %collective-permute-done.32.refs_3_ = bf16[64,512]{1,0:T(8,128)(2,1)S(1)} collective-permute-done((bf16[64,512]{1,0:T(8,128)(2,1)S(1)}, bf16[64,512]{1,0:T(8,128)(2,1)S(1)}, u32[]{:S(2)}, u32[]{:S(2)}) %collective-permute-start.32) | collective-permute-done | bytes 65568 | tf_op jit(solution)/shard_map/ppermute | solution.py:46
  70.6 0.6 late_and_early_back.3
  71.1 1.7 %collective-permute-start.37 = (bf16[64,512]{1,0:T(8,128)(2,1)S(1)}, bf16[64,512]{1,0:T(8,128)(2,1)S(1)}, u32[]{:S(2)}, u32[]{:S(2)}) collective-permute-start(bf16[64,512]{1,0:T(8,128)(2,1)S(1)} %get-tuple-element.110), channel_id=1, source_target_pairs={{0,8},{2,10},{4,12},{6,14},{8,0},{10,2},{12,4},{14,6},{16,24},{18,... | collective-permute-start | bytes 196616 | tf_op jit(solution)/shard_map/ppermute | solution.py:46
  72.8 1.5 %collective-permute-start.38 = (bf16[64,512]{1,0:T(8,128)(2,1)S(1)}, bf16[64,512]{1,0:T(8,128)(2,1)S(1)}, u32[]{:S(2)}, u32[]{:S(2)}) collective-permute-start(bf16[64,512]{1,0:T(8,128)(2,1)S(1)} %get-tuple-element.111), channel_id=1, source_target_pairs={{0,16},{2,18},{4,20},{6,22},{8,24},{10,26},{12,28},{14,30},{16,0},... | collective-permute-start | bytes 196616 | tf_op jit(solution)/shard_map/ppermute | solution.py:46
  74.7 1.4 %collective-permute-start.36 = (bf16[4,64,512]{2,1,0:T(8,128)(2,1)S(1)}, bf16[4,64,512]{2,1,0:T(8,128)(2,1)S(1)}, u32[]{:S(2)}, u32[]{:S(2)}) collective-permute-start(bf16[4,64,512]{2,1,0:T(8,128)(2,1)S(1)} %get-tuple-element.102.refs_8_), channel_id=1, source_target_pairs={{0,4},{2,6},{4,0},{6,2},{8,12},{10,14},{12,8},{14,10},{16,20},{18,... | collective-permute-start | bytes 786440 | tf_op jit(solution)/shard_map/ppermute | solution.py:46
  76.2 2.7 %collective-permute-done.38.refs_2_ = bf16[64,512]{1,0:T(8,128)(2,1)S(1)} collective-permute-done((bf16[64,512]{1,0:T(8,128)(2,1)S(1)}, bf16[64,512]{1,0:T(8,128)(2,1)S(1)}, u32[]{:S(2)}, u32[]{:S(2)}) %collective-permute-start.38) | collective-permute-done | bytes 65568 | tf_op jit(solution)/shard_map/ppermute | solution.py:46
  78.9 2.3 %collective-permute-done.39.refs_3_ = bf16[64,512]{1,0:T(8,128)(2,1)S(1)} collective-permute-done((bf16[64,512]{1,0:T(8,128)(2,1)S(1)}, bf16[64,512]{1,0:T(8,128)(2,1)S(1)}, u32[]{:S(2)}, u32[]{:S(2)}) %collective-permute-start.39) | collective-permute-done | bytes 65568 | tf_op jit(solution)/shard_map/ppermute | solution.py:46
  81.5 1.4 %collective-permute-start.41 = (bf16[4,64,512]{2,1,0:T(8,128)(2,1)S(1)}, bf16[4,64,512]{2,1,0:T(8,128)(2,1)S(1)}, u32[]{:S(2)}, u32[]{:S(2)}) collective-permute-start(bf16[4,64,512]{2,1,0:T(8,128)(2,1)S(1)} %get-tuple-element.112.refs_3_), channel_id=1, source_target_pairs={{0,4},{2,6},{4,0},{6,2},{8,12},{10,14},{12,8},{14,10},{16,20},{18,... | collective-permute-start | bytes 786440 | tf_op jit(solution)/shard_map/ppermute | solution.py:46
  83.2 1.3 %collective-permute-start.40 = (bf16[4,64,512]{2,1,0:T(8,128)(2,1)S(1)}, bf16[4,64,512]{2,1,0:T(8,128)(2,1)S(1)}, u32[]{:S(2)}, u32[]{:S(2)}) collective-permute-start(bf16[4,64,512]{2,1,0:T(8,128)(2,1)S(1)} %get-tuple-element.114.refs_3_), channel_id=1, source_target_pairs={{0,2},{2,0},{4,6},{6,4},{8,10},{10,8},{12,14},{14,12},{16,18},{18,... | collective-permute-start | bytes 786440 | tf_op jit(solution)/shard_map/ppermute | solution.py:46
  84.5 5.0 %collective-permute-done.41.refs_1_ = bf16[4,64,512]{2,1,0:T(8,128)(2,1)S(1)} collective-permute-done((bf16[4,64,512]{2,1,0:T(8,128)(2,1)S(1)}, bf16[4,64,512]{2,1,0:T(8,128)(2,1)S(1)}, u32[]{:S(2)}, u32[]{:S(2)}) %collective-permute-start.41) | collective-permute-done | bytes 262176 | tf_op jit(solution)/shard_map/ppermute | solution.py:46
  89.8 1.3 %collective-permute-start.42 = (bf16[4,64,512]{2,1,0:T(8,128)(2,1)S(1)}, bf16[4,64,512]{2,1,0:T(8,128)(2,1)S(1)}, u32[]{:S(2)}, u32[]{:S(2)}) collective-permute-start(bf16[4,64,512]{2,1,0:T(8,128)(2,1)S(1)} %get-tuple-element.116.refs_3_), channel_id=1, source_target_pairs={{0,2},{2,0},{4,6},{6,4},{8,10},{10,8},{12,14},{14,12},{16,18},{18,... | collective-permute-start | bytes 786440 | tf_op jit(solution)/shard_map/ppermute | solution.py:46
  91.1 0.9 collective-permute-start.33
  91.9 2.2 %collective-permute-start.34 = (bf16[2,64,512]{2,1,0:T(8,128)(2,1)S(1)}, bf16[2,64,512]{2,1,0:T(8,128)(2,1)S(1)}, u32[]{:S(2)}, u32[]{:S(2)}) collective-permute-start(bf16[2,64,512]{2,1,0:T(8,128)(2,1)S(1)} %get-tuple-element.106), channel_id=1, source_target_pairs={{0,16},{2,18},{4,20},{6,22},{8,24},{10,26},{12,28},{14,30},{16,0},... | collective-permute-start | bytes 393224 | tf_op jit(solution)/shard_map/ppermute | solution.py:46
  94.1 0.5 collective-permute-start.35
  94.9 2.0 %collective-permute-done.42.refs_1_ = bf16[4,64,512]{2,1,0:T(8,128)(2,1)S(1)} collective-permute-done((bf16[4,64,512]{2,1,0:T(8,128)(2,1)S(1)}, bf16[4,64,512]{2,1,0:T(8,128)(2,1)S(1)}, u32[]{:S(2)}, u32[]{:S(2)}) %collective-permute-start.42) | collective-permute-done | bytes 262176 | tf_op jit(solution)/shard_map/ppermute | solution.py:46
  97.2 1.2 %local_factors_back.1 = (bf16[512,512]{1,0:T(8,128)(2,1)S(1)}, bf16[2,512]{1,0:T(2,128)(2,1)S(1)}) custom-call(s32[2,8]{1,0:T(2,128)S(1)} %get-tuple-element.65.refs_0_.refs_5_, f32[4,64,512]{2,1,0:T(8,128)S(1)} %get-tuple-element.117.refs_1_, f32[4,64,512]{2,1,0:T(8,128)S(1)} %get-tuple-element.120.refs_2_, f32[4,64,512]{2,1,0:T(8,128)S(1)} %get-tuple-element.119.refs_3_, ...), custom_call_target="tpu_custom_call" | custom-call | tf_op jit(solution)/shard_map/local_factors_back/pallas_call | solution.py:60
  98.4 3.1 %collective-permute-start.43 = (bf16[2,512]{1,0:T(2,128)(2,1)S(1)}, bf16[2,512]{1,0:T(2,128)(2,1)S(1)}, u32[]{:S(2)}, u32[]{:S(2)}) collective-permute-start(bf16[2,512]{1,0:T(2,128)(2,1)S(1)} %get-tuple-element.123.refs_4_), channel_id=1, source_target_pairs={{2,4},{4,2},{6,8},{8,6},{10,12},{12,10},{14,16},{16,14},{18,20},{2... | collective-permute-start | bytes 6152 | tf_op jit(solution)/shard_map/ppermute | solution.py:41
  101.5 1.5 %collective-permute-start.44 = (bf16[2,512]{1,0:T(2,128)(2,1)S(1)}, bf16[2,512]{1,0:T(2,128)(2,1)S(1)}, u32[]{:S(2)}, u32[]{:S(2)}) collective-permute-start(bf16[2,512]{1,0:T(2,128)(2,1)S(1)} %get-tuple-element.123.refs_4_), channel_id=1, source_target_pairs={{0,2},{2,0},{4,6},{6,4},{8,10},{10,8},{12,14},{14,12},{16,18},{18,... | collective-permute-start | bytes 6152 | tf_op jit(solution)/shard_map/ppermute | solution.py:37
  103.1 2.6 %collective-permute-done.43.refs_1_ = bf16[2,512]{1,0:T(2,128)(2,1)S(1)} collective-permute-done((bf16[2,512]{1,0:T(2,128)(2,1)S(1)}, bf16[2,512]{1,0:T(2,128)(2,1)S(1)}, u32[]{:S(2)}, u32[]{:S(2)}) %collective-permute-start.43) | collective-permute-done | bytes 2080 | tf_op jit(solution)/shard_map/ppermute | solution.py:41
  105.7 1.2 %conv_back.1 = (bf16[512,512]{1,0:T(8,128)(2,1)}, f32[8,128]{1,0:T(8,128)S(1)}) custom-call(bf16[512,512]{1,0:T(8,128)(2,1)S(1)} %get-tuple-element.122.refs_0_, bf16[2,512]{1,0:T(2,128)(2,1)S(1)} %collective-permute-done.43.refs_1_, bf16[2,512]{1,0:T(2,128)(2,1)S(1)} %collective-permute-done.44.refs_2_, bf16[5,512]{1,0:T(8,128)(2,1)S(1)} %collective-permute-done.1.refs_3_, ...), custom_call_target="tpu_custom_call" | custom-call | tf_op jit(solution)/shard_map/conv_back/pallas_call | solution.py:60
  106.9 0.8 assemble.1
  (76 shorter events, 8.0 us)
Async XLA Ops:
  2.1 7.8 %collective-permute-start.1 = (bf16[5,512]{1,0:T(8,128)(2,1)S(1)}, bf16[5,512]{1,0:T(8,128)(2,1)S(1)}, u32[]{:S(2)}, u32[]{:S(2)}) collective-permute-start(bf16[5,512]{1,0:T(8,128)(2,1)S(1)} %pad_maximum_fusion), channel_id=1, source_target_pairs={{0,2},{2,0},{4,6},{6,4},{8,10},{10,8},{12,14},{14,12},{16,18},{18,... | collective-permute-start | bytes 15368 | tf_op jit(solution)/shard_map/ppermute | solution.py:37
  3.6 7.3 %collective-permute-start = (bf16[5,512]{1,0:T(8,128)(2,1)S(1)}, bf16[5,512]{1,0:T(8,128)(2,1)S(1)}, u32[]{:S(2)}, u32[]{:S(2)}) collective-permute-start(bf16[5,512]{1,0:T(8,128)(2,1)S(1)} %pad_maximum_fusion), channel_id=1, source_target_pairs={{2,4},{4,2},{6,8},{8,6},{10,12},{12,10},{14,16},{16,14},{18,20},{2... | collective-permute-start | bytes 15368 | tf_op jit(solution)/shard_map/ppermute | solution.py:41
  6.9 1.1 %copy-start.2 = (bf16[6,8,64,128]{3,2,1,0:T(8,128)(2,1)S(1)}, bf16[6,8,64,128]{3,2,1,0:T(8,128)(2,1)}, u32[]{:S(2)}) copy-start(bf16[6,8,64,128]{3,2,1,0:T(8,128)(2,1)} %refs_0_.1) | copy-start | bytes 2359300
  8.0 1.0 copy-start.3
  9.1 0.7 copy-start.5
  13.1 5.9 %collective-permute-start.3 = (bf16[2,64,512]{2,1,0:T(8,128)(2,1)S(1)}, bf16[2,64,512]{2,1,0:T(8,128)(2,1)S(1)}, u32[]{:S(2)}, u32[]{:S(2)}) collective-permute-start(bf16[2,64,512]{2,1,0:T(8,128)(2,1)S(1)} %get-tuple-element.69.refs_0_), channel_id=1, source_target_pairs={{0,2},{2,0},{4,6},{6,4},{8,10},{10,8},{12,14},{14,12},{16,18},{18,... | collective-permute-start | bytes 393224 | tf_op jit(solution)/shard_map/ppermute | solution.py:46
  13.7 1.0 copy-start.4
  14.8 19.9 %collective-permute-start.12 = (bf16[6,64,512]{2,1,0:T(8,128)(2,1)S(1)}, bf16[6,64,512]{2,1,0:T(8,128)(2,1)S(1)}, u32[]{:S(2)}, u32[]{:S(2)}) collective-permute-start(bf16[6,64,512]{2,1,0:T(8,128)(2,1)S(1)} %get-tuple-element.71.refs_3_), channel_id=1, source_target_pairs={{0,16},{2,18},{4,20},{6,22},{8,24},{10,26},{12,28},{14,30},{16,0},... | collective-permute-start | bytes 1179656 | tf_op jit(solution)/shard_map/ppermute | solution.py:46
  17.4 5.9 %collective-permute-start.2 = (bf16[2,64,512]{2,1,0:T(8,128)(2,1)S(1)}, bf16[2,64,512]{2,1,0:T(8,128)(2,1)S(1)}, u32[]{:S(2)}, u32[]{:S(2)}) collective-permute-start(bf16[2,64,512]{2,1,0:T(8,128)(2,1)S(1)} %get-tuple-element.68.refs_0_), channel_id=1, source_target_pairs={{0,2},{2,0},{4,6},{6,4},{8,10},{10,8},{12,14},{14,12},{16,18},{18,... | collective-permute-start | bytes 393224 | tf_op jit(solution)/shard_map/ppermute | solution.py:46
  19.2 6.1 %collective-permute-start.6 = (bf16[2,64,512]{2,1,0:T(8,128)(2,1)S(1)}, bf16[2,64,512]{2,1,0:T(8,128)(2,1)S(1)}, u32[]{:S(2)}, u32[]{:S(2)}) collective-permute-start(bf16[2,64,512]{2,1,0:T(8,128)(2,1)S(1)} %factor.8.refs_3_.refs_0_), channel_id=1, source_target_pairs={{0,4},{2,6},{4,0},{6,2},{8,12},{10,14},{12,8},{14,10},{16,20},{18,... | collective-permute-start | bytes 393224 | tf_op jit(solution)/shard_map/ppermute | solution.py:46
  19.9 13.1 %collective-permute-start.8 = (bf16[4,64,512]{2,1,0:T(8,128)(2,1)S(1)}, bf16[4,64,512]{2,1,0:T(8,128)(2,1)S(1)}, u32[]{:S(2)}, u32[]{:S(2)}) collective-permute-start(bf16[4,64,512]{2,1,0:T(8,128)(2,1)S(1)} %get-tuple-element.73), channel_id=1, source_target_pairs={{0,8},{2,10},{4,12},{6,14},{8,0},{10,2},{12,4},{14,6},{16,24},{18,... | collective-permute-start | bytes 786440 | tf_op jit(solution)/shard_map/ppermute | solution.py:46
  20.3 6.1 %collective-permute-start.5 = (bf16[2,64,512]{2,1,0:T(8,128)(2,1)S(1)}, bf16[2,64,512]{2,1,0:T(8,128)(2,1)S(1)}, u32[]{:S(2)}, u32[]{:S(2)}) collective-permute-start(bf16[2,64,512]{2,1,0:T(8,128)(2,1)S(1)} %get-tuple-element.72.refs_0_), channel_id=1, source_target_pairs={{0,2},{2,0},{4,6},{6,4},{8,10},{10,8},{12,14},{14,12},{16,18},{18,... | collective-permute-start | bytes 393224 | tf_op jit(solution)/shard_map/ppermute | solution.py:46
  23.6 5.3 %collective-permute-start.4 = (bf16[2,64,512]{2,1,0:T(8,128)(2,1)S(1)}, bf16[2,64,512]{2,1,0:T(8,128)(2,1)S(1)}, u32[]{:S(2)}, u32[]{:S(2)}) collective-permute-start(bf16[2,64,512]{2,1,0:T(8,128)(2,1)S(1)} %factor.9.refs_3_.refs_0_), channel_id=1, source_target_pairs={{0,4},{2,6},{4,0},{6,2},{8,12},{10,14},{12,8},{14,10},{16,20},{18,... | collective-permute-start | bytes 393224 | tf_op jit(solution)/shard_map/ppermute | solution.py:46
  25.6 8.7 %collective-permute-start.7 = (bf16[2,64,512]{2,1,0:T(8,128)(2,1)S(1)}, bf16[2,64,512]{2,1,0:T(8,128)(2,1)S(1)}, u32[]{:S(2)}, u32[]{:S(2)}) collective-permute-start(bf16[2,64,512]{2,1,0:T(8,128)(2,1)S(1)} %factor.10.refs_3_), channel_id=1, source_target_pairs={{0,8},{2,10},{4,12},{6,14},{8,0},{10,2},{12,4},{14,6},{16,24},{18,... | collective-permute-start | bytes 393224 | tf_op jit(solution)/shard_map/ppermute | solution.py:46
  26.4 13.6 %collective-permute-start.11 = (bf16[2,64,512]{2,1,0:T(8,128)(2,1)S(1)}, bf16[2,64,512]{2,1,0:T(8,128)(2,1)S(1)}, u32[]{:S(2)}, u32[]{:S(2)}) collective-permute-start(bf16[2,64,512]{2,1,0:T(8,128)(2,1)S(1)} %get-tuple-element.70.refs_2_.refs_0_), channel_id=1, source_target_pairs={{0,2},{2,0},{4,6},{6,4},{8,10},{10,8},{12,14},{14,12},{16,18},{18,... | collective-permute-start | bytes 393224 | tf_op jit(solution)/shard_map/ppermute | solution.py:46
  29.0 13.8 %collective-permute-start.10 = (bf16[2,64,512]{2,1,0:T(8,128)(2,1)S(1)}, bf16[2,64,512]{2,1,0:T(8,128)(2,1)S(1)}, u32[]{:S(2)}, u32[]{:S(2)}) collective-permute-start(bf16[2,64,512]{2,1,0:T(8,128)(2,1)S(1)} %factor.11.refs_3_.refs_0_), channel_id=1, source_target_pairs={{0,4},{2,6},{4,0},{6,2},{8,12},{10,14},{12,8},{14,10},{16,20},{18,... | collective-permute-start | bytes 393224 | tf_op jit(solution)/shard_map/ppermute | solution.py:46
  34.7 16.0 %copy-start = (bf16[2048,1024]{1,0:T(8,128)(2,1)S(1)}, bf16[2048,1024]{1,0:T(8,128)(2,1)}, u32[]{:S(2)}) copy-start(bf16[2048,1024]{1,0:T(8,128)(2,1)} %refs_3_.3) | copy-start | bytes 12582916
  34.8 11.7 %collective-permute-start.13 = (bf16[3,64,512]{2,1,0:T(8,128)(2,1)S(1)}, bf16[3,64,512]{2,1,0:T(8,128)(2,1)S(1)}, u32[]{:S(2)}, u32[]{:S(2)}) collective-permute-start(bf16[3,64,512]{2,1,0:T(8,128)(2,1)S(1)} %forward.1.refs_3_), channel_id=1, source_target_pairs={{0,8},{2,10},{4,12},{6,14},{8,0},{10,2},{12,4},{14,6},{16,24},{18,... | collective-permute-start | bytes 589832 | tf_op jit(solution)/shard_map/ppermute | solution.py:46
  37.3 8.9 %collective-permute-start.9 = (bf16[2,64,512]{2,1,0:T(8,128)(2,1)S(1)}, bf16[2,64,512]{2,1,0:T(8,128)(2,1)S(1)}, u32[]{:S(2)}, u32[]{:S(2)}) collective-permute-start(bf16[2,64,512]{2,1,0:T(8,128)(2,1)S(1)} %get-tuple-element.75.refs_1_), channel_id=1, source_target_pairs={{0,16},{2,18},{4,20},{6,22},{8,24},{10,26},{12,28},{14,30},{16,0},... | collective-permute-start | bytes 393224 | tf_op jit(solution)/shard_map/ppermute | solution.py:46
  40.3 5.9 %collective-permute-start.14 = (bf16[2,64,512]{2,1,0:T(8,128)(2,1)S(1)}, bf16[2,64,512]{2,1,0:T(8,128)(2,1)S(1)}, u32[]{:S(2)}, u32[]{:S(2)}) collective-permute-start(bf16[2,64,512]{2,1,0:T(8,128)(2,1)S(1)} %factor.13.refs_3_.refs_0_), channel_id=1, source_target_pairs={{0,4},{2,6},{4,0},{6,2},{8,12},{10,14},{12,8},{14,10},{16,20},{18,... | collective-permute-start | bytes 393224 | tf_op jit(solution)/shard_map/ppermute | solution.py:46
  43.1 5.0 %collective-permute-start.17 = (bf16[2,64,512]{2,1,0:T(8,128)(2,1)S(1)}, bf16[2,64,512]{2,1,0:T(8,128)(2,1)S(1)}, u32[]{:S(2)}, u32[]{:S(2)}) collective-permute-start(bf16[2,64,512]{2,1,0:T(8,128)(2,1)S(1)} %factor.14.refs_1_), channel_id=1, source_target_pairs={{0,8},{2,10},{4,12},{6,14},{8,0},{10,2},{12,4},{14,6},{16,24},{18,... | collective-permute-start | bytes 393224 | tf_op jit(solution)/shard_map/ppermute | solution.py:46
  48.1 4.0 %copy-start.1 = (bf16[1024,2048]{1,0:T(8,128)(2,1)S(1)}, bf16[1024,2048]{1,0:T(8,128)(2,1)}, u32[]{:S(2)}) copy-start(bf16[1024,2048]{1,0:T(8,128)(2,1)} %refs_5_.3) | copy-start | bytes 12582916
  48.5 2.3 %collective-permute-start.18 = (bf16[256,512]{1,0:T(8,128)(2,1)S(1)}, bf16[256,512]{1,0:T(8,128)(2,1)S(1)}, u32[]{:S(2)}, u32[]{:S(2)}) collective-permute-start(bf16[256,512]{1,0:T(8,128)(2,1)S(1)} %get-tuple-element.80.refs_0_), channel_id=1, source_target_pairs={{1,0},{0,1},{3,2},{2,3},{5,4},{4,5},{7,6},{6,7},{9,8},{8,9},{11,10... | collective-permute-start | bytes 786440 | tf_op jit(solution)/shard_map/ppermute | solution.py:51
  48.6 7.1 %collective-permute-start.19 = (bf16[256,512]{1,0:T(8,128)(2,1)S(1)}, bf16[256,512]{1,0:T(8,128)(2,1)S(1)}, u32[]{:S(2)}, u32[]{:S(2)}) collective-permute-start(bf16[256,512]{1,0:T(8,128)(2,1)S(1)} %get-tuple-element.81.refs_3_.refs_0_), channel_id=1, source_target_pairs={{1,0},{0,1},{3,2},{2,3},{5,4},{4,5},{7,6},{6,7},{9,8},{8,9},{11,10... | collective-permute-start | bytes 786440 | tf_op jit(solution)/shard_map/ppermute | solution.py:51
  49.1 3.0 %collective-permute-start.15 = (bf16[128,512]{1,0:T(8,128)(2,1)S(1)}, bf16[128,512]{1,0:T(8,128)(2,1)S(1)}, u32[]{:S(2)}, u32[]{:S(2)}) collective-permute-start(bf16[128,512]{1,0:T(8,128)(2,1)S(1)} %get-tuple-element.76.refs_0_.refs_1_), channel_id=1, source_target_pairs={{1,0},{0,1},{3,2},{2,3},{5,4},{4,5},{7,6},{6,7},{9,8},{8,9},{11,10... | collective-permute-start | bytes 393224 | tf_op jit(solution)/shard_map/ppermute | solution.py:51
  49.2 2.9 %collective-permute-start.16 = (bf16[128,512]{1,0:T(8,128)(2,1)S(1)}, bf16[128,512]{1,0:T(8,128)(2,1)S(1)}, u32[]{:S(2)}, u32[]{:S(2)}) collective-permute-start(bf16[128,512]{1,0:T(8,128)(2,1)S(1)} %get-tuple-element.77.refs_4_.refs_1_.refs_2_), channel_id=1, source_target_pairs={{1,0},{0,1},{3,2},{2,3},{5,4},{4,5},{7,6},{6,7},{9,8},{8,9},{11,10... | collective-permute-start | bytes 393224 | tf_op jit(solution)/shard_map/ppermute | solution.py:51
  49.6 8.6 %collective-permute-start.20 = (bf16[2,64,512]{2,1,0:T(8,128)(2,1)S(1)}, bf16[2,64,512]{2,1,0:T(8,128)(2,1)S(1)}, u32[]{:S(2)}, u32[]{:S(2)}) collective-permute-start(bf16[2,64,512]{2,1,0:T(8,128)(2,1)S(1)} %get-tuple-element.79.refs_4_), channel_id=1, source_target_pairs={{0,16},{2,18},{4,20},{6,22},{8,24},{10,26},{12,28},{14,30},{16,0},... | collective-permute-start | bytes 393224 | tf_op jit(solution)/shard_map/ppermute | solution.py:46
  55.1 4.1 %collective-permute-start.23 = (bf16[128,512]{1,0:T(8,128)(2,1)S(1)}, bf16[128,512]{1,0:T(8,128)(2,1)S(1)}, u32[]{:S(2)}, u32[]{:S(2)}) collective-permute-start(bf16[128,512]{1,0:T(8,128)(2,1)S(1)} %get-tuple-element.90), channel_id=1, source_target_pairs={{1,0},{0,1},{3,2},{2,3},{5,4},{4,5},{7,6},{6,7},{9,8},{8,9},{11,10... | collective-permute-start | bytes 393224 | tf_op jit(solution)/shard_map/ppermute | solution.py:51
  55.2 4.0 %collective-permute-start.24 = (bf16[128,512]{1,0:T(8,128)(2,1)S(1)}, bf16[128,512]{1,0:T(8,128)(2,1)S(1)}, u32[]{:S(2)}, u32[]{:S(2)}) collective-permute-start(bf16[128,512]{1,0:T(8,128)(2,1)S(1)} %get-tuple-element.83.refs_3_), channel_id=1, source_target_pairs={{1,0},{0,1},{3,2},{2,3},{5,4},{4,5},{7,6},{6,7},{9,8},{8,9},{11,10... | collective-permute-start | bytes 393224 | tf_op jit(solution)/shard_map/ppermute | solution.py:51
  58.6 4.9 %collective-permute-start.21 = (bf16[128,512]{1,0:T(8,128)(2,1)S(1)}, bf16[128,512]{1,0:T(8,128)(2,1)S(1)}, u32[]{:S(2)}, u32[]{:S(2)}) collective-permute-start(bf16[128,512]{1,0:T(8,128)(2,1)S(1)} %get-tuple-element.87.refs_0_.refs_1_), channel_id=1, source_target_pairs={{1,0},{0,1},{3,2},{2,3},{5,4},{4,5},{7,6},{6,7},{9,8},{8,9},{11,10... | collective-permute-start | bytes 393224 | tf_op jit(solution)/shard_map/ppermute | solution.py:51
  58.7 4.8 %collective-permute-start.22 = (bf16[128,512]{1,0:T(8,128)(2,1)S(1)}, bf16[128,512]{1,0:T(8,128)(2,1)S(1)}, u32[]{:S(2)}, u32[]{:S(2)}) collective-permute-start(bf16[128,512]{1,0:T(8,128)(2,1)S(1)} %get-tuple-element.88.refs_8_.refs_1_.refs_2_), channel_id=1, source_target_pairs={{1,0},{0,1},{3,2},{2,3},{5,4},{4,5},{7,6},{6,7},{9,8},{8,9},{11,10... | collective-permute-start | bytes 393224 | tf_op jit(solution)/shard_map/ppermute | solution.py:51
  59.8 7.3 %collective-permute-start.30 = (bf16[64,512]{1,0:T(8,128)(2,1)S(1)}, bf16[64,512]{1,0:T(8,128)(2,1)S(1)}, u32[]{:S(2)}, u32[]{:S(2)}) collective-permute-start(bf16[64,512]{1,0:T(8,128)(2,1)S(1)} %get-tuple-element.100), channel_id=1, source_target_pairs={{0,8},{2,10},{4,12},{6,14},{8,0},{10,2},{12,4},{14,6},{16,24},{18,... | collective-permute-start | bytes 196616 | tf_op jit(solution)/shard_map/ppermute | solution.py:46
  61.8 14.3 %collective-permute-start.25 = (bf16[256,512]{1,0:T(8,128)(2,1)S(1)}, bf16[256,512]{1,0:T(8,128)(2,1)S(1)}, u32[]{:S(2)}, u32[]{:S(2)}) collective-permute-start(bf16[256,512]{1,0:T(8,128)(2,1)S(1)} %get-tuple-element.86.refs_6_), channel_id=1, source_target_pairs={{1,0},{0,1},{3,2},{2,3},{5,4},{4,5},{7,6},{6,7},{9,8},{8,9},{11,10... | collective-permute-start | bytes 786440 | tf_op jit(solution)/shard_map/ppermute | solution.py:51
  61.8 6.8 %collective-permute-start.31 = (bf16[64,512]{1,0:T(8,128)(2,1)S(1)}, bf16[64,512]{1,0:T(8,128)(2,1)S(1)}, u32[]{:S(2)}, u32[]{:S(2)}) collective-permute-start(bf16[64,512]{1,0:T(8,128)(2,1)S(1)} %get-tuple-element.101), channel_id=1, source_target_pairs={{0,16},{2,18},{4,20},{6,22},{8,24},{10,26},{12,28},{14,30},{16,0},... | collective-permute-start | bytes 196616 | tf_op jit(solution)/shard_map/ppermute | solution.py:46
  63.5 6.6 %collective-permute-start.32 = (bf16[64,512]{1,0:T(8,128)(2,1)S(1)}, bf16[64,512]{1,0:T(8,128)(2,1)S(1)}, u32[]{:S(2)}, u32[]{:S(2)}) collective-permute-start(bf16[64,512]{1,0:T(8,128)(2,1)S(1)} %get-tuple-element.91.refs_6_), channel_id=1, source_target_pairs={{0,24},{2,26},{4,28},{6,30},{8,16},{10,18},{12,20},{14,22},{16,8},... | collective-permute-start | bytes 196616 | tf_op jit(solution)/shard_map/ppermute | solution.py:46
  66.7 3.8 %collective-permute-start.28 = (bf16[128,512]{1,0:T(8,128)(2,1)S(1)}, bf16[128,512]{1,0:T(8,128)(2,1)S(1)}, u32[]{:S(2)}, u32[]{:S(2)}) collective-permute-start(bf16[128,512]{1,0:T(8,128)(2,1)S(1)} %get-tuple-element.98), channel_id=1, source_target_pairs={{1,0},{0,1},{3,2},{2,3},{5,4},{4,5},{7,6},{6,7},{9,8},{8,9},{11,10... | collective-permute-start | bytes 393224 | tf_op jit(solution)/shard_map/ppermute | solution.py:51
  67.0 3.5 %collective-permute-start.29 = (bf16[128,512]{1,0:T(8,128)(2,1)S(1)}, bf16[128,512]{1,0:T(8,128)(2,1)S(1)}, u32[]{:S(2)}, u32[]{:S(2)}) collective-permute-start(bf16[128,512]{1,0:T(8,128)(2,1)S(1)} %get-tuple-element.93.refs_4_), channel_id=1, source_target_pairs={{1,0},{0,1},{3,2},{2,3},{5,4},{4,5},{7,6},{6,7},{9,8},{8,9},{11,10... | collective-permute-start | bytes 393224 | tf_op jit(solution)/shard_map/ppermute | solution.py:51
  68.6 5.7 %collective-permute-start.26 = (bf16[128,512]{1,0:T(8,128)(2,1)S(1)}, bf16[128,512]{1,0:T(8,128)(2,1)S(1)}, u32[]{:S(2)}, u32[]{:S(2)}) collective-permute-start(bf16[128,512]{1,0:T(8,128)(2,1)S(1)} %get-tuple-element.95), channel_id=1, source_target_pairs={{1,0},{0,1},{3,2},{2,3},{5,4},{4,5},{7,6},{6,7},{9,8},{8,9},{11,10... | collective-permute-start | bytes 393224 | tf_op jit(solution)/shard_map/ppermute | solution.py:51
  70.1 4.6 %collective-permute-start.27 = (bf16[128,512]{1,0:T(8,128)(2,1)S(1)}, bf16[128,512]{1,0:T(8,128)(2,1)S(1)}, u32[]{:S(2)}, u32[]{:S(2)}) collective-permute-start(bf16[128,512]{1,0:T(8,128)(2,1)S(1)} %get-tuple-element.96.refs_5_), channel_id=1, source_target_pairs={{1,0},{0,1},{3,2},{2,3},{5,4},{4,5},{7,6},{6,7},{9,8},{8,9},{11,10... | collective-permute-start | bytes 393224 | tf_op jit(solution)/shard_map/ppermute | solution.py:51
  71.1 5.0 %collective-permute-start.37 = (bf16[64,512]{1,0:T(8,128)(2,1)S(1)}, bf16[64,512]{1,0:T(8,128)(2,1)S(1)}, u32[]{:S(2)}, u32[]{:S(2)}) collective-permute-start(bf16[64,512]{1,0:T(8,128)(2,1)S(1)} %get-tuple-element.110), channel_id=1, source_target_pairs={{0,8},{2,10},{4,12},{6,14},{8,0},{10,2},{12,4},{14,6},{16,24},{18,... | collective-permute-start | bytes 196616 | tf_op jit(solution)/shard_map/ppermute | solution.py:46
  72.8 6.0 %collective-permute-start.38 = (bf16[64,512]{1,0:T(8,128)(2,1)S(1)}, bf16[64,512]{1,0:T(8,128)(2,1)S(1)}, u32[]{:S(2)}, u32[]{:S(2)}) collective-permute-start(bf16[64,512]{1,0:T(8,128)(2,1)S(1)} %get-tuple-element.111), channel_id=1, source_target_pairs={{0,16},{2,18},{4,20},{6,22},{8,24},{10,26},{12,28},{14,30},{16,0},... | collective-permute-start | bytes 196616 | tf_op jit(solution)/shard_map/ppermute | solution.py:46
  74.3 6.8 %collective-permute-start.39 = (bf16[64,512]{1,0:T(8,128)(2,1)S(1)}, bf16[64,512]{1,0:T(8,128)(2,1)S(1)}, u32[]{:S(2)}, u32[]{:S(2)}) collective-permute-start(bf16[64,512]{1,0:T(8,128)(2,1)S(1)} %get-tuple-element.103.refs_5_), channel_id=1, source_target_pairs={{0,24},{2,26},{4,28},{6,30},{8,16},{10,18},{12,20},{14,22},{16,8},... | collective-permute-start | bytes 196616 | tf_op jit(solution)/shard_map/ppermute | solution.py:46
  74.7 8.2 %collective-permute-start.36 = (bf16[4,64,512]{2,1,0:T(8,128)(2,1)S(1)}, bf16[4,64,512]{2,1,0:T(8,128)(2,1)S(1)}, u32[]{:S(2)}, u32[]{:S(2)}) collective-permute-start(bf16[4,64,512]{2,1,0:T(8,128)(2,1)S(1)} %get-tuple-element.102.refs_8_), channel_id=1, source_target_pairs={{0,4},{2,6},{4,0},{6,2},{8,12},{10,14},{12,8},{14,10},{16,20},{18,... | collective-permute-start | bytes 786440 | tf_op jit(solution)/shard_map/ppermute | solution.py:46
  81.5 8.0 %collective-permute-start.41 = (bf16[4,64,512]{2,1,0:T(8,128)(2,1)S(1)}, bf16[4,64,512]{2,1,0:T(8,128)(2,1)S(1)}, u32[]{:S(2)}, u32[]{:S(2)}) collective-permute-start(bf16[4,64,512]{2,1,0:T(8,128)(2,1)S(1)} %get-tuple-element.112.refs_3_), channel_id=1, source_target_pairs={{0,4},{2,6},{4,0},{6,2},{8,12},{10,14},{12,8},{14,10},{16,20},{18,... | collective-permute-start | bytes 786440 | tf_op jit(solution)/shard_map/ppermute | solution.py:46
  83.2 11.4 %collective-permute-start.40 = (bf16[4,64,512]{2,1,0:T(8,128)(2,1)S(1)}, bf16[4,64,512]{2,1,0:T(8,128)(2,1)S(1)}, u32[]{:S(2)}, u32[]{:S(2)}) collective-permute-start(bf16[4,64,512]{2,1,0:T(8,128)(2,1)S(1)} %get-tuple-element.114.refs_3_), channel_id=1, source_target_pairs={{0,2},{2,0},{4,6},{6,4},{8,10},{10,8},{12,14},{14,12},{16,18},{18,... | collective-permute-start | bytes 786440 | tf_op jit(solution)/shard_map/ppermute | solution.py:46
  89.8 7.1 %collective-permute-start.42 = (bf16[4,64,512]{2,1,0:T(8,128)(2,1)S(1)}, bf16[4,64,512]{2,1,0:T(8,128)(2,1)S(1)}, u32[]{:S(2)}, u32[]{:S(2)}) collective-permute-start(bf16[4,64,512]{2,1,0:T(8,128)(2,1)S(1)} %get-tuple-element.116.refs_3_), channel_id=1, source_target_pairs={{0,2},{2,0},{4,6},{6,4},{8,10},{10,8},{12,14},{14,12},{16,18},{18,... | collective-permute-start | bytes 786440 | tf_op jit(solution)/shard_map/ppermute | solution.py:46
  91.1 15.8 %collective-permute-start.33 = (bf16[2,64,512]{2,1,0:T(8,128)(2,1)S(1)}, bf16[2,64,512]{2,1,0:T(8,128)(2,1)S(1)}, u32[]{:S(2)}, u32[]{:S(2)}) collective-permute-start(bf16[2,64,512]{2,1,0:T(8,128)(2,1)S(1)} %get-tuple-element.105), channel_id=1, source_target_pairs={{0,8},{2,10},{4,12},{6,14},{8,0},{10,2},{12,4},{14,6},{16,24},{18,... | collective-permute-start | bytes 393224 | tf_op jit(solution)/shard_map/ppermute | solution.py:46
  91.9 14.9 %collective-permute-start.34 = (bf16[2,64,512]{2,1,0:T(8,128)(2,1)S(1)}, bf16[2,64,512]{2,1,0:T(8,128)(2,1)S(1)}, u32[]{:S(2)}, u32[]{:S(2)}) collective-permute-start(bf16[2,64,512]{2,1,0:T(8,128)(2,1)S(1)} %get-tuple-element.106), channel_id=1, source_target_pairs={{0,16},{2,18},{4,20},{6,22},{8,24},{10,26},{12,28},{14,30},{16,0},... | collective-permute-start | bytes 393224 | tf_op jit(solution)/shard_map/ppermute | solution.py:46
  94.1 12.8 %collective-permute-start.35 = (bf16[2,64,512]{2,1,0:T(8,128)(2,1)S(1)}, bf16[2,64,512]{2,1,0:T(8,128)(2,1)S(1)}, u32[]{:S(2)}, u32[]{:S(2)}) collective-permute-start(bf16[2,64,512]{2,1,0:T(8,128)(2,1)S(1)} %get-tuple-element.107.refs_5_), channel_id=1, source_target_pairs={{0,24},{2,26},{4,28},{6,30},{8,16},{10,18},{12,20},{14,22},{16,8},... | collective-permute-start | bytes 393224 | tf_op jit(solution)/shard_map/ppermute | solution.py:46
  98.4 7.3 %collective-permute-start.43 = (bf16[2,512]{1,0:T(2,128)(2,1)S(1)}, bf16[2,512]{1,0:T(2,128)(2,1)S(1)}, u32[]{:S(2)}, u32[]{:S(2)}) collective-permute-start(bf16[2,512]{1,0:T(2,128)(2,1)S(1)} %get-tuple-element.123.refs_4_), channel_id=1, source_target_pairs={{2,4},{4,2},{6,8},{8,6},{10,12},{12,10},{14,16},{16,14},{18,20},{2... | collective-permute-start | bytes 6152 | tf_op jit(solution)/shard_map/ppermute | solution.py:41
  101.5 4.2 %collective-permute-start.44 = (bf16[2,512]{1,0:T(2,128)(2,1)S(1)}, bf16[2,512]{1,0:T(2,128)(2,1)S(1)}, u32[]{:S(2)}, u32[]{:S(2)}) collective-permute-start(bf16[2,512]{1,0:T(2,128)(2,1)S(1)} %get-tuple-element.123.refs_4_), channel_id=1, source_target_pairs={{0,2},{2,0},{4,6},{6,4},{8,10},{10,8},{12,14},{14,12},{16,18},{18,... | collective-permute-start | bytes 6152 | tf_op jit(solution)/shard_map/ppermute | solution.py:37

commit v3 on v2

--- a/solution.py
+++ b/solution.py
@@ -140,10 +140,11 @@
     return message.at[pieces + number // across, :, lanes]
 
 
-def load_kernel(mixing_far, cells_far, pattern_far, mixing, cells, pattern, arrivals):
-    pairs = ((mixing_far, mixing), (cells_far, cells), (pattern_far, pattern))
+def load_kernel(count, *rest):
+    fars, nears, arrivals = rest[:count], rest[count : 2 * count], rest[2 * count]
     fetches = [
-        pltpu.make_async_copy(far, near, arrivals.at[i]) for i, (far, near) in enumerate(pairs)
+        pltpu.make_async_copy(far, near, arrivals.at[i])
+        for i, (far, near) in enumerate(zip(fars, nears))
     ]
     for fetch in fetches:
         fetch.start()
@@ -439,14 +440,22 @@
     per_block = chan_count // (2 * BLOCK)
     lengths = [pieces + -(-pieces * 2 * (1 + (flip == 1)) // per_block) for flip in (1, 2, 3)]
     length = lengths[1]
-    mixing, cells, pattern = run(
-        load_kernel,
+    distant = [cotangent.reshape(blocks, BLOCK, chan_count), mixing, inputs, pattern]
+    cots, mixing, cells, pattern = run(
+        functools.partial(load_kernel, len(distant)),
         "load",
-        [(array.shape, array.dtype) for array in (mixing, inputs, pattern)],
+        [(array.shape, array.dtype) for array in distant],
         [],
-        [mixing, inputs, pattern],
-        [pltpu.SemaphoreType.DMA((3,))],
+        distant,
+        [pltpu.SemaphoreType.DMA((len(distant),))],
         limit=ALL,
+    )
+    latest += [far, near]
+    own_cots, soon_message, across = run(
+        functools.partial(pack_kernel, last, pieces, length),
+        "pack",
+        [blocks_of(pieces), blocks_of(lengths[0]), blocks_of(2 * length)],
+        [cots, mixing],
     )
     units = [(s,) for s in range(2 * pieces)]
     convolved, *states = run(
@@ -458,13 +467,7 @@
         [pltpu.VMEM((blocks, BLOCK, chan_count), jnp.bfloat16)] * 2
         + [pltpu.SMEM(pattern.shape, jnp.int32), pltpu.SemaphoreType.DMA],
     )
-    own_cots, *messages = run(
-        functools.partial(pack_kernel, last, pieces, length),
-        "pack",
-        [((pieces, BLOCK, chan_count), jnp.bfloat16)]
-        + [blocks_of(lengths[0]), blocks_of(2 * length)],
-        [cotangent.reshape(blocks, BLOCK, chan_count), mixing],
-    )
+    messages = [soon_message, across]
     messages = [from_flipped(m, "seq", mask) for m, mask in zip(messages, masks[1:])]
 
     def forward():
@@ -617,8 +620,8 @@
         if plain[-i] == plain[-1] and u == len(units) - 2:
             arrive(0)
         if plain[-i] == plain[-1] and u == 1:
+            forward()
             early_factor(0)
-            forward()
     late_factor(0)
     for p in range(1, pieces):
         early_factor(p)

time: 108 us -> 109 us (level)
  transfers between devices with their start and end apart: 45 -> 45, of which waited for: 14 -> 15; matrix products, arithmetic and copies ran while one was open for 0% -> 0% of each run, Pallas kernels for 19% -> 21%
where the time goes in v3:
time: 109 us; the launch traced here: 108 us
  starting transfers between devices  48.9 us (45%)
  waiting for transfers between devices  29.5 us (27%)
  Pallas kernels  23.6 us (22%)
  local copies, waits for them, and re-layouts  4.62 us (4%)
    ppermute x28, starting transfers between devices, from_flipped(): return lax.ppermute(block, axis, [(i, i ^ mask) for i in range(count)])  36.8 us
    ppermute x28, waiting for transfers between devices, from_flipped(): return lax.ppermute(block, axis, [(i, i ^ mask) for i in range(count)])  26.5 us
    pallas_call x36, Pallas kernels, call(): pl.pallas_call(body, out_shape=[jax.ShapeDtypeStruct(shape, kind) for sha...  23.6 us
    ppermute x2, starting transfers between devices, neighbours(): return (near, lax.ppermute(edges, axis, route))  5.99 us
    unnamed x12, local copies, waits for them, and re-layouts  3.9 us
    ppermute x2, starting transfers between devices, neighbours(): near = lax.ppermute(edges, axis, [(i, i ^ 1) for i in range(count)])  3.12 us
    ppermute x13, starting transfers between devices, from_offset(): lax.ppermute(block, axis, [((i + offset) % count, i) for i in range(count)])  3 us
    ppermute x2, waiting for transfers between devices, neighbours(): return (near, lax.ppermute(edges, axis, route))  2.99 us
  transfers between devices with their start and end apart: 45, of which 15 were waited for; matrix products, arithmetic and copies ran while one was open for 0% of the time, Pallas kernels for 21%

profile of v3, /device:TPU:8, one launch (start us, length us, event | category | flops | bytes accessed | tf_op | source)
XLA Modules:
  0.0 108.4 jit_solution(11477556342438375199)
XLA Ops:
  0.6 0.7 fusion
  1.4 0.7 pad_maximum_fusion
  2.1 1.6 %collective-permute-start.1 = (bf16[5,512]{1,0:T(8,128)(2,1)S(1)}, bf16[5,512]{1,0:T(8,128)(2,1)S(1)}, u32[]{:S(2)}, u32[]{:S(2)}) collective-permute-start(bf16[5,512]{1,0:T(8,128)(2,1)S(1)} %pad_maximum_fusion), channel_id=1, source_target_pairs={{0,2},{2,0},{4,6},{6,4},{8,10},{10,8},{12,14},{14,12},{16,18},{18,... | collective-permute-start | bytes 15368 | tf_op jit(solution)/shard_map/ppermute | solution.py:37
  3.6 3.3 %collective-permute-start = (bf16[5,512]{1,0:T(8,128)(2,1)S(1)}, bf16[5,512]{1,0:T(8,128)(2,1)S(1)}, u32[]{:S(2)}, u32[]{:S(2)}) collective-permute-start(bf16[5,512]{1,0:T(8,128)(2,1)S(1)} %pad_maximum_fusion), channel_id=1, source_target_pairs={{2,4},{4,2},{6,8},{8,6},{10,12},{12,10},{14,16},{16,14},{18,20},{2... | collective-permute-start | bytes 15368 | tf_op jit(solution)/shard_map/ppermute | solution.py:41
  6.9 1.1 %copy-done.2 = bf16[6,8,64,128]{3,2,1,0:T(8,128)(2,1)S(1)} copy-done((bf16[6,8,64,128]{3,2,1,0:T(8,128)(2,1)S(1)}, bf16[6,8,64,128]{3,2,1,0:T(8,128)(2,1)}, u32[]{:S(2)}) %copy-start.2) | copy-done | bytes 786456
  8.0 1.0 copy-done.3
  9.1 1.0 copy-done.4
  10.1 0.7 copy-done.5
  11.1 2.7 %collective-permute-start.9 = (bf16[6,64,512]{2,1,0:T(8,128)(2,1)S(1)}, bf16[6,64,512]{2,1,0:T(8,128)(2,1)S(1)}, u32[]{:S(2)}, u32[]{:S(2)}) collective-permute-start(bf16[6,64,512]{2,1,0:T(8,128)(2,1)S(1)} %get-tuple-element.70.refs_5_), channel_id=1, source_target_pairs={{0,16},{2,18},{4,20},{6,22},{8,24},{10,26},{12,28},{14,30},{16,0},... | collective-permute-start | bytes 1179656 | tf_op jit(solution)/shard_map/ppermute | solution.py:46
  13.7 2.1 %conv_and_local_factors.1 = (bf16[512,512]{1,0:T(8,128)(2,1)}, bf16[2,64,512]{2,1,0:T(8,128)(2,1)S(1)}, bf16[2,64,512]{2,1,0:T(8,128)(2,1)S(1)}, bf16[2,64,512]{2,1,0:T(8,128)(2,1)S(1)}, bf16[2,64,512]{2,1,0:T(8,128)(2,1)S(1)}) custom-call(s32[2,8]{1,0:T(2,128)S(1)} %get-tuple-element.66.refs_2_.refs_0_, bf16[512,512]{1,0:T(8,128)(2,1)S(1)} %get-tuple-element.67.refs_1_, ...), custom_call_target="tpu_custom_call" | custom-call | tf_op jit(solution)/shard_map/conv_and_local_factors/pallas_call | solution.py:60
  15.8 1.7 %collective-permute-start.3 = (bf16[2,64,512]{2,1,0:T(8,128)(2,1)S(1)}, bf16[2,64,512]{2,1,0:T(8,128)(2,1)S(1)}, u32[]{:S(2)}, u32[]{:S(2)}) collective-permute-start(bf16[2,64,512]{2,1,0:T(8,128)(2,1)S(1)} %get-tuple-element.72.refs_0_), channel_id=1, source_target_pairs={{0,2},{2,0},{4,6},{6,4},{8,10},{10,8},{12,14},{14,12},{16,18},{18,... | collective-permute-start | bytes 393224 | tf_op jit(solution)/shard_map/ppermute | solution.py:46
  17.9 3.8 %collective-permute-done.3.refs_1_ = bf16[2,64,512]{2,1,0:T(8,128)(2,1)S(1)} collective-permute-done((bf16[2,64,512]{2,1,0:T(8,128)(2,1)S(1)}, bf16[2,64,512]{2,1,0:T(8,128)(2,1)S(1)}, u32[]{:S(2)}, u32[]{:S(2)}) %collective-permute-start.3) | collective-permute-done | bytes 131104 | tf_op jit(solution)/shard_map/ppermute | solution.py:46
  22.0 0.7 collective-permute-start.6
  22.7 1.3 %collective-permute-start.8 = (bf16[4,64,512]{2,1,0:T(8,128)(2,1)S(1)}, bf16[4,64,512]{2,1,0:T(8,128)(2,1)S(1)}, u32[]{:S(2)}, u32[]{:S(2)}) collective-permute-start(bf16[4,64,512]{2,1,0:T(8,128)(2,1)S(1)} %get-tuple-element.75), channel_id=1, source_target_pairs={{0,8},{2,10},{4,12},{6,14},{8,0},{10,2},{12,4},{14,6},{16,24},{18,... | collective-permute-start | bytes 786440 | tf_op jit(solution)/shard_map/ppermute | solution.py:46
  24.0 1.7 %collective-permute-start.5 = (bf16[2,64,512]{2,1,0:T(8,128)(2,1)S(1)}, bf16[2,64,512]{2,1,0:T(8,128)(2,1)S(1)}, u32[]{:S(2)}, u32[]{:S(2)}) collective-permute-start(bf16[2,64,512]{2,1,0:T(8,128)(2,1)S(1)} %get-tuple-element.74.refs_0_), channel_id=1, source_target_pairs={{0,2},{2,0},{4,6},{6,4},{8,10},{10,8},{12,14},{14,12},{16,18},{18,... | collective-permute-start | bytes 393224 | tf_op jit(solution)/shard_map/ppermute | solution.py:46
  25.9 0.6 collective-permute-start.4
  26.5 1.1 collective-permute-done.6.refs_1_
  27.8 0.8 collective-permute-start.7
  28.6 1.1 %collective-permute-done.5.refs_1_ = bf16[2,64,512]{2,1,0:T(8,128)(2,1)S(1)} collective-permute-done((bf16[2,64,512]{2,1,0:T(8,128)(2,1)S(1)}, bf16[2,64,512]{2,1,0:T(8,128)(2,1)S(1)}, u32[]{:S(2)}, u32[]{:S(2)}) %collective-permute-start.5) | collective-permute-done | bytes 131104 | tf_op jit(solution)/shard_map/ppermute | solution.py:46
  29.7 1.6 %collective-permute-start.12 = (bf16[2,64,512]{2,1,0:T(8,128)(2,1)S(1)}, bf16[2,64,512]{2,1,0:T(8,128)(2,1)S(1)}, u32[]{:S(2)}, u32[]{:S(2)}) collective-permute-start(bf16[2,64,512]{2,1,0:T(8,128)(2,1)S(1)} %get-tuple-element.73.refs_3_.refs_0_), channel_id=1, source_target_pairs={{0,2},{2,0},{4,6},{6,4},{8,10},{10,8},{12,14},{14,12},{16,18},{18,... | collective-permute-start | bytes 393224 | tf_op jit(solution)/shard_map/ppermute | solution.py:46
  31.6 0.6 collective-permute-done.4.refs_1_
  32.2 0.6 collective-permute-start.11
  33.2 1.5 %collective-permute-start.13 = (bf16[3,64,512]{2,1,0:T(8,128)(2,1)S(1)}, bf16[3,64,512]{2,1,0:T(8,128)(2,1)S(1)}, u32[]{:S(2)}, u32[]{:S(2)}) collective-permute-start(bf16[3,64,512]{2,1,0:T(8,128)(2,1)S(1)} %forward.1.refs_4_), channel_id=1, source_target_pairs={{0,8},{2,10},{4,12},{6,14},{8,0},{10,2},{12,4},{14,6},{16,24},{18,... | collective-permute-start | bytes 589832 | tf_op jit(solution)/shard_map/ppermute | solution.py:46
  34.7 2.6 %collective-permute-done.7.refs_1_ = bf16[2,64,512]{2,1,0:T(8,128)(2,1)S(1)} collective-permute-done((bf16[2,64,512]{2,1,0:T(8,128)(2,1)S(1)}, bf16[2,64,512]{2,1,0:T(8,128)(2,1)S(1)}, u32[]{:S(2)}, u32[]{:S(2)}) %collective-permute-start.7) | collective-permute-done | bytes 131104 | tf_op jit(solution)/shard_map/ppermute | solution.py:46
  37.6 4.6 %collective-permute-start.10 = (bf16[2,64,512]{2,1,0:T(8,128)(2,1)S(1)}, bf16[2,64,512]{2,1,0:T(8,128)(2,1)S(1)}, u32[]{:S(2)}, u32[]{:S(2)}) collective-permute-start(bf16[2,64,512]{2,1,0:T(8,128)(2,1)S(1)} %get-tuple-element.77.refs_3_), channel_id=1, source_target_pairs={{0,16},{2,18},{4,20},{6,22},{8,24},{10,26},{12,28},{14,30},{16,0},... | collective-permute-start | bytes 393224 | tf_op jit(solution)/shard_map/ppermute | solution.py:46
  42.5 0.7 collective-permute-start.14
  43.6 2.4 %collective-permute-done.10.refs_0_ = bf16[2,64,512]{2,1,0:T(8,128)(2,1)S(1)} collective-permute-done((bf16[2,64,512]{2,1,0:T(8,128)(2,1)S(1)}, bf16[2,64,512]{2,1,0:T(8,128)(2,1)S(1)}, u32[]{:S(2)}, u32[]{:S(2)}) %collective-permute-start.10) | collective-permute-done | bytes 131104 | tf_op jit(solution)/shard_map/ppermute | solution.py:46
  46.0 1.6 %collective-permute-done.14.refs_1_ = bf16[2,64,512]{2,1,0:T(8,128)(2,1)S(1)} collective-permute-done((bf16[2,64,512]{2,1,0:T(8,128)(2,1)S(1)}, bf16[2,64,512]{2,1,0:T(8,128)(2,1)S(1)}, u32[]{:S(2)}, u32[]{:S(2)}) %collective-permute-start.14) | collective-permute-done | bytes 131104 | tf_op jit(solution)/shard_map/ppermute | solution.py:46
  49.0 0.5 collective-permute-start.19
  50.0 1.4 %collective-permute-start.20 = (bf16[2,64,512]{2,1,0:T(8,128)(2,1)S(1)}, bf16[2,64,512]{2,1,0:T(8,128)(2,1)S(1)}, u32[]{:S(2)}, u32[]{:S(2)}) collective-permute-start(bf16[2,64,512]{2,1,0:T(8,128)(2,1)S(1)} %get-tuple-element.81.refs_4_), channel_id=1, source_target_pairs={{0,16},{2,18},{4,20},{6,22},{8,24},{10,26},{12,28},{14,30},{16,0},... | collective-permute-start | bytes 393224 | tf_op jit(solution)/shard_map/ppermute | solution.py:46
  51.4 1.3 %grad_act.2.refs_4_.refs_6_ = bf16[256,2048]{1,0:T(8,128)(2,1)S(1)} custom-call(bf16[256,512]{1,0:T(8,128)(2,1)S(1)} %get-tuple-element.82.refs_0_, bf16[256,512]{1,0:T(8,128)(2,1)S(1)} %collective-permute-done.18.refs_1_, bf16[2048,1024]{1,0:T(8,128)(2,1)S(1)} %copy-done, bf16[256,512]{1,0:T(8,128)(2,1)S(1)} %get-tuple-element.83.refs_3_.refs_0_), custom_call_target="tpu_custom_call" | custom-call | tf_op jit(solution)/shard_map/grad_act/pallas_call | solution.py:60
  52.7 3.0 %mlp_hidden_and_grad.2 = (bf16[256,2048]{1,0:T(8,128)(2,1)S(1)}, f32[256,512]{1,0:T(8,128)S(1)}, bf16[128,512]{1,0:T(8,128)(2,1)S(1)}, bf16[128,512]{1,0:T(8,128)(2,1)S(1)}) custom-call(bf16[128,512]{1,0:T(8,128)(2,1)S(1)} %get-tuple-element.78.refs_0_.refs_1_, bf16[128,512]{1,0:T(8,128)(2,1)S(1)} %get-tuple-element.79.refs_4_.refs_1_.refs_2_, ...), custom_call_target="tpu_custom_call" | custom-call | tf_op jit(solution)/shard_map/mlp_hidden_and_grad/pallas_call | solution.py:60
  55.8 0.5 collective-permute-start.24
  56.3 1.3 %grad_act.3.refs_4_ = bf16[256,2048]{1,0:T(8,128)(2,1)S(1)} custom-call(bf16[256,512]{1,0:T(8,128)(2,1)S(1)} %get-tuple-element.83.refs_3_.refs_0_, bf16[256,512]{1,0:T(8,128)(2,1)S(1)} %collective-permute-done.19.refs_1_, bf16[2048,1024]{1,0:T(8,128)(2,1)S(1)} %copy-done, bf16[128,512]{1,0:T(8,128)(2,1)S(1)} %get-tuple-element.85.refs_3_), custom_call_target="tpu_custom_call" | custom-call | tf_op jit(solution)/shard_map/grad_act/pallas_call | solution.py:60
  57.6 1.3 %mlp_out.2 = (f32[256,512]{1,0:T(8,128)S(1)}, bf16[256,512]{1,0:T(8,128)(2,1)S(1)}) custom-call(bf16[256,2048]{1,0:T(8,128)(2,1)S(1)} %get-tuple-element.84.refs_0_, bf16[128,512]{1,0:T(8,128)(2,1)S(1)} %get-tuple-element.78.refs_0_.refs_1_, bf16[128,512]{1,0:T(8,128)(2,1)S(1)} %get-tuple-element.79.refs_4_.refs_1_.refs_2_, bf16[2048,1024]{1,0:T(8,128)(2,1)S(1)} %copy-done, ...), custom_call_target="tpu_custom_call" | custom-call | tf_op jit(solution)/shard_map/mlp_out/pallas_call | solution.py:60
  59.4 0.4 collective-permute-start.22
  59.8 0.6 late_and_early_back.2
  60.4 0.6 collective-permute-start.30
  61.0 1.2 %collective-permute-start.31 = (bf16[64,512]{1,0:T(8,128)(2,1)S(1)}, bf16[64,512]{1,0:T(8,128)(2,1)S(1)}, u32[]{:S(2)}, u32[]{:S(2)}) collective-permute-start(bf16[64,512]{1,0:T(8,128)(2,1)S(1)} %get-tuple-element.103), channel_id=1, source_target_pairs={{0,16},{2,18},{4,20},{6,22},{8,24},{10,26},{12,28},{14,30},{16,0},... | collective-permute-start | bytes 196616 | tf_op jit(solution)/shard_map/ppermute | solution.py:46
  62.2 1.7 %collective-permute-start.32 = (bf16[64,512]{1,0:T(8,128)(2,1)S(1)}, bf16[64,512]{1,0:T(8,128)(2,1)S(1)}, u32[]{:S(2)}, u32[]{:S(2)}) collective-permute-start(bf16[64,512]{1,0:T(8,128)(2,1)S(1)} %get-tuple-element.93.refs_6_), channel_id=1, source_target_pairs={{0,24},{2,26},{4,28},{6,30},{8,16},{10,18},{12,20},{14,22},{16,8},... | collective-permute-start | bytes 196616 | tf_op jit(solution)/shard_map/ppermute | solution.py:46
  63.9 3.2 %mlp_hidden_and_grad.3 = (bf16[256,2048]{1,0:T(8,128)(2,1)S(1)}, f32[256,512]{1,0:T(8,128)S(1)}, bf16[128,512]{1,0:T(8,128)(2,1)S(1)}, bf16[128,512]{1,0:T(8,128)(2,1)S(1)}) custom-call(bf16[128,512]{1,0:T(8,128)(2,1)S(1)} %get-tuple-element.89.refs_0_.refs_1_, bf16[128,512]{1,0:T(8,128)(2,1)S(1)} %get-tuple-element.90.refs_8_.refs_1_.refs_2_, ...), custom_call_target="tpu_custom_call" | custom-call | tf_op jit(solution)/shard_map/mlp_hidden_and_grad/pallas_call | solution.py:60
  67.2 0.5 collective-permute-start.29
  67.7 1.3 %mlp_out.3 = (f32[256,512]{1,0:T(8,128)S(1)}, bf16[128,512]{1,0:T(8,128)(2,1)S(1)}, bf16[128,512]{1,0:T(8,128)(2,1)S(1)}) custom-call(bf16[256,2048]{1,0:T(8,128)(2,1)S(1)} %get-tuple-element.94.refs_0_, bf16[128,512]{1,0:T(8,128)(2,1)S(1)} %get-tuple-element.89.refs_0_.refs_1_, bf16[128,512]{1,0:T(8,128)(2,1)S(1)} %get-tuple-element.90.refs_8_.refs_1_.refs_2_, ...), custom_call_target="tpu_custom_call" | custom-call | tf_op jit(solution)/shard_map/mlp_out/pallas_call | solution.py:60
  69.1 1.5 %collective-permute-done.32.refs_3_ = bf16[64,512]{1,0:T(8,128)(2,1)S(1)} collective-permute-done((bf16[64,512]{1,0:T(8,128)(2,1)S(1)}, bf16[64,512]{1,0:T(8,128)(2,1)S(1)}, u32[]{:S(2)}, u32[]{:S(2)}) %collective-permute-start.32) | collective-permute-done | bytes 65568 | tf_op jit(solution)/shard_map/ppermute | solution.py:46
  71.0 0.6 late_and_early_back.3
  71.6 0.6 collective-permute-start.37
  72.2 1.2 %collective-permute-start.38 = (bf16[64,512]{1,0:T(8,128)(2,1)S(1)}, bf16[64,512]{1,0:T(8,128)(2,1)S(1)}, u32[]{:S(2)}, u32[]{:S(2)}) collective-permute-start(bf16[64,512]{1,0:T(8,128)(2,1)S(1)} %get-tuple-element.113), channel_id=1, source_target_pairs={{0,16},{2,18},{4,20},{6,22},{8,24},{10,26},{12,28},{14,30},{16,0},... | collective-permute-start | bytes 196616 | tf_op jit(solution)/shard_map/ppermute | solution.py:46
  73.5 1.7 %collective-permute-start.39 = (bf16[64,512]{1,0:T(8,128)(2,1)S(1)}, bf16[64,512]{1,0:T(8,128)(2,1)S(1)}, u32[]{:S(2)}, u32[]{:S(2)}) collective-permute-start(bf16[64,512]{1,0:T(8,128)(2,1)S(1)} %get-tuple-element.105.refs_5_), channel_id=1, source_target_pairs={{0,24},{2,26},{4,28},{6,30},{8,16},{10,18},{12,20},{14,22},{16,8},... | collective-permute-start | bytes 196616 | tf_op jit(solution)/shard_map/ppermute | solution.py:46
  75.2 1.1 collective-permute-start.36
  76.6 1.7 %collective-permute-done.38.refs_2_ = bf16[64,512]{1,0:T(8,128)(2,1)S(1)} collective-permute-done((bf16[64,512]{1,0:T(8,128)(2,1)S(1)}, bf16[64,512]{1,0:T(8,128)(2,1)S(1)}, u32[]{:S(2)}, u32[]{:S(2)}) %collective-permute-start.38) | collective-permute-done | bytes 65568 | tf_op jit(solution)/shard_map/ppermute | solution.py:46
  78.3 3.1 %collective-permute-done.39.refs_3_ = bf16[64,512]{1,0:T(8,128)(2,1)S(1)} collective-permute-done((bf16[64,512]{1,0:T(8,128)(2,1)S(1)}, bf16[64,512]{1,0:T(8,128)(2,1)S(1)}, u32[]{:S(2)}, u32[]{:S(2)}) %collective-permute-start.39) | collective-permute-done | bytes 65568 | tf_op jit(solution)/shard_map/ppermute | solution.py:46
  81.7 1.2 %collective-permute-start.41 = (bf16[4,64,512]{2,1,0:T(8,128)(2,1)S(1)}, bf16[4,64,512]{2,1,0:T(8,128)(2,1)S(1)}, u32[]{:S(2)}, u32[]{:S(2)}) collective-permute-start(bf16[4,64,512]{2,1,0:T(8,128)(2,1)S(1)} %get-tuple-element.114.refs_3_), channel_id=1, source_target_pairs={{0,4},{2,6},{4,0},{6,2},{8,12},{10,14},{12,8},{14,10},{16,20},{18,... | collective-permute-start | bytes 786440 | tf_op jit(solution)/shard_map/ppermute | solution.py:46
  83.3 1.8 %collective-permute-start.40 = (bf16[4,64,512]{2,1,0:T(8,128)(2,1)S(1)}, bf16[4,64,512]{2,1,0:T(8,128)(2,1)S(1)}, u32[]{:S(2)}, u32[]{:S(2)}) collective-permute-start(bf16[4,64,512]{2,1,0:T(8,128)(2,1)S(1)} %get-tuple-element.116.refs_3_), channel_id=1, source_target_pairs={{0,2},{2,0},{4,6},{6,4},{8,10},{10,8},{12,14},{14,12},{16,18},{18,... | collective-permute-start | bytes 786440 | tf_op jit(solution)/shard_map/ppermute | solution.py:46
  85.2 4.7 %collective-permute-done.41.refs_1_ = bf16[4,64,512]{2,1,0:T(8,128)(2,1)S(1)} collective-permute-done((bf16[4,64,512]{2,1,0:T(8,128)(2,1)S(1)}, bf16[4,64,512]{2,1,0:T(8,128)(2,1)S(1)}, u32[]{:S(2)}, u32[]{:S(2)}) %collective-permute-start.41) | collective-permute-done | bytes 262176 | tf_op jit(solution)/shard_map/ppermute | solution.py:46
  90.2 1.8 %collective-permute-start.42 = (bf16[4,64,512]{2,1,0:T(8,128)(2,1)S(1)}, bf16[4,64,512]{2,1,0:T(8,128)(2,1)S(1)}, u32[]{:S(2)}, u32[]{:S(2)}) collective-permute-start(bf16[4,64,512]{2,1,0:T(8,128)(2,1)S(1)} %get-tuple-element.118.refs_3_), channel_id=1, source_target_pairs={{0,2},{2,0},{4,6},{6,4},{8,10},{10,8},{12,14},{14,12},{16,18},{18,... | collective-permute-start | bytes 786440 | tf_op jit(solution)/shard_map/ppermute | solution.py:46
  92.1 1.8 %collective-permute-start.34 = (bf16[2,64,512]{2,1,0:T(8,128)(2,1)S(1)}, bf16[2,64,512]{2,1,0:T(8,128)(2,1)S(1)}, u32[]{:S(2)}, u32[]{:S(2)}) collective-permute-start(bf16[2,64,512]{2,1,0:T(8,128)(2,1)S(1)} %get-tuple-element.108), channel_id=1, source_target_pairs={{0,16},{2,18},{4,20},{6,22},{8,24},{10,26},{12,28},{14,30},{16,0},... | collective-permute-start | bytes 393224 | tf_op jit(solution)/shard_map/ppermute | solution.py:46
  93.9 1.7 %collective-permute-start.35 = (bf16[2,64,512]{2,1,0:T(8,128)(2,1)S(1)}, bf16[2,64,512]{2,1,0:T(8,128)(2,1)S(1)}, u32[]{:S(2)}, u32[]{:S(2)}) collective-permute-start(bf16[2,64,512]{2,1,0:T(8,128)(2,1)S(1)} %get-tuple-element.109.refs_5_), channel_id=1, source_target_pairs={{0,24},{2,26},{4,28},{6,30},{8,16},{10,18},{12,20},{14,22},{16,8},... | collective-permute-start | bytes 393224 | tf_op jit(solution)/shard_map/ppermute | solution.py:46
  95.9 1.7 %collective-permute-done.42.refs_1_ = bf16[4,64,512]{2,1,0:T(8,128)(2,1)S(1)} collective-permute-done((bf16[4,64,512]{2,1,0:T(8,128)(2,1)S(1)}, bf16[4,64,512]{2,1,0:T(8,128)(2,1)S(1)}, u32[]{:S(2)}, u32[]{:S(2)}) %collective-permute-start.42) | collective-permute-done | bytes 262176 | tf_op jit(solution)/shard_map/ppermute | solution.py:46
  97.9 1.2 %local_factors_back.1 = (bf16[512,512]{1,0:T(8,128)(2,1)S(1)}, bf16[2,512]{1,0:T(2,128)(2,1)S(1)}) custom-call(s32[2,8]{1,0:T(2,128)S(1)} %get-tuple-element.66.refs_2_.refs_0_, f32[4,64,512]{2,1,0:T(8,128)S(1)} %get-tuple-element.119.refs_1_, f32[4,64,512]{2,1,0:T(8,128)S(1)} %get-tuple-element.122.refs_2_, f32[4,64,512]{2,1,0:T(8,128)S(1)} %get-tuple-element.121.refs_3_, ...), custom_call_target="tpu_custom_call" | custom-call | tf_op jit(solution)/shard_map/local_factors_back/pallas_call | solution.py:60
  99.1 2.7 %collective-permute-start.43 = (bf16[2,512]{1,0:T(2,128)(2,1)S(1)}, bf16[2,512]{1,0:T(2,128)(2,1)S(1)}, u32[]{:S(2)}, u32[]{:S(2)}) collective-permute-start(bf16[2,512]{1,0:T(2,128)(2,1)S(1)} %get-tuple-element.125.refs_4_), channel_id=1, source_target_pairs={{2,4},{4,2},{6,8},{8,6},{10,12},{12,10},{14,16},{16,14},{18,20},{2... | collective-permute-start | bytes 6152 | tf_op jit(solution)/shard_map/ppermute | solution.py:41
  101.8 1.6 %collective-permute-start.44 = (bf16[2,512]{1,0:T(2,128)(2,1)S(1)}, bf16[2,512]{1,0:T(2,128)(2,1)S(1)}, u32[]{:S(2)}, u32[]{:S(2)}) collective-permute-start(bf16[2,512]{1,0:T(2,128)(2,1)S(1)} %get-tuple-element.125.refs_4_), channel_id=1, source_target_pairs={{0,2},{2,0},{4,6},{6,4},{8,10},{10,8},{12,14},{14,12},{16,18},{18,... | collective-permute-start | bytes 6152 | tf_op jit(solution)/shard_map/ppermute | solution.py:37
  103.4 3.0 %collective-permute-done.43.refs_1_ = bf16[2,512]{1,0:T(2,128)(2,1)S(1)} collective-permute-done((bf16[2,512]{1,0:T(2,128)(2,1)S(1)}, bf16[2,512]{1,0:T(2,128)(2,1)S(1)}, u32[]{:S(2)}, u32[]{:S(2)}) %collective-permute-start.43) | collective-permute-done | bytes 2080 | tf_op jit(solution)/shard_map/ppermute | solution.py:41
  106.4 1.2 %conv_back.1 = (bf16[512,512]{1,0:T(8,128)(2,1)}, f32[8,128]{1,0:T(8,128)S(1)}) custom-call(bf16[512,512]{1,0:T(8,128)(2,1)S(1)} %get-tuple-element.124.refs_0_, bf16[2,512]{1,0:T(2,128)(2,1)S(1)} %collective-permute-done.43.refs_1_, bf16[2,512]{1,0:T(2,128)(2,1)S(1)} %collective-permute-done.44.refs_2_, ...), custom_call_target="tpu_custom_call" | custom-call | tf_op jit(solution)/shard_map/conv_back/pallas_call | solution.py:60
  107.6 0.8 assemble.1
  (76 shorter events, 8.2 us)
Async XLA Ops:
  2.1 8.9 %collective-permute-start.1 = (bf16[5,512]{1,0:T(8,128)(2,1)S(1)}, bf16[5,512]{1,0:T(8,128)(2,1)S(1)}, u32[]{:S(2)}, u32[]{:S(2)}) collective-permute-start(bf16[5,512]{1,0:T(8,128)(2,1)S(1)} %pad_maximum_fusion), channel_id=1, source_target_pairs={{0,2},{2,0},{4,6},{6,4},{8,10},{10,8},{12,14},{14,12},{16,18},{18,... | collective-permute-start | bytes 15368 | tf_op jit(solution)/shard_map/ppermute | solution.py:37
  3.6 7.4 %collective-permute-start = (bf16[5,512]{1,0:T(8,128)(2,1)S(1)}, bf16[5,512]{1,0:T(8,128)(2,1)S(1)}, u32[]{:S(2)}, u32[]{:S(2)}) collective-permute-start(bf16[5,512]{1,0:T(8,128)(2,1)S(1)} %pad_maximum_fusion), channel_id=1, source_target_pairs={{2,4},{4,2},{6,8},{8,6},{10,12},{12,10},{14,16},{16,14},{18,20},{2... | collective-permute-start | bytes 15368 | tf_op jit(solution)/shard_map/ppermute | solution.py:41
  6.9 1.1 %copy-start.2 = (bf16[6,8,64,128]{3,2,1,0:T(8,128)(2,1)S(1)}, bf16[6,8,64,128]{3,2,1,0:T(8,128)(2,1)}, u32[]{:S(2)}) copy-start(bf16[6,8,64,128]{3,2,1,0:T(8,128)(2,1)} %refs_1_.1) | copy-start | bytes 2359300
  8.0 1.0 copy-start.3
  9.1 1.0 copy-start.4
  10.1 0.7 copy-start.5
  11.1 22.0 %collective-permute-start.9 = (bf16[6,64,512]{2,1,0:T(8,128)(2,1)S(1)}, bf16[6,64,512]{2,1,0:T(8,128)(2,1)S(1)}, u32[]{:S(2)}, u32[]{:S(2)}) collective-permute-start(bf16[6,64,512]{2,1,0:T(8,128)(2,1)S(1)} %get-tuple-element.70.refs_5_), channel_id=1, source_target_pairs={{0,16},{2,18},{4,20},{6,22},{8,24},{10,26},{12,28},{14,30},{16,0},... | collective-permute-start | bytes 1179656 | tf_op jit(solution)/shard_map/ppermute | solution.py:46
  15.8 5.9 %collective-permute-start.3 = (bf16[2,64,512]{2,1,0:T(8,128)(2,1)S(1)}, bf16[2,64,512]{2,1,0:T(8,128)(2,1)S(1)}, u32[]{:S(2)}, u32[]{:S(2)}) collective-permute-start(bf16[2,64,512]{2,1,0:T(8,128)(2,1)S(1)} %get-tuple-element.72.refs_0_), channel_id=1, source_target_pairs={{0,2},{2,0},{4,6},{6,4},{8,10},{10,8},{12,14},{14,12},{16,18},{18,... | collective-permute-start | bytes 393224 | tf_op jit(solution)/shard_map/ppermute | solution.py:46
  17.5 8.1 %collective-permute-start.2 = (bf16[2,64,512]{2,1,0:T(8,128)(2,1)S(1)}, bf16[2,64,512]{2,1,0:T(8,128)(2,1)S(1)}, u32[]{:S(2)}, u32[]{:S(2)}) collective-permute-start(bf16[2,64,512]{2,1,0:T(8,128)(2,1)S(1)} %get-tuple-element.71.refs_0_), channel_id=1, source_target_pairs={{0,2},{2,0},{4,6},{6,4},{8,10},{10,8},{12,14},{14,12},{16,18},{18,... | collective-permute-start | bytes 393224 | tf_op jit(solution)/shard_map/ppermute | solution.py:46
  22.0 5.6 %collective-permute-start.6 = (bf16[2,64,512]{2,1,0:T(8,128)(2,1)S(1)}, bf16[2,64,512]{2,1,0:T(8,128)(2,1)S(1)}, u32[]{:S(2)}, u32[]{:S(2)}) collective-permute-start(bf16[2,64,512]{2,1,0:T(8,128)(2,1)S(1)} %factor.8.refs_3_.refs_0_), channel_id=1, source_target_pairs={{0,4},{2,6},{4,0},{6,2},{8,12},{10,14},{12,8},{14,10},{16,20},{18,... | collective-permute-start | bytes 393224 | tf_op jit(solution)/shard_map/ppermute | solution.py:46
  22.7 12.0 %collective-permute-start.8 = (bf16[4,64,512]{2,1,0:T(8,128)(2,1)S(1)}, bf16[4,64,512]{2,1,0:T(8,128)(2,1)S(1)}, u32[]{:S(2)}, u32[]{:S(2)}) collective-permute-start(bf16[4,64,512]{2,1,0:T(8,128)(2,1)S(1)} %get-tuple-element.75), channel_id=1, source_target_pairs={{0,8},{2,10},{4,12},{6,14},{8,0},{10,2},{12,4},{14,6},{16,24},{18,... | collective-permute-start | bytes 786440 | tf_op jit(solution)/shard_map/ppermute | solution.py:46
  24.0 5.8 %collective-permute-start.5 = (bf16[2,64,512]{2,1,0:T(8,128)(2,1)S(1)}, bf16[2,64,512]{2,1,0:T(8,128)(2,1)S(1)}, u32[]{:S(2)}, u32[]{:S(2)}) collective-permute-start(bf16[2,64,512]{2,1,0:T(8,128)(2,1)S(1)} %get-tuple-element.74.refs_0_), channel_id=1, source_target_pairs={{0,2},{2,0},{4,6},{6,4},{8,10},{10,8},{12,14},{14,12},{16,18},{18,... | collective-permute-start | bytes 393224 | tf_op jit(solution)/shard_map/ppermute | solution.py:46
  25.9 6.3 %collective-permute-start.4 = (bf16[2,64,512]{2,1,0:T(8,128)(2,1)S(1)}, bf16[2,64,512]{2,1,0:T(8,128)(2,1)S(1)}, u32[]{:S(2)}, u32[]{:S(2)}) collective-permute-start(bf16[2,64,512]{2,1,0:T(8,128)(2,1)S(1)} %factor.9.refs_3_.refs_0_), channel_id=1, source_target_pairs={{0,4},{2,6},{4,0},{6,2},{8,12},{10,14},{12,8},{14,10},{16,20},{18,... | collective-permute-start | bytes 393224 | tf_op jit(solution)/shard_map/ppermute | solution.py:46
  27.8 9.4 %collective-permute-start.7 = (bf16[2,64,512]{2,1,0:T(8,128)(2,1)S(1)}, bf16[2,64,512]{2,1,0:T(8,128)(2,1)S(1)}, u32[]{:S(2)}, u32[]{:S(2)}) collective-permute-start(bf16[2,64,512]{2,1,0:T(8,128)(2,1)S(1)} %factor.10.refs_3_), channel_id=1, source_target_pairs={{0,8},{2,10},{4,12},{6,14},{8,0},{10,2},{12,4},{14,6},{16,24},{18,... | collective-permute-start | bytes 393224 | tf_op jit(solution)/shard_map/ppermute | solution.py:46
  29.7 12.5 %collective-permute-start.12 = (bf16[2,64,512]{2,1,0:T(8,128)(2,1)S(1)}, bf16[2,64,512]{2,1,0:T(8,128)(2,1)S(1)}, u32[]{:S(2)}, u32[]{:S(2)}) collective-permute-start(bf16[2,64,512]{2,1,0:T(8,128)(2,1)S(1)} %get-tuple-element.73.refs_3_.refs_0_), channel_id=1, source_target_pairs={{0,2},{2,0},{4,6},{6,4},{8,10},{10,8},{12,14},{14,12},{16,18},{18,... | collective-permute-start | bytes 393224 | tf_op jit(solution)/shard_map/ppermute | solution.py:46
  32.2 11.0 %collective-permute-start.11 = (bf16[2,64,512]{2,1,0:T(8,128)(2,1)S(1)}, bf16[2,64,512]{2,1,0:T(8,128)(2,1)S(1)}, u32[]{:S(2)}, u32[]{:S(2)}) collective-permute-start(bf16[2,64,512]{2,1,0:T(8,128)(2,1)S(1)} %factor.11.refs_3_.refs_0_), channel_id=1, source_target_pairs={{0,4},{2,6},{4,0},{6,2},{8,12},{10,14},{12,8},{14,10},{16,20},{18,... | collective-permute-start | bytes 393224 | tf_op jit(solution)/shard_map/ppermute | solution.py:46
  33.2 14.7 %collective-permute-start.13 = (bf16[3,64,512]{2,1,0:T(8,128)(2,1)S(1)}, bf16[3,64,512]{2,1,0:T(8,128)(2,1)S(1)}, u32[]{:S(2)}, u32[]{:S(2)}) collective-permute-start(bf16[3,64,512]{2,1,0:T(8,128)(2,1)S(1)} %forward.1.refs_4_), channel_id=1, source_target_pairs={{0,8},{2,10},{4,12},{6,14},{8,0},{10,2},{12,4},{14,6},{16,24},{18,... | collective-permute-start | bytes 589832 | tf_op jit(solution)/shard_map/ppermute | solution.py:46
  37.6 13.8 %copy-start = (bf16[2048,1024]{1,0:T(8,128)(2,1)S(1)}, bf16[2048,1024]{1,0:T(8,128)(2,1)}, u32[]{:S(2)}) copy-start(bf16[2048,1024]{1,0:T(8,128)(2,1)} %refs_3_.5) | copy-start | bytes 12582916
  37.6 8.3 %collective-permute-start.10 = (bf16[2,64,512]{2,1,0:T(8,128)(2,1)S(1)}, bf16[2,64,512]{2,1,0:T(8,128)(2,1)S(1)}, u32[]{:S(2)}, u32[]{:S(2)}) collective-permute-start(bf16[2,64,512]{2,1,0:T(8,128)(2,1)S(1)} %get-tuple-element.77.refs_3_), channel_id=1, source_target_pairs={{0,16},{2,18},{4,20},{6,22},{8,24},{10,26},{12,28},{14,30},{16,0},... | collective-permute-start | bytes 393224 | tf_op jit(solution)/shard_map/ppermute | solution.py:46
  42.5 5.0 %collective-permute-start.14 = (bf16[2,64,512]{2,1,0:T(8,128)(2,1)S(1)}, bf16[2,64,512]{2,1,0:T(8,128)(2,1)S(1)}, u32[]{:S(2)}, u32[]{:S(2)}) collective-permute-start(bf16[2,64,512]{2,1,0:T(8,128)(2,1)S(1)} %factor.13.refs_3_.refs_0_), channel_id=1, source_target_pairs={{0,4},{2,6},{4,0},{6,2},{8,12},{10,14},{12,8},{14,10},{16,20},{18,... | collective-permute-start | bytes 393224 | tf_op jit(solution)/shard_map/ppermute | solution.py:46
  43.5 5.0 %collective-permute-start.17 = (bf16[2,64,512]{2,1,0:T(8,128)(2,1)S(1)}, bf16[2,64,512]{2,1,0:T(8,128)(2,1)S(1)}, u32[]{:S(2)}, u32[]{:S(2)}) collective-permute-start(bf16[2,64,512]{2,1,0:T(8,128)(2,1)S(1)} %factor.14.refs_1_), channel_id=1, source_target_pairs={{0,8},{2,10},{4,12},{6,14},{8,0},{10,2},{12,4},{14,6},{16,24},{18,... | collective-permute-start | bytes 393224 | tf_op jit(solution)/shard_map/ppermute | solution.py:46
  48.5 4.2 %copy-start.1 = (bf16[1024,2048]{1,0:T(8,128)(2,1)S(1)}, bf16[1024,2048]{1,0:T(8,128)(2,1)}, u32[]{:S(2)}) copy-start(bf16[1024,2048]{1,0:T(8,128)(2,1)} %refs_5_.3) | copy-start | bytes 12582916
  48.9 2.5 %collective-permute-start.18 = (bf16[256,512]{1,0:T(8,128)(2,1)S(1)}, bf16[256,512]{1,0:T(8,128)(2,1)S(1)}, u32[]{:S(2)}, u32[]{:S(2)}) collective-permute-start(bf16[256,512]{1,0:T(8,128)(2,1)S(1)} %get-tuple-element.82.refs_0_), channel_id=1, source_target_pairs={{1,0},{0,1},{3,2},{2,3},{5,4},{4,5},{7,6},{6,7},{9,8},{8,9},{11,10... | collective-permute-start | bytes 786440 | tf_op jit(solution)/shard_map/ppermute | solution.py:51
  49.0 7.3 %collective-permute-start.19 = (bf16[256,512]{1,0:T(8,128)(2,1)S(1)}, bf16[256,512]{1,0:T(8,128)(2,1)S(1)}, u32[]{:S(2)}, u32[]{:S(2)}) collective-permute-start(bf16[256,512]{1,0:T(8,128)(2,1)S(1)} %get-tuple-element.83.refs_3_.refs_0_), channel_id=1, source_target_pairs={{1,0},{0,1},{3,2},{2,3},{5,4},{4,5},{7,6},{6,7},{9,8},{8,9},{11,10... | collective-permute-start | bytes 786440 | tf_op jit(solution)/shard_map/ppermute | solution.py:51
  49.5 3.2 %collective-permute-start.15 = (bf16[128,512]{1,0:T(8,128)(2,1)S(1)}, bf16[128,512]{1,0:T(8,128)(2,1)S(1)}, u32[]{:S(2)}, u32[]{:S(2)}) collective-permute-start(bf16[128,512]{1,0:T(8,128)(2,1)S(1)} %get-tuple-element.78.refs_0_.refs_1_), channel_id=1, source_target_pairs={{1,0},{0,1},{3,2},{2,3},{5,4},{4,5},{7,6},{6,7},{9,8},{8,9},{11,10... | collective-permute-start | bytes 393224 | tf_op jit(solution)/shard_map/ppermute | solution.py:51
  49.6 3.1 %collective-permute-start.16 = (bf16[128,512]{1,0:T(8,128)(2,1)S(1)}, bf16[128,512]{1,0:T(8,128)(2,1)S(1)}, u32[]{:S(2)}, u32[]{:S(2)}) collective-permute-start(bf16[128,512]{1,0:T(8,128)(2,1)S(1)} %get-tuple-element.79.refs_4_.refs_1_.refs_2_), channel_id=1, source_target_pairs={{1,0},{0,1},{3,2},{2,3},{5,4},{4,5},{7,6},{6,7},{9,8},{8,9},{11,10... | collective-permute-start | bytes 393224 | tf_op jit(solution)/shard_map/ppermute | solution.py:51
  50.0 8.8 %collective-permute-start.20 = (bf16[2,64,512]{2,1,0:T(8,128)(2,1)S(1)}, bf16[2,64,512]{2,1,0:T(8,128)(2,1)S(1)}, u32[]{:S(2)}, u32[]{:S(2)}) collective-permute-start(bf16[2,64,512]{2,1,0:T(8,128)(2,1)S(1)} %get-tuple-element.81.refs_4_), channel_id=1, source_target_pairs={{0,16},{2,18},{4,20},{6,22},{8,24},{10,26},{12,28},{14,30},{16,0},... | collective-permute-start | bytes 393224 | tf_op jit(solution)/shard_map/ppermute | solution.py:46
  55.7 4.1 %collective-permute-start.23 = (bf16[128,512]{1,0:T(8,128)(2,1)S(1)}, bf16[128,512]{1,0:T(8,128)(2,1)S(1)}, u32[]{:S(2)}, u32[]{:S(2)}) collective-permute-start(bf16[128,512]{1,0:T(8,128)(2,1)S(1)} %get-tuple-element.92), channel_id=1, source_target_pairs={{1,0},{0,1},{3,2},{2,3},{5,4},{4,5},{7,6},{6,7},{9,8},{8,9},{11,10... | collective-permute-start | bytes 393224 | tf_op jit(solution)/shard_map/ppermute | solution.py:51
  55.8 4.0 %collective-permute-start.24 = (bf16[128,512]{1,0:T(8,128)(2,1)S(1)}, bf16[128,512]{1,0:T(8,128)(2,1)S(1)}, u32[]{:S(2)}, u32[]{:S(2)}) collective-permute-start(bf16[128,512]{1,0:T(8,128)(2,1)S(1)} %get-tuple-element.85.refs_3_), channel_id=1, source_target_pairs={{1,0},{0,1},{3,2},{2,3},{5,4},{4,5},{7,6},{6,7},{9,8},{8,9},{11,10... | collective-permute-start | bytes 393224 | tf_op jit(solution)/shard_map/ppermute | solution.py:51
  59.2 3.0 %collective-permute-start.21 = (bf16[128,512]{1,0:T(8,128)(2,1)S(1)}, bf16[128,512]{1,0:T(8,128)(2,1)S(1)}, u32[]{:S(2)}, u32[]{:S(2)}) collective-permute-start(bf16[128,512]{1,0:T(8,128)(2,1)S(1)} %get-tuple-element.89.refs_0_.refs_1_), channel_id=1, source_target_pairs={{1,0},{0,1},{3,2},{2,3},{5,4},{4,5},{7,6},{6,7},{9,8},{8,9},{11,10... | collective-permute-start | bytes 393224 | tf_op jit(solution)/shard_map/ppermute | solution.py:51
  59.4 4.6 %collective-permute-start.22 = (bf16[128,512]{1,0:T(8,128)(2,1)S(1)}, bf16[128,512]{1,0:T(8,128)(2,1)S(1)}, u32[]{:S(2)}, u32[]{:S(2)}) collective-permute-start(bf16[128,512]{1,0:T(8,128)(2,1)S(1)} %get-tuple-element.90.refs_8_.refs_1_.refs_2_), channel_id=1, source_target_pairs={{1,0},{0,1},{3,2},{2,3},{5,4},{4,5},{7,6},{6,7},{9,8},{8,9},{11,10... | collective-permute-start | bytes 393224 | tf_op jit(solution)/shard_map/ppermute | solution.py:51
  60.4 6.8 %collective-permute-start.30 = (bf16[64,512]{1,0:T(8,128)(2,1)S(1)}, bf16[64,512]{1,0:T(8,128)(2,1)S(1)}, u32[]{:S(2)}, u32[]{:S(2)}) collective-permute-start(bf16[64,512]{1,0:T(8,128)(2,1)S(1)} %get-tuple-element.102), channel_id=1, source_target_pairs={{0,8},{2,10},{4,12},{6,14},{8,0},{10,2},{12,4},{14,6},{16,24},{18,... | collective-permute-start | bytes 196616 | tf_op jit(solution)/shard_map/ppermute | solution.py:46
  61.0 15.3 %collective-permute-start.25 = (bf16[256,512]{1,0:T(8,128)(2,1)S(1)}, bf16[256,512]{1,0:T(8,128)(2,1)S(1)}, u32[]{:S(2)}, u32[]{:S(2)}) collective-permute-start(bf16[256,512]{1,0:T(8,128)(2,1)S(1)} %get-tuple-element.88.refs_6_), channel_id=1, source_target_pairs={{1,0},{0,1},{3,2},{2,3},{5,4},{4,5},{7,6},{6,7},{9,8},{8,9},{11,10... | collective-permute-start | bytes 786440 | tf_op jit(solution)/shard_map/ppermute | solution.py:51
  61.0 8.0 %collective-permute-start.31 = (bf16[64,512]{1,0:T(8,128)(2,1)S(1)}, bf16[64,512]{1,0:T(8,128)(2,1)S(1)}, u32[]{:S(2)}, u32[]{:S(2)}) collective-permute-start(bf16[64,512]{1,0:T(8,128)(2,1)S(1)} %get-tuple-element.103), channel_id=1, source_target_pairs={{0,16},{2,18},{4,20},{6,22},{8,24},{10,26},{12,28},{14,30},{16,0},... | collective-permute-start | bytes 196616 | tf_op jit(solution)/shard_map/ppermute | solution.py:46
  62.2 8.4 %collective-permute-start.32 = (bf16[64,512]{1,0:T(8,128)(2,1)S(1)}, bf16[64,512]{1,0:T(8,128)(2,1)S(1)}, u32[]{:S(2)}, u32[]{:S(2)}) collective-permute-start(bf16[64,512]{1,0:T(8,128)(2,1)S(1)} %get-tuple-element.93.refs_6_), channel_id=1, source_target_pairs={{0,24},{2,26},{4,28},{6,30},{8,16},{10,18},{12,20},{14,22},{16,8},... | collective-permute-start | bytes 196616 | tf_op jit(solution)/shard_map/ppermute | solution.py:46
  67.1 3.9 %collective-permute-start.28 = (bf16[128,512]{1,0:T(8,128)(2,1)S(1)}, bf16[128,512]{1,0:T(8,128)(2,1)S(1)}, u32[]{:S(2)}, u32[]{:S(2)}) collective-permute-start(bf16[128,512]{1,0:T(8,128)(2,1)S(1)} %get-tuple-element.100), channel_id=1, source_target_pairs={{1,0},{0,1},{3,2},{2,3},{5,4},{4,5},{7,6},{6,7},{9,8},{8,9},{11,10... | collective-permute-start | bytes 393224 | tf_op jit(solution)/shard_map/ppermute | solution.py:51
  67.2 3.8 %collective-permute-start.29 = (bf16[128,512]{1,0:T(8,128)(2,1)S(1)}, bf16[128,512]{1,0:T(8,128)(2,1)S(1)}, u32[]{:S(2)}, u32[]{:S(2)}) collective-permute-start(bf16[128,512]{1,0:T(8,128)(2,1)S(1)} %get-tuple-element.95.refs_4_), channel_id=1, source_target_pairs={{1,0},{0,1},{3,2},{2,3},{5,4},{4,5},{7,6},{6,7},{9,8},{8,9},{11,10... | collective-permute-start | bytes 393224 | tf_op jit(solution)/shard_map/ppermute | solution.py:51
  69.0 4.5 %collective-permute-start.26 = (bf16[128,512]{1,0:T(8,128)(2,1)S(1)}, bf16[128,512]{1,0:T(8,128)(2,1)S(1)}, u32[]{:S(2)}, u32[]{:S(2)}) collective-permute-start(bf16[128,512]{1,0:T(8,128)(2,1)S(1)} %get-tuple-element.97), channel_id=1, source_target_pairs={{1,0},{0,1},{3,2},{2,3},{5,4},{4,5},{7,6},{6,7},{9,8},{8,9},{11,10... | collective-permute-start | bytes 393224 | tf_op jit(solution)/shard_map/ppermute | solution.py:51
  70.6 4.6 %collective-permute-start.27 = (bf16[128,512]{1,0:T(8,128)(2,1)S(1)}, bf16[128,512]{1,0:T(8,128)(2,1)S(1)}, u32[]{:S(2)}, u32[]{:S(2)}) collective-permute-start(bf16[128,512]{1,0:T(8,128)(2,1)S(1)} %get-tuple-element.98.refs_5_), channel_id=1, source_target_pairs={{1,0},{0,1},{3,2},{2,3},{5,4},{4,5},{7,6},{6,7},{9,8},{8,9},{11,10... | collective-permute-start | bytes 393224 | tf_op jit(solution)/shard_map/ppermute | solution.py:51
  71.6 5.0 %collective-permute-start.37 = (bf16[64,512]{1,0:T(8,128)(2,1)S(1)}, bf16[64,512]{1,0:T(8,128)(2,1)S(1)}, u32[]{:S(2)}, u32[]{:S(2)}) collective-permute-start(bf16[64,512]{1,0:T(8,128)(2,1)S(1)} %get-tuple-element.112), channel_id=1, source_target_pairs={{0,8},{2,10},{4,12},{6,14},{8,0},{10,2},{12,4},{14,6},{16,24},{18,... | collective-permute-start | bytes 196616 | tf_op jit(solution)/shard_map/ppermute | solution.py:46
  72.2 6.1 %collective-permute-start.38 = (bf16[64,512]{1,0:T(8,128)(2,1)S(1)}, bf16[64,512]{1,0:T(8,128)(2,1)S(1)}, u32[]{:S(2)}, u32[]{:S(2)}) collective-permute-start(bf16[64,512]{1,0:T(8,128)(2,1)S(1)} %get-tuple-element.113), channel_id=1, source_target_pairs={{0,16},{2,18},{4,20},{6,22},{8,24},{10,26},{12,28},{14,30},{16,0},... | collective-permute-start | bytes 196616 | tf_op jit(solution)/shard_map/ppermute | solution.py:46
  73.5 7.9 %collective-permute-start.39 = (bf16[64,512]{1,0:T(8,128)(2,1)S(1)}, bf16[64,512]{1,0:T(8,128)(2,1)S(1)}, u32[]{:S(2)}, u32[]{:S(2)}) collective-permute-start(bf16[64,512]{1,0:T(8,128)(2,1)S(1)} %get-tuple-element.105.refs_5_), channel_id=1, source_target_pairs={{0,24},{2,26},{4,28},{6,30},{8,16},{10,18},{12,20},{14,22},{16,8},... | collective-permute-start | bytes 196616 | tf_op jit(solution)/shard_map/ppermute | solution.py:46
  75.2 7.8 %collective-permute-start.36 = (bf16[4,64,512]{2,1,0:T(8,128)(2,1)S(1)}, bf16[4,64,512]{2,1,0:T(8,128)(2,1)S(1)}, u32[]{:S(2)}, u32[]{:S(2)}) collective-permute-start(bf16[4,64,512]{2,1,0:T(8,128)(2,1)S(1)} %get-tuple-element.104.refs_8_), channel_id=1, source_target_pairs={{0,4},{2,6},{4,0},{6,2},{8,12},{10,14},{12,8},{14,10},{16,20},{18,... | collective-permute-start | bytes 786440 | tf_op jit(solution)/shard_map/ppermute | solution.py:46
  81.7 8.2 %collective-permute-start.41 = (bf16[4,64,512]{2,1,0:T(8,128)(2,1)S(1)}, bf16[4,64,512]{2,1,0:T(8,128)(2,1)S(1)}, u32[]{:S(2)}, u32[]{:S(2)}) collective-permute-start(bf16[4,64,512]{2,1,0:T(8,128)(2,1)S(1)} %get-tuple-element.114.refs_3_), channel_id=1, source_target_pairs={{0,4},{2,6},{4,0},{6,2},{8,12},{10,14},{12,8},{14,10},{16,20},{18,... | collective-permute-start | bytes 786440 | tf_op jit(solution)/shard_map/ppermute | solution.py:46
  83.3 12.2 %collective-permute-start.40 = (bf16[4,64,512]{2,1,0:T(8,128)(2,1)S(1)}, bf16[4,64,512]{2,1,0:T(8,128)(2,1)S(1)}, u32[]{:S(2)}, u32[]{:S(2)}) collective-permute-start(bf16[4,64,512]{2,1,0:T(8,128)(2,1)S(1)} %get-tuple-element.116.refs_3_), channel_id=1, source_target_pairs={{0,2},{2,0},{4,6},{6,4},{8,10},{10,8},{12,14},{14,12},{16,18},{18,... | collective-permute-start | bytes 786440 | tf_op jit(solution)/shard_map/ppermute | solution.py:46
  90.2 7.3 %collective-permute-start.42 = (bf16[4,64,512]{2,1,0:T(8,128)(2,1)S(1)}, bf16[4,64,512]{2,1,0:T(8,128)(2,1)S(1)}, u32[]{:S(2)}, u32[]{:S(2)}) collective-permute-start(bf16[4,64,512]{2,1,0:T(8,128)(2,1)S(1)} %get-tuple-element.118.refs_3_), channel_id=1, source_target_pairs={{0,2},{2,0},{4,6},{6,4},{8,10},{10,8},{12,14},{14,12},{16,18},{18,... | collective-permute-start | bytes 786440 | tf_op jit(solution)/shard_map/ppermute | solution.py:46
  92.1 15.5 %collective-permute-start.33 = (bf16[2,64,512]{2,1,0:T(8,128)(2,1)S(1)}, bf16[2,64,512]{2,1,0:T(8,128)(2,1)S(1)}, u32[]{:S(2)}, u32[]{:S(2)}) collective-permute-start(bf16[2,64,512]{2,1,0:T(8,128)(2,1)S(1)} %get-tuple-element.107), channel_id=1, source_target_pairs={{0,8},{2,10},{4,12},{6,14},{8,0},{10,2},{12,4},{14,6},{16,24},{18,... | collective-permute-start | bytes 393224 | tf_op jit(solution)/shard_map/ppermute | solution.py:46
  92.1 15.4 %collective-permute-start.34 = (bf16[2,64,512]{2,1,0:T(8,128)(2,1)S(1)}, bf16[2,64,512]{2,1,0:T(8,128)(2,1)S(1)}, u32[]{:S(2)}, u32[]{:S(2)}) collective-permute-start(bf16[2,64,512]{2,1,0:T(8,128)(2,1)S(1)} %get-tuple-element.108), channel_id=1, source_target_pairs={{0,16},{2,18},{4,20},{6,22},{8,24},{10,26},{12,28},{14,30},{16,0},... | collective-permute-start | bytes 393224 | tf_op jit(solution)/shard_map/ppermute | solution.py:46
  93.9 13.7 %collective-permute-start.35 = (bf16[2,64,512]{2,1,0:T(8,128)(2,1)S(1)}, bf16[2,64,512]{2,1,0:T(8,128)(2,1)S(1)}, u32[]{:S(2)}, u32[]{:S(2)}) collective-permute-start(bf16[2,64,512]{2,1,0:T(8,128)(2,1)S(1)} %get-tuple-element.109.refs_5_), channel_id=1, source_target_pairs={{0,24},{2,26},{4,28},{6,30},{8,16},{10,18},{12,20},{14,22},{16,8},... | collective-permute-start | bytes 393224 | tf_op jit(solution)/shard_map/ppermute | solution.py:46
  99.1 7.3 %collective-permute-start.43 = (bf16[2,512]{1,0:T(2,128)(2,1)S(1)}, bf16[2,512]{1,0:T(2,128)(2,1)S(1)}, u32[]{:S(2)}, u32[]{:S(2)}) collective-permute-start(bf16[2,512]{1,0:T(2,128)(2,1)S(1)} %get-tuple-element.125.refs_4_), channel_id=1, source_target_pairs={{2,4},{4,2},{6,8},{8,6},{10,12},{12,10},{14,16},{16,14},{18,20},{2... | collective-permute-start | bytes 6152 | tf_op jit(solution)/shard_map/ppermute | solution.py:41
  101.8 4.6 %collective-permute-start.44 = (bf16[2,512]{1,0:T(2,128)(2,1)S(1)}, bf16[2,512]{1,0:T(2,128)(2,1)S(1)}, u32[]{:S(2)}, u32[]{:S(2)}) collective-permute-start(bf16[2,512]{1,0:T(2,128)(2,1)S(1)} %get-tuple-element.125.refs_4_), channel_id=1, source_target_pairs={{0,2},{2,0},{4,6},{6,4},{8,10},{10,8},{12,14},{14,12},{16,18},{18,... | collective-permute-start | bytes 6152 | tf_op jit(solution)/shard_map/ppermute | solution.py:37

commit v4 on v2

--- a/solution.py
+++ b/solution.py
@@ -10,7 +10,7 @@
 BLOCK = 64
 LOCAL = 2
 QUARTERS = 4
-TILE = 512
+TILE = 256
 SMALL = 8 * 1024 * 1024
 LARGE = 20 * 1024 * 1024
 ALL = 44 * 1024 * 1024

time: 108 us -> 109 us (level)
  no operation moved by 1% of the time
where the time goes in v4:
time: 109 us; the launch traced here: 108 us
  starting transfers between devices  48.8 us (45%)
  waiting for transfers between devices  28.8 us (26%)
  Pallas kernels  23.7 us (22%)
  local copies, waits for them, and re-layouts  4.62 us (4%)
    ppermute x28, starting transfers between devices, from_flipped(): return lax.ppermute(block, axis, [(i, i ^ mask) for i in range(count)])  36.1 us
    ppermute x28, waiting for transfers between devices, from_flipped(): return lax.ppermute(block, axis, [(i, i ^ mask) for i in range(count)])  25.1 us
    pallas_call x36, Pallas kernels, call(): pl.pallas_call(body, out_shape=[jax.ShapeDtypeStruct(shape, kind) for sha...  23.7 us
    ppermute x2, starting transfers between devices, neighbours(): return (near, lax.ppermute(edges, axis, route))  6.43 us
    unnamed x12, local copies, waits for them, and re-layouts  3.9 us
    ppermute x2, waiting for transfers between devices, neighbours(): return (near, lax.ppermute(edges, axis, route))  3.64 us
    ppermute x13, starting transfers between devices, from_offset(): lax.ppermute(block, axis, [((i + offset) % count, i) for i in range(count)])  3.19 us
    ppermute x2, starting transfers between devices, neighbours(): near = lax.ppermute(edges, axis, [(i, i ^ 1) for i in range(count)])  3.07 us
  transfers between devices with their start and end apart: 45, of which 14 were waited for; matrix products, arithmetic and copies ran while one was open for 0% of the time, Pallas kernels for 19%

profile of v4, /device:TPU:8, one launch (start us, length us, event | category | flops | bytes accessed | tf_op | source)
XLA Modules:
  0.0 107.8 jit_solution(17809913055493726536)
XLA Ops:
  0.6 0.7 fusion
  1.4 0.7 pad_maximum_fusion
  2.1 1.6 %collective-permute-start.1 = (bf16[5,512]{1,0:T(8,128)(2,1)S(1)}, bf16[5,512]{1,0:T(8,128)(2,1)S(1)}, u32[]{:S(2)}, u32[]{:S(2)}) collective-permute-start(bf16[5,512]{1,0:T(8,128)(2,1)S(1)} %pad_maximum_fusion), channel_id=1, source_target_pairs={{0,2},{2,0},{4,6},{6,4},{8,10},{10,8},{12,14},{14,12},{16,18},{18,... | collective-permute-start | bytes 15368 | tf_op jit(solution)/shard_map/ppermute | solution.py:37
  3.6 3.3 %collective-permute-start = (bf16[5,512]{1,0:T(8,128)(2,1)S(1)}, bf16[5,512]{1,0:T(8,128)(2,1)S(1)}, u32[]{:S(2)}, u32[]{:S(2)}) collective-permute-start(bf16[5,512]{1,0:T(8,128)(2,1)S(1)} %pad_maximum_fusion), channel_id=1, source_target_pairs={{2,4},{4,2},{6,8},{8,6},{10,12},{12,10},{14,16},{16,14},{18,20},{2... | collective-permute-start | bytes 15368 | tf_op jit(solution)/shard_map/ppermute | solution.py:41
  6.9 1.1 %copy-done.2 = bf16[6,8,64,128]{3,2,1,0:T(8,128)(2,1)S(1)} copy-done((bf16[6,8,64,128]{3,2,1,0:T(8,128)(2,1)S(1)}, bf16[6,8,64,128]{3,2,1,0:T(8,128)(2,1)}, u32[]{:S(2)}) %copy-start.2) | copy-done | bytes 786456
  8.0 1.0 copy-done.3
  9.1 0.7 copy-done.5
  9.9 1.1 collective-permute-done.refs_2_
  10.9 2.1 %conv_and_local_factors.1 = (bf16[512,512]{1,0:T(8,128)(2,1)}, bf16[2,64,512]{2,1,0:T(8,128)(2,1)S(1)}, bf16[2,64,512]{2,1,0:T(8,128)(2,1)S(1)}, bf16[2,64,512]{2,1,0:T(8,128)(2,1)S(1)}, bf16[2,64,512]{2,1,0:T(8,128)(2,1)S(1)}) custom-call(s32[2,8]{1,0:T(2,128)S(1)} %get-tuple-element.65.refs_0_.refs_5_, bf16[512,512]{1,0:T(8,128)(2,1)S(1)} %get-tuple-element.66.refs_1_, ...), custom_call_target="tpu_custom_call" | custom-call | tf_op jit(solution)/shard_map/conv_and_local_factors/pallas_call | solution.py:60
  13.1 0.6 collective-permute-start.3
  13.7 1.0 copy-done.4
  14.8 2.7 %collective-permute-start.12 = (bf16[6,64,512]{2,1,0:T(8,128)(2,1)S(1)}, bf16[6,64,512]{2,1,0:T(8,128)(2,1)S(1)}, u32[]{:S(2)}, u32[]{:S(2)}) collective-permute-start(bf16[6,64,512]{2,1,0:T(8,128)(2,1)S(1)} %get-tuple-element.71.refs_3_), channel_id=1, source_target_pairs={{0,16},{2,18},{4,20},{6,22},{8,24},{10,26},{12,28},{14,30},{16,0},... | collective-permute-start | bytes 1179656 | tf_op jit(solution)/shard_map/ppermute | solution.py:46
  17.4 1.5 %collective-permute-start.2 = (bf16[2,64,512]{2,1,0:T(8,128)(2,1)S(1)}, bf16[2,64,512]{2,1,0:T(8,128)(2,1)S(1)}, u32[]{:S(2)}, u32[]{:S(2)}) collective-permute-start(bf16[2,64,512]{2,1,0:T(8,128)(2,1)S(1)} %get-tuple-element.68.refs_0_), channel_id=1, source_target_pairs={{0,2},{2,0},{4,6},{6,4},{8,10},{10,8},{12,14},{14,12},{16,18},{18,... | collective-permute-start | bytes 393224 | tf_op jit(solution)/shard_map/ppermute | solution.py:46
  19.2 0.7 collective-permute-start.6
  19.9 0.4 collective-permute-start.8
  20.3 1.5 %collective-permute-start.5 = (bf16[2,64,512]{2,1,0:T(8,128)(2,1)S(1)}, bf16[2,64,512]{2,1,0:T(8,128)(2,1)S(1)}, u32[]{:S(2)}, u32[]{:S(2)}) collective-permute-start(bf16[2,64,512]{2,1,0:T(8,128)(2,1)S(1)} %get-tuple-element.72.refs_0_), channel_id=1, source_target_pairs={{0,2},{2,0},{4,6},{6,4},{8,10},{10,8},{12,14},{14,12},{16,18},{18,... | collective-permute-start | bytes 393224 | tf_op jit(solution)/shard_map/ppermute | solution.py:46
  21.8 1.6 %collective-permute-done.2.refs_1_ = bf16[2,64,512]{2,1,0:T(8,128)(2,1)S(1)} collective-permute-done((bf16[2,64,512]{2,1,0:T(8,128)(2,1)S(1)}, bf16[2,64,512]{2,1,0:T(8,128)(2,1)S(1)}, u32[]{:S(2)}, u32[]{:S(2)}) %collective-permute-start.2) | collective-permute-done | bytes 131104 | tf_op jit(solution)/shard_map/ppermute | solution.py:46
  24.0 1.4 %collective-permute-done.6.refs_1_ = bf16[2,64,512]{2,1,0:T(8,128)(2,1)S(1)} collective-permute-done((bf16[2,64,512]{2,1,0:T(8,128)(2,1)S(1)}, bf16[2,64,512]{2,1,0:T(8,128)(2,1)S(1)}, u32[]{:S(2)}, u32[]{:S(2)}) %collective-permute-start.6) | collective-permute-done | bytes 131104 | tf_op jit(solution)/shard_map/ppermute | solution.py:46
  25.6 0.8 collective-permute-start.7
  26.4 0.4 collective-permute-start.11
  27.1 1.8 %collective-permute-done.4.refs_1_ = bf16[2,64,512]{2,1,0:T(8,128)(2,1)S(1)} collective-permute-done((bf16[2,64,512]{2,1,0:T(8,128)(2,1)S(1)}, bf16[2,64,512]{2,1,0:T(8,128)(2,1)S(1)}, u32[]{:S(2)}, u32[]{:S(2)}) %collective-permute-start.4) | collective-permute-done | bytes 131104 | tf_op jit(solution)/shard_map/ppermute | solution.py:46
  29.2 3.7 %collective-permute-done.8.refs_3_.refs_1_.refs_5_ = bf16[4,64,512]{2,1,0:T(8,128)(2,1)S(1)} collective-permute-done((bf16[4,64,512]{2,1,0:T(8,128)(2,1)S(1)}, bf16[4,64,512]{2,1,0:T(8,128)(2,1)S(1)}, u32[]{:S(2)}, u32[]{:S(2)}) %collective-permute-start.8) | collective-permute-done | bytes 262176 | tf_op jit(solution)/shard_map/ppermute | solution.py:46
  33.0 1.4 %collective-permute-done.7.refs_1_ = bf16[2,64,512]{2,1,0:T(8,128)(2,1)S(1)} collective-permute-done((bf16[2,64,512]{2,1,0:T(8,128)(2,1)S(1)}, bf16[2,64,512]{2,1,0:T(8,128)(2,1)S(1)}, u32[]{:S(2)}, u32[]{:S(2)}) %collective-permute-start.7) | collective-permute-done | bytes 131104 | tf_op jit(solution)/shard_map/ppermute | solution.py:46
  34.8 2.5 %collective-permute-start.13 = (bf16[3,64,512]{2,1,0:T(8,128)(2,1)S(1)}, bf16[3,64,512]{2,1,0:T(8,128)(2,1)S(1)}, u32[]{:S(2)}, u32[]{:S(2)}) collective-permute-start(bf16[3,64,512]{2,1,0:T(8,128)(2,1)S(1)} %forward.1.refs_3_), channel_id=1, source_target_pairs={{0,8},{2,10},{4,12},{6,14},{8,0},{10,2},{12,4},{14,6},{16,24},{18,... | collective-permute-start | bytes 589832 | tf_op jit(solution)/shard_map/ppermute | solution.py:46
  37.3 2.7 %collective-permute-start.9 = (bf16[2,64,512]{2,1,0:T(8,128)(2,1)S(1)}, bf16[2,64,512]{2,1,0:T(8,128)(2,1)S(1)}, u32[]{:S(2)}, u32[]{:S(2)}) collective-permute-start(bf16[2,64,512]{2,1,0:T(8,128)(2,1)S(1)} %get-tuple-element.75.refs_1_), channel_id=1, source_target_pairs={{0,16},{2,18},{4,20},{6,22},{8,24},{10,26},{12,28},{14,30},{16,0},... | collective-permute-start | bytes 393224 | tf_op jit(solution)/shard_map/ppermute | solution.py:46
  40.3 2.5 %collective-permute-start.14 = (bf16[2,64,512]{2,1,0:T(8,128)(2,1)S(1)}, bf16[2,64,512]{2,1,0:T(8,128)(2,1)S(1)}, u32[]{:S(2)}, u32[]{:S(2)}) collective-permute-start(bf16[2,64,512]{2,1,0:T(8,128)(2,1)S(1)} %factor.13.refs_3_.refs_0_), channel_id=1, source_target_pairs={{0,4},{2,6},{4,0},{6,2},{8,12},{10,14},{12,8},{14,10},{16,20},{18,... | collective-permute-start | bytes 393224 | tf_op jit(solution)/shard_map/ppermute | solution.py:46
  43.1 2.0 %collective-permute-start.17 = (bf16[2,64,512]{2,1,0:T(8,128)(2,1)S(1)}, bf16[2,64,512]{2,1,0:T(8,128)(2,1)S(1)}, u32[]{:S(2)}, u32[]{:S(2)}) collective-permute-start(bf16[2,64,512]{2,1,0:T(8,128)(2,1)S(1)} %factor.14.refs_1_), channel_id=1, source_target_pairs={{0,8},{2,10},{4,12},{6,14},{8,0},{10,2},{12,4},{14,6},{16,24},{18,... | collective-permute-start | bytes 393224 | tf_op jit(solution)/shard_map/ppermute | solution.py:46
  45.1 1.0 collective-permute-done.9.refs_0_
  46.8 1.3 %collective-permute-done.17.refs_1_ = bf16[2,64,512]{2,1,0:T(8,128)(2,1)S(1)} collective-permute-done((bf16[2,64,512]{2,1,0:T(8,128)(2,1)S(1)}, bf16[2,64,512]{2,1,0:T(8,128)(2,1)S(1)}, u32[]{:S(2)}, u32[]{:S(2)}) %collective-permute-start.17) | collective-permute-done | bytes 131104 | tf_op jit(solution)/shard_map/ppermute | solution.py:46
  48.6 0.5 collective-permute-start.19
  49.2 0.4 collective-permute-start.16
  49.6 1.2 %collective-permute-start.20 = (bf16[2,64,512]{2,1,0:T(8,128)(2,1)S(1)}, bf16[2,64,512]{2,1,0:T(8,128)(2,1)S(1)}, u32[]{:S(2)}, u32[]{:S(2)}) collective-permute-start(bf16[2,64,512]{2,1,0:T(8,128)(2,1)S(1)} %get-tuple-element.79.refs_4_), channel_id=1, source_target_pairs={{0,16},{2,18},{4,20},{6,22},{8,24},{10,26},{12,28},{14,30},{16,0},... | collective-permute-start | bytes 393224 | tf_op jit(solution)/shard_map/ppermute | solution.py:46
  50.8 1.3 %grad_act.2.refs_4_.refs_6_ = bf16[256,2048]{1,0:T(8,128)(2,1)S(1)} custom-call(bf16[256,512]{1,0:T(8,128)(2,1)S(1)} %get-tuple-element.80.refs_0_, bf16[256,512]{1,0:T(8,128)(2,1)S(1)} %collective-permute-done.18.refs_1_, bf16[2048,1024]{1,0:T(8,128)(2,1)S(1)} %copy-done, bf16[256,512]{1,0:T(8,128)(2,1)S(1)} %get-tuple-element.81.refs_3_.refs_0_), custom_call_target="tpu_custom_call" | custom-call | tf_op jit(solution)/shard_map/grad_act/pallas_call | solution.py:60
  52.1 3.1 %mlp_hidden_and_grad.2 = (bf16[256,2048]{1,0:T(8,128)(2,1)S(1)}, f32[256,512]{1,0:T(8,128)S(1)}, bf16[128,512]{1,0:T(8,128)(2,1)S(1)}, bf16[128,512]{1,0:T(8,128)(2,1)S(1)}) custom-call(bf16[128,512]{1,0:T(8,128)(2,1)S(1)} %get-tuple-element.76.refs_0_.refs_1_, bf16[128,512]{1,0:T(8,128)(2,1)S(1)} %get-tuple-element.77.refs_4_.refs_1_.refs_2_, ...), custom_call_target="tpu_custom_call" | custom-call | tf_op jit(solution)/shard_map/mlp_hidden_and_grad/pallas_call | solution.py:60
  55.3 0.5 collective-permute-start.24
  55.8 1.3 %grad_act.3.refs_4_ = bf16[256,2048]{1,0:T(8,128)(2,1)S(1)} custom-call(bf16[256,512]{1,0:T(8,128)(2,1)S(1)} %get-tuple-element.81.refs_3_.refs_0_, bf16[256,512]{1,0:T(8,128)(2,1)S(1)} %collective-permute-done.19.refs_1_, bf16[2048,1024]{1,0:T(8,128)(2,1)S(1)} %copy-done, bf16[128,512]{1,0:T(8,128)(2,1)S(1)} %get-tuple-element.83.refs_3_), custom_call_target="tpu_custom_call" | custom-call | tf_op jit(solution)/shard_map/grad_act/pallas_call | solution.py:60
  57.1 1.3 %mlp_out.2 = (f32[256,512]{1,0:T(8,128)S(1)}, bf16[256,512]{1,0:T(8,128)(2,1)S(1)}) custom-call(bf16[256,2048]{1,0:T(8,128)(2,1)S(1)} %get-tuple-element.82.refs_0_, bf16[128,512]{1,0:T(8,128)(2,1)S(1)} %get-tuple-element.76.refs_0_.refs_1_, bf16[128,512]{1,0:T(8,128)(2,1)S(1)} %get-tuple-element.77.refs_4_.refs_1_.refs_2_, bf16[2048,1024]{1,0:T(8,128)(2,1)S(1)} %copy-done, ...), custom_call_target="tpu_custom_call" | custom-call | tf_op jit(solution)/shard_map/mlp_out/pallas_call | solution.py:60
  58.8 0.4 collective-permute-start.22
  59.3 0.6 late_and_early_back.2
  59.9 2.0 %collective-permute-start.30 = (bf16[64,512]{1,0:T(8,128)(2,1)S(1)}, bf16[64,512]{1,0:T(8,128)(2,1)S(1)}, u32[]{:S(2)}, u32[]{:S(2)}) collective-permute-start(bf16[64,512]{1,0:T(8,128)(2,1)S(1)} %get-tuple-element.100), channel_id=1, source_target_pairs={{0,8},{2,10},{4,12},{6,14},{8,0},{10,2},{12,4},{14,6},{16,24},{18,... | collective-permute-start | bytes 196616 | tf_op jit(solution)/shard_map/ppermute | solution.py:46
  61.8 1.8 %collective-permute-start.31 = (bf16[64,512]{1,0:T(8,128)(2,1)S(1)}, bf16[64,512]{1,0:T(8,128)(2,1)S(1)}, u32[]{:S(2)}, u32[]{:S(2)}) collective-permute-start(bf16[64,512]{1,0:T(8,128)(2,1)S(1)} %get-tuple-element.101), channel_id=1, source_target_pairs={{0,16},{2,18},{4,20},{6,22},{8,24},{10,26},{12,28},{14,30},{16,0},... | collective-permute-start | bytes 196616 | tf_op jit(solution)/shard_map/ppermute | solution.py:46
  63.7 3.3 %mlp_hidden_and_grad.3 = (bf16[256,2048]{1,0:T(8,128)(2,1)S(1)}, f32[256,512]{1,0:T(8,128)S(1)}, bf16[128,512]{1,0:T(8,128)(2,1)S(1)}, bf16[128,512]{1,0:T(8,128)(2,1)S(1)}) custom-call(bf16[128,512]{1,0:T(8,128)(2,1)S(1)} %get-tuple-element.87.refs_0_.refs_1_, bf16[128,512]{1,0:T(8,128)(2,1)S(1)} %get-tuple-element.88.refs_8_.refs_1_.refs_2_, ...), custom_call_target="tpu_custom_call" | custom-call | tf_op jit(solution)/shard_map/mlp_hidden_and_grad/pallas_call | solution.py:60
  67.5 1.3 %mlp_out.3 = (f32[256,512]{1,0:T(8,128)S(1)}, bf16[128,512]{1,0:T(8,128)(2,1)S(1)}, bf16[128,512]{1,0:T(8,128)(2,1)S(1)}) custom-call(bf16[256,2048]{1,0:T(8,128)(2,1)S(1)} %get-tuple-element.92.refs_0_, bf16[128,512]{1,0:T(8,128)(2,1)S(1)} %get-tuple-element.87.refs_0_.refs_1_, bf16[128,512]{1,0:T(8,128)(2,1)S(1)} %get-tuple-element.88.refs_8_.refs_1_.refs_2_, ...), custom_call_target="tpu_custom_call" | custom-call | tf_op jit(solution)/shard_map/mlp_out/pallas_call | solution.py:60
  69.1 1.1 collective-permute-done.32.refs_3_
  70.6 0.6 late_and_early_back.3
  71.2 1.8 %collective-permute-start.37 = (bf16[64,512]{1,0:T(8,128)(2,1)S(1)}, bf16[64,512]{1,0:T(8,128)(2,1)S(1)}, u32[]{:S(2)}, u32[]{:S(2)}) collective-permute-start(bf16[64,512]{1,0:T(8,128)(2,1)S(1)} %get-tuple-element.110), channel_id=1, source_target_pairs={{0,8},{2,10},{4,12},{6,14},{8,0},{10,2},{12,4},{14,6},{16,24},{18,... | collective-permute-start | bytes 196616 | tf_op jit(solution)/shard_map/ppermute | solution.py:46
  73.0 1.5 %collective-permute-start.38 = (bf16[64,512]{1,0:T(8,128)(2,1)S(1)}, bf16[64,512]{1,0:T(8,128)(2,1)S(1)}, u32[]{:S(2)}, u32[]{:S(2)}) collective-permute-start(bf16[64,512]{1,0:T(8,128)(2,1)S(1)} %get-tuple-element.111), channel_id=1, source_target_pairs={{0,16},{2,18},{4,20},{6,22},{8,24},{10,26},{12,28},{14,30},{16,0},... | collective-permute-start | bytes 196616 | tf_op jit(solution)/shard_map/ppermute | solution.py:46
  74.8 1.4 %collective-permute-start.36 = (bf16[4,64,512]{2,1,0:T(8,128)(2,1)S(1)}, bf16[4,64,512]{2,1,0:T(8,128)(2,1)S(1)}, u32[]{:S(2)}, u32[]{:S(2)}) collective-permute-start(bf16[4,64,512]{2,1,0:T(8,128)(2,1)S(1)} %get-tuple-element.102.refs_8_), channel_id=1, source_target_pairs={{0,4},{2,6},{4,0},{6,2},{8,12},{10,14},{12,8},{14,10},{16,20},{18,... | collective-permute-start | bytes 786440 | tf_op jit(solution)/shard_map/ppermute | solution.py:46
  76.3 2.7 %collective-permute-done.38.refs_2_ = bf16[64,512]{1,0:T(8,128)(2,1)S(1)} collective-permute-done((bf16[64,512]{1,0:T(8,128)(2,1)S(1)}, bf16[64,512]{1,0:T(8,128)(2,1)S(1)}, u32[]{:S(2)}, u32[]{:S(2)}) %collective-permute-start.38) | collective-permute-done | bytes 65568 | tf_op jit(solution)/shard_map/ppermute | solution.py:46
  79.0 2.2 %collective-permute-done.39.refs_3_ = bf16[64,512]{1,0:T(8,128)(2,1)S(1)} collective-permute-done((bf16[64,512]{1,0:T(8,128)(2,1)S(1)}, bf16[64,512]{1,0:T(8,128)(2,1)S(1)}, u32[]{:S(2)}, u32[]{:S(2)}) %collective-permute-start.39) | collective-permute-done | bytes 65568 | tf_op jit(solution)/shard_map/ppermute | solution.py:46
  81.5 1.4 %collective-permute-start.41 = (bf16[4,64,512]{2,1,0:T(8,128)(2,1)S(1)}, bf16[4,64,512]{2,1,0:T(8,128)(2,1)S(1)}, u32[]{:S(2)}, u32[]{:S(2)}) collective-permute-start(bf16[4,64,512]{2,1,0:T(8,128)(2,1)S(1)} %get-tuple-element.112.refs_3_), channel_id=1, source_target_pairs={{0,4},{2,6},{4,0},{6,2},{8,12},{10,14},{12,8},{14,10},{16,20},{18,... | collective-permute-start | bytes 786440 | tf_op jit(solution)/shard_map/ppermute | solution.py:46
  83.3 1.3 %collective-permute-start.40 = (bf16[4,64,512]{2,1,0:T(8,128)(2,1)S(1)}, bf16[4,64,512]{2,1,0:T(8,128)(2,1)S(1)}, u32[]{:S(2)}, u32[]{:S(2)}) collective-permute-start(bf16[4,64,512]{2,1,0:T(8,128)(2,1)S(1)} %get-tuple-element.114.refs_3_), channel_id=1, source_target_pairs={{0,2},{2,0},{4,6},{6,4},{8,10},{10,8},{12,14},{14,12},{16,18},{18,... | collective-permute-start | bytes 786440 | tf_op jit(solution)/shard_map/ppermute | solution.py:46
  84.6 4.9 %collective-permute-done.41.refs_1_ = bf16[4,64,512]{2,1,0:T(8,128)(2,1)S(1)} collective-permute-done((bf16[4,64,512]{2,1,0:T(8,128)(2,1)S(1)}, bf16[4,64,512]{2,1,0:T(8,128)(2,1)S(1)}, u32[]{:S(2)}, u32[]{:S(2)}) %collective-permute-start.41) | collective-permute-done | bytes 262176 | tf_op jit(solution)/shard_map/ppermute | solution.py:46
  89.9 1.3 %collective-permute-start.42 = (bf16[4,64,512]{2,1,0:T(8,128)(2,1)S(1)}, bf16[4,64,512]{2,1,0:T(8,128)(2,1)S(1)}, u32[]{:S(2)}, u32[]{:S(2)}) collective-permute-start(bf16[4,64,512]{2,1,0:T(8,128)(2,1)S(1)} %get-tuple-element.116.refs_3_), channel_id=1, source_target_pairs={{0,2},{2,0},{4,6},{6,4},{8,10},{10,8},{12,14},{14,12},{16,18},{18,... | collective-permute-start | bytes 786440 | tf_op jit(solution)/shard_map/ppermute | solution.py:46
  91.2 0.9 collective-permute-start.33
  92.0 2.2 %collective-permute-start.34 = (bf16[2,64,512]{2,1,0:T(8,128)(2,1)S(1)}, bf16[2,64,512]{2,1,0:T(8,128)(2,1)S(1)}, u32[]{:S(2)}, u32[]{:S(2)}) collective-permute-start(bf16[2,64,512]{2,1,0:T(8,128)(2,1)S(1)} %get-tuple-element.106), channel_id=1, source_target_pairs={{0,16},{2,18},{4,20},{6,22},{8,24},{10,26},{12,28},{14,30},{16,0},... | collective-permute-start | bytes 393224 | tf_op jit(solution)/shard_map/ppermute | solution.py:46
  94.2 0.4 collective-permute-start.35
  95.0 1.9 %collective-permute-done.42.refs_1_ = bf16[4,64,512]{2,1,0:T(8,128)(2,1)S(1)} collective-permute-done((bf16[4,64,512]{2,1,0:T(8,128)(2,1)S(1)}, bf16[4,64,512]{2,1,0:T(8,128)(2,1)S(1)}, u32[]{:S(2)}, u32[]{:S(2)}) %collective-permute-start.42) | collective-permute-done | bytes 262176 | tf_op jit(solution)/shard_map/ppermute | solution.py:46
  97.3 1.2 %local_factors_back.1 = (bf16[512,512]{1,0:T(8,128)(2,1)S(1)}, bf16[2,512]{1,0:T(2,128)(2,1)S(1)}) custom-call(s32[2,8]{1,0:T(2,128)S(1)} %get-tuple-element.65.refs_0_.refs_5_, f32[4,64,512]{2,1,0:T(8,128)S(1)} %get-tuple-element.117.refs_1_, f32[4,64,512]{2,1,0:T(8,128)S(1)} %get-tuple-element.120.refs_2_, f32[4,64,512]{2,1,0:T(8,128)S(1)} %get-tuple-element.119.refs_3_, ...), custom_call_target="tpu_custom_call" | custom-call | tf_op jit(solution)/shard_map/local_factors_back/pallas_call | solution.py:60
  98.5 3.2 %collective-permute-start.43 = (bf16[2,512]{1,0:T(2,128)(2,1)S(1)}, bf16[2,512]{1,0:T(2,128)(2,1)S(1)}, u32[]{:S(2)}, u32[]{:S(2)}) collective-permute-start(bf16[2,512]{1,0:T(2,128)(2,1)S(1)} %get-tuple-element.123.refs_4_), channel_id=1, source_target_pairs={{2,4},{4,2},{6,8},{8,6},{10,12},{12,10},{14,16},{16,14},{18,20},{2... | collective-permute-start | bytes 6152 | tf_op jit(solution)/shard_map/ppermute | solution.py:41
  101.6 1.5 %collective-permute-start.44 = (bf16[2,512]{1,0:T(2,128)(2,1)S(1)}, bf16[2,512]{1,0:T(2,128)(2,1)S(1)}, u32[]{:S(2)}, u32[]{:S(2)}) collective-permute-start(bf16[2,512]{1,0:T(2,128)(2,1)S(1)} %get-tuple-element.123.refs_4_), channel_id=1, source_target_pairs={{0,2},{2,0},{4,6},{6,4},{8,10},{10,8},{12,14},{14,12},{16,18},{18,... | collective-permute-start | bytes 6152 | tf_op jit(solution)/shard_map/ppermute | solution.py:37
  103.1 2.6 %collective-permute-done.43.refs_1_ = bf16[2,512]{1,0:T(2,128)(2,1)S(1)} collective-permute-done((bf16[2,512]{1,0:T(2,128)(2,1)S(1)}, bf16[2,512]{1,0:T(2,128)(2,1)S(1)}, u32[]{:S(2)}, u32[]{:S(2)}) %collective-permute-start.43) | collective-permute-done | bytes 2080 | tf_op jit(solution)/shard_map/ppermute | solution.py:41
  105.7 1.2 %conv_back.1 = (bf16[512,512]{1,0:T(8,128)(2,1)}, f32[8,128]{1,0:T(8,128)S(1)}) custom-call(bf16[512,512]{1,0:T(8,128)(2,1)S(1)} %get-tuple-element.122.refs_0_, bf16[2,512]{1,0:T(2,128)(2,1)S(1)} %collective-permute-done.43.refs_1_, bf16[2,512]{1,0:T(2,128)(2,1)S(1)} %collective-permute-done.44.refs_2_, bf16[5,512]{1,0:T(8,128)(2,1)S(1)} %collective-permute-done.1.refs_3_, ...), custom_call_target="tpu_custom_call" | custom-call | tf_op jit(solution)/shard_map/conv_back/pallas_call | solution.py:60
  106.9 0.8 assemble.1
  (76 shorter events, 7.9 us)
Async XLA Ops:
  2.1 7.8 %collective-permute-start.1 = (bf16[5,512]{1,0:T(8,128)(2,1)S(1)}, bf16[5,512]{1,0:T(8,128)(2,1)S(1)}, u32[]{:S(2)}, u32[]{:S(2)}) collective-permute-start(bf16[5,512]{1,0:T(8,128)(2,1)S(1)} %pad_maximum_fusion), channel_id=1, source_target_pairs={{0,2},{2,0},{4,6},{6,4},{8,10},{10,8},{12,14},{14,12},{16,18},{18,... | collective-permute-start | bytes 15368 | tf_op jit(solution)/shard_map/ppermute | solution.py:37
  3.6 7.3 %collective-permute-start = (bf16[5,512]{1,0:T(8,128)(2,1)S(1)}, bf16[5,512]{1,0:T(8,128)(2,1)S(1)}, u32[]{:S(2)}, u32[]{:S(2)}) collective-permute-start(bf16[5,512]{1,0:T(8,128)(2,1)S(1)} %pad_maximum_fusion), channel_id=1, source_target_pairs={{2,4},{4,2},{6,8},{8,6},{10,12},{12,10},{14,16},{16,14},{18,20},{2... | collective-permute-start | bytes 15368 | tf_op jit(solution)/shard_map/ppermute | solution.py:41
  6.9 1.1 %copy-start.2 = (bf16[6,8,64,128]{3,2,1,0:T(8,128)(2,1)S(1)}, bf16[6,8,64,128]{3,2,1,0:T(8,128)(2,1)}, u32[]{:S(2)}) copy-start(bf16[6,8,64,128]{3,2,1,0:T(8,128)(2,1)} %refs_0_.1) | copy-start | bytes 2359300
  8.0 1.0 copy-start.3
  9.1 0.7 copy-start.5
  13.1 5.9 %collective-permute-start.3 = (bf16[2,64,512]{2,1,0:T(8,128)(2,1)S(1)}, bf16[2,64,512]{2,1,0:T(8,128)(2,1)S(1)}, u32[]{:S(2)}, u32[]{:S(2)}) collective-permute-start(bf16[2,64,512]{2,1,0:T(8,128)(2,1)S(1)} %get-tuple-element.69.refs_0_), channel_id=1, source_target_pairs={{0,2},{2,0},{4,6},{6,4},{8,10},{10,8},{12,14},{14,12},{16,18},{18,... | collective-permute-start | bytes 393224 | tf_op jit(solution)/shard_map/ppermute | solution.py:46
  13.7 1.0 copy-start.4
  14.8 19.9 %collective-permute-start.12 = (bf16[6,64,512]{2,1,0:T(8,128)(2,1)S(1)}, bf16[6,64,512]{2,1,0:T(8,128)(2,1)S(1)}, u32[]{:S(2)}, u32[]{:S(2)}) collective-permute-start(bf16[6,64,512]{2,1,0:T(8,128)(2,1)S(1)} %get-tuple-element.71.refs_3_), channel_id=1, source_target_pairs={{0,16},{2,18},{4,20},{6,22},{8,24},{10,26},{12,28},{14,30},{16,0},... | collective-permute-start | bytes 1179656 | tf_op jit(solution)/shard_map/ppermute | solution.py:46
  17.4 5.9 %collective-permute-start.2 = (bf16[2,64,512]{2,1,0:T(8,128)(2,1)S(1)}, bf16[2,64,512]{2,1,0:T(8,128)(2,1)S(1)}, u32[]{:S(2)}, u32[]{:S(2)}) collective-permute-start(bf16[2,64,512]{2,1,0:T(8,128)(2,1)S(1)} %get-tuple-element.68.refs_0_), channel_id=1, source_target_pairs={{0,2},{2,0},{4,6},{6,4},{8,10},{10,8},{12,14},{14,12},{16,18},{18,... | collective-permute-start | bytes 393224 | tf_op jit(solution)/shard_map/ppermute | solution.py:46
  19.2 6.1 %collective-permute-start.6 = (bf16[2,64,512]{2,1,0:T(8,128)(2,1)S(1)}, bf16[2,64,512]{2,1,0:T(8,128)(2,1)S(1)}, u32[]{:S(2)}, u32[]{:S(2)}) collective-permute-start(bf16[2,64,512]{2,1,0:T(8,128)(2,1)S(1)} %factor.8.refs_3_.refs_0_), channel_id=1, source_target_pairs={{0,4},{2,6},{4,0},{6,2},{8,12},{10,14},{12,8},{14,10},{16,20},{18,... | collective-permute-start | bytes 393224 | tf_op jit(solution)/shard_map/ppermute | solution.py:46
  19.9 13.1 %collective-permute-start.8 = (bf16[4,64,512]{2,1,0:T(8,128)(2,1)S(1)}, bf16[4,64,512]{2,1,0:T(8,128)(2,1)S(1)}, u32[]{:S(2)}, u32[]{:S(2)}) collective-permute-start(bf16[4,64,512]{2,1,0:T(8,128)(2,1)S(1)} %get-tuple-element.73), channel_id=1, source_target_pairs={{0,8},{2,10},{4,12},{6,14},{8,0},{10,2},{12,4},{14,6},{16,24},{18,... | collective-permute-start | bytes 786440 | tf_op jit(solution)/shard_map/ppermute | solution.py:46
  20.3 6.1 %collective-permute-start.5 = (bf16[2,64,512]{2,1,0:T(8,128)(2,1)S(1)}, bf16[2,64,512]{2,1,0:T(8,128)(2,1)S(1)}, u32[]{:S(2)}, u32[]{:S(2)}) collective-permute-start(bf16[2,64,512]{2,1,0:T(8,128)(2,1)S(1)} %get-tuple-element.72.refs_0_), channel_id=1, source_target_pairs={{0,2},{2,0},{4,6},{6,4},{8,10},{10,8},{12,14},{14,12},{16,18},{18,... | collective-permute-start | bytes 393224 | tf_op jit(solution)/shard_map/ppermute | solution.py:46
  23.6 5.3 %collective-permute-start.4 = (bf16[2,64,512]{2,1,0:T(8,128)(2,1)S(1)}, bf16[2,64,512]{2,1,0:T(8,128)(2,1)S(1)}, u32[]{:S(2)}, u32[]{:S(2)}) collective-permute-start(bf16[2,64,512]{2,1,0:T(8,128)(2,1)S(1)} %factor.9.refs_3_.refs_0_), channel_id=1, source_target_pairs={{0,4},{2,6},{4,0},{6,2},{8,12},{10,14},{12,8},{14,10},{16,20},{18,... | collective-permute-start | bytes 393224 | tf_op jit(solution)/shard_map/ppermute | solution.py:46
  25.6 8.7 %collective-permute-start.7 = (bf16[2,64,512]{2,1,0:T(8,128)(2,1)S(1)}, bf16[2,64,512]{2,1,0:T(8,128)(2,1)S(1)}, u32[]{:S(2)}, u32[]{:S(2)}) collective-permute-start(bf16[2,64,512]{2,1,0:T(8,128)(2,1)S(1)} %factor.10.refs_3_), channel_id=1, source_target_pairs={{0,8},{2,10},{4,12},{6,14},{8,0},{10,2},{12,4},{14,6},{16,24},{18,... | collective-permute-start | bytes 393224 | tf_op jit(solution)/shard_map/ppermute | solution.py:46
  26.4 13.6 %collective-permute-start.11 = (bf16[2,64,512]{2,1,0:T(8,128)(2,1)S(1)}, bf16[2,64,512]{2,1,0:T(8,128)(2,1)S(1)}, u32[]{:S(2)}, u32[]{:S(2)}) collective-permute-start(bf16[2,64,512]{2,1,0:T(8,128)(2,1)S(1)} %get-tuple-element.70.refs_2_.refs_0_), channel_id=1, source_target_pairs={{0,2},{2,0},{4,6},{6,4},{8,10},{10,8},{12,14},{14,12},{16,18},{18,... | collective-permute-start | bytes 393224 | tf_op jit(solution)/shard_map/ppermute | solution.py:46
  29.0 13.9 %collective-permute-start.10 = (bf16[2,64,512]{2,1,0:T(8,128)(2,1)S(1)}, bf16[2,64,512]{2,1,0:T(8,128)(2,1)S(1)}, u32[]{:S(2)}, u32[]{:S(2)}) collective-permute-start(bf16[2,64,512]{2,1,0:T(8,128)(2,1)S(1)} %factor.11.refs_3_.refs_0_), channel_id=1, source_target_pairs={{0,4},{2,6},{4,0},{6,2},{8,12},{10,14},{12,8},{14,10},{16,20},{18,... | collective-permute-start | bytes 393224 | tf_op jit(solution)/shard_map/ppermute | solution.py:46
  34.7 16.0 %copy-start = (bf16[2048,1024]{1,0:T(8,128)(2,1)S(1)}, bf16[2048,1024]{1,0:T(8,128)(2,1)}, u32[]{:S(2)}) copy-start(bf16[2048,1024]{1,0:T(8,128)(2,1)} %refs_3_.3) | copy-start | bytes 12582916
  34.8 11.7 %collective-permute-start.13 = (bf16[3,64,512]{2,1,0:T(8,128)(2,1)S(1)}, bf16[3,64,512]{2,1,0:T(8,128)(2,1)S(1)}, u32[]{:S(2)}, u32[]{:S(2)}) collective-permute-start(bf16[3,64,512]{2,1,0:T(8,128)(2,1)S(1)} %forward.1.refs_3_), channel_id=1, source_target_pairs={{0,8},{2,10},{4,12},{6,14},{8,0},{10,2},{12,4},{14,6},{16,24},{18,... | collective-permute-start | bytes 589832 | tf_op jit(solution)/shard_map/ppermute | solution.py:46
  37.3 8.9 %collective-permute-start.9 = (bf16[2,64,512]{2,1,0:T(8,128)(2,1)S(1)}, bf16[2,64,512]{2,1,0:T(8,128)(2,1)S(1)}, u32[]{:S(2)}, u32[]{:S(2)}) collective-permute-start(bf16[2,64,512]{2,1,0:T(8,128)(2,1)S(1)} %get-tuple-element.75.refs_1_), channel_id=1, source_target_pairs={{0,16},{2,18},{4,20},{6,22},{8,24},{10,26},{12,28},{14,30},{16,0},... | collective-permute-start | bytes 393224 | tf_op jit(solution)/shard_map/ppermute | solution.py:46
  40.3 5.9 %collective-permute-start.14 = (bf16[2,64,512]{2,1,0:T(8,128)(2,1)S(1)}, bf16[2,64,512]{2,1,0:T(8,128)(2,1)S(1)}, u32[]{:S(2)}, u32[]{:S(2)}) collective-permute-start(bf16[2,64,512]{2,1,0:T(8,128)(2,1)S(1)} %factor.13.refs_3_.refs_0_), channel_id=1, source_target_pairs={{0,4},{2,6},{4,0},{6,2},{8,12},{10,14},{12,8},{14,10},{16,20},{18,... | collective-permute-start | bytes 393224 | tf_op jit(solution)/shard_map/ppermute | solution.py:46
  43.1 5.0 %collective-permute-start.17 = (bf16[2,64,512]{2,1,0:T(8,128)(2,1)S(1)}, bf16[2,64,512]{2,1,0:T(8,128)(2,1)S(1)}, u32[]{:S(2)}, u32[]{:S(2)}) collective-permute-start(bf16[2,64,512]{2,1,0:T(8,128)(2,1)S(1)} %factor.14.refs_1_), channel_id=1, source_target_pairs={{0,8},{2,10},{4,12},{6,14},{8,0},{10,2},{12,4},{14,6},{16,24},{18,... | collective-permute-start | bytes 393224 | tf_op jit(solution)/shard_map/ppermute | solution.py:46
  48.1 4.0 %copy-start.1 = (bf16[1024,2048]{1,0:T(8,128)(2,1)S(1)}, bf16[1024,2048]{1,0:T(8,128)(2,1)}, u32[]{:S(2)}) copy-start(bf16[1024,2048]{1,0:T(8,128)(2,1)} %refs_5_.3) | copy-start | bytes 12582916
  48.5 2.2 %collective-permute-start.18 = (bf16[256,512]{1,0:T(8,128)(2,1)S(1)}, bf16[256,512]{1,0:T(8,128)(2,1)S(1)}, u32[]{:S(2)}, u32[]{:S(2)}) collective-permute-start(bf16[256,512]{1,0:T(8,128)(2,1)S(1)} %get-tuple-element.80.refs_0_), channel_id=1, source_target_pairs={{1,0},{0,1},{3,2},{2,3},{5,4},{4,5},{7,6},{6,7},{9,8},{8,9},{11,10... | collective-permute-start | bytes 786440 | tf_op jit(solution)/shard_map/ppermute | solution.py:51
  48.6 7.2 %collective-permute-start.19 = (bf16[256,512]{1,0:T(8,128)(2,1)S(1)}, bf16[256,512]{1,0:T(8,128)(2,1)S(1)}, u32[]{:S(2)}, u32[]{:S(2)}) collective-permute-start(bf16[256,512]{1,0:T(8,128)(2,1)S(1)} %get-tuple-element.81.refs_3_.refs_0_), channel_id=1, source_target_pairs={{1,0},{0,1},{3,2},{2,3},{5,4},{4,5},{7,6},{6,7},{9,8},{8,9},{11,10... | collective-permute-start | bytes 786440 | tf_op jit(solution)/shard_map/ppermute | solution.py:51
  49.1 3.0 %collective-permute-start.15 = (bf16[128,512]{1,0:T(8,128)(2,1)S(1)}, bf16[128,512]{1,0:T(8,128)(2,1)S(1)}, u32[]{:S(2)}, u32[]{:S(2)}) collective-permute-start(bf16[128,512]{1,0:T(8,128)(2,1)S(1)} %get-tuple-element.76.refs_0_.refs_1_), channel_id=1, source_target_pairs={{1,0},{0,1},{3,2},{2,3},{5,4},{4,5},{7,6},{6,7},{9,8},{8,9},{11,10... | collective-permute-start | bytes 393224 | tf_op jit(solution)/shard_map/ppermute | solution.py:51
  49.2 2.9 %collective-permute-start.16 = (bf16[128,512]{1,0:T(8,128)(2,1)S(1)}, bf16[128,512]{1,0:T(8,128)(2,1)S(1)}, u32[]{:S(2)}, u32[]{:S(2)}) collective-permute-start(bf16[128,512]{1,0:T(8,128)(2,1)S(1)} %get-tuple-element.77.refs_4_.refs_1_.refs_2_), channel_id=1, source_target_pairs={{1,0},{0,1},{3,2},{2,3},{5,4},{4,5},{7,6},{6,7},{9,8},{8,9},{11,10... | collective-permute-start | bytes 393224 | tf_op jit(solution)/shard_map/ppermute | solution.py:51
  49.6 8.7 %collective-permute-start.20 = (bf16[2,64,512]{2,1,0:T(8,128)(2,1)S(1)}, bf16[2,64,512]{2,1,0:T(8,128)(2,1)S(1)}, u32[]{:S(2)}, u32[]{:S(2)}) collective-permute-start(bf16[2,64,512]{2,1,0:T(8,128)(2,1)S(1)} %get-tuple-element.79.refs_4_), channel_id=1, source_target_pairs={{0,16},{2,18},{4,20},{6,22},{8,24},{10,26},{12,28},{14,30},{16,0},... | collective-permute-start | bytes 393224 | tf_op jit(solution)/shard_map/ppermute | solution.py:46
  55.2 4.1 %collective-permute-start.23 = (bf16[128,512]{1,0:T(8,128)(2,1)S(1)}, bf16[128,512]{1,0:T(8,128)(2,1)S(1)}, u32[]{:S(2)}, u32[]{:S(2)}) collective-permute-start(bf16[128,512]{1,0:T(8,128)(2,1)S(1)} %get-tuple-element.90), channel_id=1, source_target_pairs={{1,0},{0,1},{3,2},{2,3},{5,4},{4,5},{7,6},{6,7},{9,8},{8,9},{11,10... | collective-permute-start | bytes 393224 | tf_op jit(solution)/shard_map/ppermute | solution.py:51
  55.3 4.0 %collective-permute-start.24 = (bf16[128,512]{1,0:T(8,128)(2,1)S(1)}, bf16[128,512]{1,0:T(8,128)(2,1)S(1)}, u32[]{:S(2)}, u32[]{:S(2)}) collective-permute-start(bf16[128,512]{1,0:T(8,128)(2,1)S(1)} %get-tuple-element.83.refs_3_), channel_id=1, source_target_pairs={{1,0},{0,1},{3,2},{2,3},{5,4},{4,5},{7,6},{6,7},{9,8},{8,9},{11,10... | collective-permute-start | bytes 393224 | tf_op jit(solution)/shard_map/ppermute | solution.py:51
  58.7 4.9 %collective-permute-start.21 = (bf16[128,512]{1,0:T(8,128)(2,1)S(1)}, bf16[128,512]{1,0:T(8,128)(2,1)S(1)}, u32[]{:S(2)}, u32[]{:S(2)}) collective-permute-start(bf16[128,512]{1,0:T(8,128)(2,1)S(1)} %get-tuple-element.87.refs_0_.refs_1_), channel_id=1, source_target_pairs={{1,0},{0,1},{3,2},{2,3},{5,4},{4,5},{7,6},{6,7},{9,8},{8,9},{11,10... | collective-permute-start | bytes 393224 | tf_op jit(solution)/shard_map/ppermute | solution.py:51
  58.8 4.8 %collective-permute-start.22 = (bf16[128,512]{1,0:T(8,128)(2,1)S(1)}, bf16[128,512]{1,0:T(8,128)(2,1)S(1)}, u32[]{:S(2)}, u32[]{:S(2)}) collective-permute-start(bf16[128,512]{1,0:T(8,128)(2,1)S(1)} %get-tuple-element.88.refs_8_.refs_1_.refs_2_), channel_id=1, source_target_pairs={{1,0},{0,1},{3,2},{2,3},{5,4},{4,5},{7,6},{6,7},{9,8},{8,9},{11,10... | collective-permute-start | bytes 393224 | tf_op jit(solution)/shard_map/ppermute | solution.py:51
  59.9 7.4 %collective-permute-start.30 = (bf16[64,512]{1,0:T(8,128)(2,1)S(1)}, bf16[64,512]{1,0:T(8,128)(2,1)S(1)}, u32[]{:S(2)}, u32[]{:S(2)}) collective-permute-start(bf16[64,512]{1,0:T(8,128)(2,1)S(1)} %get-tuple-element.100), channel_id=1, source_target_pairs={{0,8},{2,10},{4,12},{6,14},{8,0},{10,2},{12,4},{14,6},{16,24},{18,... | collective-permute-start | bytes 196616 | tf_op jit(solution)/shard_map/ppermute | solution.py:46
  61.8 14.3 %collective-permute-start.25 = (bf16[256,512]{1,0:T(8,128)(2,1)S(1)}, bf16[256,512]{1,0:T(8,128)(2,1)S(1)}, u32[]{:S(2)}, u32[]{:S(2)}) collective-permute-start(bf16[256,512]{1,0:T(8,128)(2,1)S(1)} %get-tuple-element.86.refs_6_), channel_id=1, source_target_pairs={{1,0},{0,1},{3,2},{2,3},{5,4},{4,5},{7,6},{6,7},{9,8},{8,9},{11,10... | collective-permute-start | bytes 786440 | tf_op jit(solution)/shard_map/ppermute | solution.py:51
  61.8 7.0 %collective-permute-start.31 = (bf16[64,512]{1,0:T(8,128)(2,1)S(1)}, bf16[64,512]{1,0:T(8,128)(2,1)S(1)}, u32[]{:S(2)}, u32[]{:S(2)}) collective-permute-start(bf16[64,512]{1,0:T(8,128)(2,1)S(1)} %get-tuple-element.101), channel_id=1, source_target_pairs={{0,16},{2,18},{4,20},{6,22},{8,24},{10,26},{12,28},{14,30},{16,0},... | collective-permute-start | bytes 196616 | tf_op jit(solution)/shard_map/ppermute | solution.py:46
  63.6 6.5 %collective-permute-start.32 = (bf16[64,512]{1,0:T(8,128)(2,1)S(1)}, bf16[64,512]{1,0:T(8,128)(2,1)S(1)}, u32[]{:S(2)}, u32[]{:S(2)}) collective-permute-start(bf16[64,512]{1,0:T(8,128)(2,1)S(1)} %get-tuple-element.91.refs_6_), channel_id=1, source_target_pairs={{0,24},{2,26},{4,28},{6,30},{8,16},{10,18},{12,20},{14,22},{16,8},... | collective-permute-start | bytes 196616 | tf_op jit(solution)/shard_map/ppermute | solution.py:46
  66.9 3.7 %collective-permute-start.28 = (bf16[128,512]{1,0:T(8,128)(2,1)S(1)}, bf16[128,512]{1,0:T(8,128)(2,1)S(1)}, u32[]{:S(2)}, u32[]{:S(2)}) collective-permute-start(bf16[128,512]{1,0:T(8,128)(2,1)S(1)} %get-tuple-element.98), channel_id=1, source_target_pairs={{1,0},{0,1},{3,2},{2,3},{5,4},{4,5},{7,6},{6,7},{9,8},{8,9},{11,10... | collective-permute-start | bytes 393224 | tf_op jit(solution)/shard_map/ppermute | solution.py:51
  67.2 3.4 %collective-permute-start.29 = (bf16[128,512]{1,0:T(8,128)(2,1)S(1)}, bf16[128,512]{1,0:T(8,128)(2,1)S(1)}, u32[]{:S(2)}, u32[]{:S(2)}) collective-permute-start(bf16[128,512]{1,0:T(8,128)(2,1)S(1)} %get-tuple-element.93.refs_4_), channel_id=1, source_target_pairs={{1,0},{0,1},{3,2},{2,3},{5,4},{4,5},{7,6},{6,7},{9,8},{8,9},{11,10... | collective-permute-start | bytes 393224 | tf_op jit(solution)/shard_map/ppermute | solution.py:51
  68.8 5.6 %collective-permute-start.26 = (bf16[128,512]{1,0:T(8,128)(2,1)S(1)}, bf16[128,512]{1,0:T(8,128)(2,1)S(1)}, u32[]{:S(2)}, u32[]{:S(2)}) collective-permute-start(bf16[128,512]{1,0:T(8,128)(2,1)S(1)} %get-tuple-element.95), channel_id=1, source_target_pairs={{1,0},{0,1},{3,2},{2,3},{5,4},{4,5},{7,6},{6,7},{9,8},{8,9},{11,10... | collective-permute-start | bytes 393224 | tf_op jit(solution)/shard_map/ppermute | solution.py:51
  70.2 4.6 %collective-permute-start.27 = (bf16[128,512]{1,0:T(8,128)(2,1)S(1)}, bf16[128,512]{1,0:T(8,128)(2,1)S(1)}, u32[]{:S(2)}, u32[]{:S(2)}) collective-permute-start(bf16[128,512]{1,0:T(8,128)(2,1)S(1)} %get-tuple-element.96.refs_5_), channel_id=1, source_target_pairs={{1,0},{0,1},{3,2},{2,3},{5,4},{4,5},{7,6},{6,7},{9,8},{8,9},{11,10... | collective-permute-start | bytes 393224 | tf_op jit(solution)/shard_map/ppermute | solution.py:51
  71.2 5.1 %collective-permute-start.37 = (bf16[64,512]{1,0:T(8,128)(2,1)S(1)}, bf16[64,512]{1,0:T(8,128)(2,1)S(1)}, u32[]{:S(2)}, u32[]{:S(2)}) collective-permute-start(bf16[64,512]{1,0:T(8,128)(2,1)S(1)} %get-tuple-element.110), channel_id=1, source_target_pairs={{0,8},{2,10},{4,12},{6,14},{8,0},{10,2},{12,4},{14,6},{16,24},{18,... | collective-permute-start | bytes 196616 | tf_op jit(solution)/shard_map/ppermute | solution.py:46
  73.0 6.0 %collective-permute-start.38 = (bf16[64,512]{1,0:T(8,128)(2,1)S(1)}, bf16[64,512]{1,0:T(8,128)(2,1)S(1)}, u32[]{:S(2)}, u32[]{:S(2)}) collective-permute-start(bf16[64,512]{1,0:T(8,128)(2,1)S(1)} %get-tuple-element.111), channel_id=1, source_target_pairs={{0,16},{2,18},{4,20},{6,22},{8,24},{10,26},{12,28},{14,30},{16,0},... | collective-permute-start | bytes 196616 | tf_op jit(solution)/shard_map/ppermute | solution.py:46
  74.4 6.8 %collective-permute-start.39 = (bf16[64,512]{1,0:T(8,128)(2,1)S(1)}, bf16[64,512]{1,0:T(8,128)(2,1)S(1)}, u32[]{:S(2)}, u32[]{:S(2)}) collective-permute-start(bf16[64,512]{1,0:T(8,128)(2,1)S(1)} %get-tuple-element.103.refs_5_), channel_id=1, source_target_pairs={{0,24},{2,26},{4,28},{6,30},{8,16},{10,18},{12,20},{14,22},{16,8},... | collective-permute-start | bytes 196616 | tf_op jit(solution)/shard_map/ppermute | solution.py:46
  74.8 8.2 %collective-permute-start.36 = (bf16[4,64,512]{2,1,0:T(8,128)(2,1)S(1)}, bf16[4,64,512]{2,1,0:T(8,128)(2,1)S(1)}, u32[]{:S(2)}, u32[]{:S(2)}) collective-permute-start(bf16[4,64,512]{2,1,0:T(8,128)(2,1)S(1)} %get-tuple-element.102.refs_8_), channel_id=1, source_target_pairs={{0,4},{2,6},{4,0},{6,2},{8,12},{10,14},{12,8},{14,10},{16,20},{18,... | collective-permute-start | bytes 786440 | tf_op jit(solution)/shard_map/ppermute | solution.py:46
  81.5 8.0 %collective-permute-start.41 = (bf16[4,64,512]{2,1,0:T(8,128)(2,1)S(1)}, bf16[4,64,512]{2,1,0:T(8,128)(2,1)S(1)}, u32[]{:S(2)}, u32[]{:S(2)}) collective-permute-start(bf16[4,64,512]{2,1,0:T(8,128)(2,1)S(1)} %get-tuple-element.112.refs_3_), channel_id=1, source_target_pairs={{0,4},{2,6},{4,0},{6,2},{8,12},{10,14},{12,8},{14,10},{16,20},{18,... | collective-permute-start | bytes 786440 | tf_op jit(solution)/shard_map/ppermute | solution.py:46
  83.3 11.4 %collective-permute-start.40 = (bf16[4,64,512]{2,1,0:T(8,128)(2,1)S(1)}, bf16[4,64,512]{2,1,0:T(8,128)(2,1)S(1)}, u32[]{:S(2)}, u32[]{:S(2)}) collective-permute-start(bf16[4,64,512]{2,1,0:T(8,128)(2,1)S(1)} %get-tuple-element.114.refs_3_), channel_id=1, source_target_pairs={{0,2},{2,0},{4,6},{6,4},{8,10},{10,8},{12,14},{14,12},{16,18},{18,... | collective-permute-start | bytes 786440 | tf_op jit(solution)/shard_map/ppermute | solution.py:46
  89.9 7.1 %collective-permute-start.42 = (bf16[4,64,512]{2,1,0:T(8,128)(2,1)S(1)}, bf16[4,64,512]{2,1,0:T(8,128)(2,1)S(1)}, u32[]{:S(2)}, u32[]{:S(2)}) collective-permute-start(bf16[4,64,512]{2,1,0:T(8,128)(2,1)S(1)} %get-tuple-element.116.refs_3_), channel_id=1, source_target_pairs={{0,2},{2,0},{4,6},{6,4},{8,10},{10,8},{12,14},{14,12},{16,18},{18,... | collective-permute-start | bytes 786440 | tf_op jit(solution)/shard_map/ppermute | solution.py:46
  91.2 15.7 %collective-permute-start.33 = (bf16[2,64,512]{2,1,0:T(8,128)(2,1)S(1)}, bf16[2,64,512]{2,1,0:T(8,128)(2,1)S(1)}, u32[]{:S(2)}, u32[]{:S(2)}) collective-permute-start(bf16[2,64,512]{2,1,0:T(8,128)(2,1)S(1)} %get-tuple-element.105), channel_id=1, source_target_pairs={{0,8},{2,10},{4,12},{6,14},{8,0},{10,2},{12,4},{14,6},{16,24},{18,... | collective-permute-start | bytes 393224 | tf_op jit(solution)/shard_map/ppermute | solution.py:46
  92.0 14.9 %collective-permute-start.34 = (bf16[2,64,512]{2,1,0:T(8,128)(2,1)S(1)}, bf16[2,64,512]{2,1,0:T(8,128)(2,1)S(1)}, u32[]{:S(2)}, u32[]{:S(2)}) collective-permute-start(bf16[2,64,512]{2,1,0:T(8,128)(2,1)S(1)} %get-tuple-element.106), channel_id=1, source_target_pairs={{0,16},{2,18},{4,20},{6,22},{8,24},{10,26},{12,28},{14,30},{16,0},... | collective-permute-start | bytes 393224 | tf_op jit(solution)/shard_map/ppermute | solution.py:46
  94.2 12.7 %collective-permute-start.35 = (bf16[2,64,512]{2,1,0:T(8,128)(2,1)S(1)}, bf16[2,64,512]{2,1,0:T(8,128)(2,1)S(1)}, u32[]{:S(2)}, u32[]{:S(2)}) collective-permute-start(bf16[2,64,512]{2,1,0:T(8,128)(2,1)S(1)} %get-tuple-element.107.refs_5_), channel_id=1, source_target_pairs={{0,24},{2,26},{4,28},{6,30},{8,16},{10,18},{12,20},{14,22},{16,8},... | collective-permute-start | bytes 393224 | tf_op jit(solution)/shard_map/ppermute | solution.py:46
  98.5 7.3 %collective-permute-start.43 = (bf16[2,512]{1,0:T(2,128)(2,1)S(1)}, bf16[2,512]{1,0:T(2,128)(2,1)S(1)}, u32[]{:S(2)}, u32[]{:S(2)}) collective-permute-start(bf16[2,512]{1,0:T(2,128)(2,1)S(1)} %get-tuple-element.123.refs_4_), channel_id=1, source_target_pairs={{2,4},{4,2},{6,8},{8,6},{10,12},{12,10},{14,16},{16,14},{18,20},{2... | collective-permute-start | bytes 6152 | tf_op jit(solution)/shard_map/ppermute | solution.py:41
  101.6 4.1 %collective-permute-start.44 = (bf16[2,512]{1,0:T(2,128)(2,1)S(1)}, bf16[2,512]{1,0:T(2,128)(2,1)S(1)}, u32[]{:S(2)}, u32[]{:S(2)}) collective-permute-start(bf16[2,512]{1,0:T(2,128)(2,1)S(1)} %get-tuple-element.123.refs_4_), channel_id=1, source_target_pairs={{0,2},{2,0},{4,6},{6,4},{8,10},{10,8},{12,14},{14,12},{16,18},{18,... | collective-permute-start | bytes 6152 | tf_op jit(solution)/shard_map/ppermute | solution.py:37
